TPU v7x, 128 devices: a whole 4x4x4 slice. The times are simulated.
128 devices in a mesh: row: 16 (over x, y), col: 8 (over z, core).
Axes of the slice: x: 4, y: 4, z: 4, core: 2. Of those that a mesh axis runs over, the one named last changes fastest.
Arguments:
- subgrid_pixels: float32 [16384, 2, 2, 1024], P(('row', 'col')), may hold values from -6 to 6
- tile_offsets: int32 [16384, 2], P(('row', 'col')), may hold values from 0 to 255, as said below
- station_pairs: int32 [16384, 2], P(('row', 'col')), may hold values from 0 to 511
- time_blocks: int32 [16384], P(('row', 'col')), may hold values from 0 to 1
- channel_blocks: int32 [16384], P(('row', 'col')), may hold values from 0 to 7
- valid_counts: int32 [128], P(('row', 'col')), may hold values from 64 to 128, as said below
- aterms: bfloat16 [512, 2, 2, 2, 1024], replicated, may hold values from -4 to 4
- channel_weights: float32 [8], replicated, may hold values from 0.5 to 2
Outputs:
- image: float32 [2, 8192, 8192], P(None, ('row', 'col'))
Inputs may be any that keep to these rules, and one draw needn't show every extreme that they name: `tile_offsets`: within the valid entries of one device's list, at most 2 subgrids lie in the grid block of any one device (rows 512 r to 512 (r + 1) - 1, columns 1024 c to 1024 (c + 1) - 1 of device index r * 8 + c), and some device's block receives exactly 2 valid subgrids from every device. `valid_counts`: entry d counts the valid subgrids of device d, which are the first slots of its list; some device's list is full.
All inputs are finite; a program needn't handle non-finite values.
Results may differ from a plain program's by a relative error of at most 0.0003.
Values sent between devices are 32-bit elements; how exact they have to be, the bound alone decides.
A program may use at most 192 MiB of HBM per device.

v0:
```python
import math

import jax
import jax.numpy as jnp
from jax import lax
from jax.sharding import PartitionSpec as P

G = 8192
SUB = 32


EXACT = lax.Precision.HIGHEST


def phase_table(row_size, column_size, modulus):
    row_index = jnp.arange(row_size, dtype=jnp.int32)[:, None]
    column_index = jnp.arange(column_size, dtype=jnp.int32)[None, :]
    phase_angle = (
        -2.0 * math.pi / modulus * (row_index * column_index % modulus).astype(jnp.float32)
    )
    return (jnp.cos(phase_angle), jnp.sin(phase_angle))


def kron_table(subgrid_side):
    pixel_index = jnp.arange(subgrid_side * subgrid_side, dtype=jnp.int32)
    coarse_index = pixel_index // subgrid_side
    fine_index = pixel_index % subgrid_side
    turn_count = (
        coarse_index[:, None] * coarse_index[None, :] + fine_index[:, None] * fine_index[None, :]
    ) % subgrid_side
    phase_angle = -2.0 * math.pi / subgrid_side * turn_count.astype(jnp.float32)
    return (jnp.cos(phase_angle) / subgrid_side, jnp.sin(phase_angle) / subgrid_side)


def complex_einsum(formula, left_real, left_imag, right_real, right_imag):
    real_real = jnp.einsum(formula, left_real, right_real, precision=EXACT)
    imag_imag = jnp.einsum(formula, left_imag, right_imag, precision=EXACT)
    real_imag = jnp.einsum(formula, left_real, right_imag, precision=EXACT)
    imag_real = jnp.einsum(formula, left_imag, right_real, precision=EXACT)
    return (real_real - imag_imag, real_imag + imag_real)


def correct_subgrids(
    pixels, station_pair, time_index, channel_index, aterms, channel_weights, dft_real, dft_imag
):
    beam_first = aterms[station_pair[:, 0], time_index].astype(jnp.float32)
    beam_second = aterms[station_pair[:, 1], time_index].astype(jnp.float32)
    gain_real = beam_first[:, 0] * beam_second[:, 0] + beam_first[:, 1] * beam_second[:, 1]
    gain_imag = beam_first[:, 1] * beam_second[:, 0] - beam_first[:, 0] * beam_second[:, 1]
    matches = (
        channel_index[:, None] == jnp.arange(channel_weights.shape[0], dtype=jnp.int32)[None, :]
    )
    weight = jnp.sum(jnp.where(matches, channel_weights[None, :], 0.0), axis=1)[:, None, None]
    pixel_real = pixels[:, 0]
    pixel_imag = pixels[:, 1]
    fixed_real = (pixel_real * gain_real - pixel_imag * gain_imag) * weight
    fixed_imag = (pixel_real * gain_imag + pixel_imag * gain_real) * weight
    item_count = pixels.shape[0]
    feed_count = pixels.shape[2]
    pixel_count = pixels.shape[3]
    flat_real = fixed_real.reshape(item_count * feed_count, pixel_count)
    flat_imag = fixed_imag.reshape(item_count * feed_count, pixel_count)
    out_real = jnp.dot(flat_real, dft_real, precision=EXACT) - jnp.dot(
        flat_imag, dft_imag, precision=EXACT
    )
    out_imag = jnp.dot(flat_real, dft_imag, precision=EXACT) + jnp.dot(
        flat_imag, dft_real, precision=EXACT
    )
    return jnp.stack(
        [
            out_real.reshape(item_count, feed_count, pixel_count),
            out_imag.reshape(item_count, feed_count, pixel_count),
        ],
        axis=1,
    )


def local(
    subgrid_pixels,
    tile_offsets,
    station_pairs,
    time_blocks,
    channel_blocks,
    valid_counts,
    aterms,
    channel_weights,
):
    row_count = lax.axis_size("row")
    column_count = lax.axis_size("col")
    devices = row_count * column_count
    slot_count = subgrid_pixels.shape[0]
    capacity = 2 * slot_count // devices
    rows_dev = G // row_count
    cols_dev = G // column_count
    tile_rows = rows_dev // SUB
    tile_cols = cols_dev // SUB
    tiles_dev = tile_rows * tile_cols
    buffer_rows = devices * capacity
    dft_real, dft_imag = kron_table(SUB)
    slot_index = jnp.arange(slot_count, dtype=jnp.int32)
    is_valid = slot_index < valid_counts[0]
    tile_row = tile_offsets[:, 0]
    tile_column = tile_offsets[:, 1]
    owner_index = tile_row // tile_rows * column_count + tile_column // tile_cols
    local_tile = tile_row % tile_rows * tile_cols + tile_column % tile_cols
    earlier = (
        (owner_index[:, None] == owner_index[None, :])
        & (slot_index[None, :] < slot_index[:, None])
        & is_valid[None, :]
    )
    owner_rank = jnp.sum(earlier.astype(jnp.int32), axis=1)
    target = jnp.where(is_valid, owner_index * capacity + owner_rank, buffer_rows)
    details = jnp.stack(
        [local_tile, station_pairs[:, 0], station_pairs[:, 1], time_blocks, channel_blocks], axis=1
    ).astype(jnp.float32)
    blank_rows = jnp.zeros((buffer_rows, 5), jnp.float32).at[:, 0].set(float(tiles_dev))
    send_details = blank_rows.at[target].set(details, mode="drop")
    send_pixels = (
        jnp.zeros((buffer_rows,) + subgrid_pixels.shape[1:], jnp.float32)
        .at[target]
        .set(subgrid_pixels, mode="drop")
    )
    got_pixels, got_details = (
        lax.all_to_all(send_pixels, ("row", "col"), split_axis=0, concat_axis=0, tiled=True),
        lax.all_to_all(send_details, ("row", "col"), split_axis=0, concat_axis=0, tiled=True),
    )
    decoded = got_details.astype(jnp.int32)
    spectra = correct_subgrids(
        got_pixels,
        decoded[:, 1:3],
        decoded[:, 3],
        decoded[:, 4],
        aterms,
        channel_weights,
        dft_real,
        dft_imag,
    )
    tile_index = decoded[:, 0]
    summed = jax.ops.segment_sum(spectra, tile_index, num_segments=tiles_dev + 1)[:tiles_dev]
    uv_grid = (
        summed.reshape(tile_rows, tile_cols, 2, 2, SUB, SUB)
        .transpose(2, 3, 0, 4, 1, 5)
        .reshape(4, rows_dev, cols_dev)
    )
    stripe = rows_dev // column_count
    rows_block = lax.all_to_all(uv_grid, "col", split_axis=1, concat_axis=2, tiled=True)
    factor = G // 128
    shaped = rows_block.reshape(4, stripe, factor, 128)
    first_real, first_imag = phase_table(factor, factor, factor)
    mid_real, mid_imag = complex_einsum(
        "prba,kb->prka", shaped[:2], shaped[2:], first_real, first_imag
    )
    twist_real, twist_imag = phase_table(factor, 128, G)
    mid_real, mid_imag = (
        mid_real * twist_real - mid_imag * twist_imag,
        mid_real * twist_imag + mid_imag * twist_real,
    )
    second_real, second_imag = phase_table(128, 128, 128)
    out_real, out_imag = complex_einsum(
        "prka,wa->pwrk", mid_real, mid_imag, second_real, second_imag
    )
    spectrum = jnp.concatenate([out_real, out_imag], axis=0).reshape(4, devices, -1)
    spectrum = lax.all_to_all(spectrum, ("row", "col"), split_axis=1, concat_axis=1, tiled=True)
    spectrum_block = spectrum.reshape(4, devices, 128 // devices, stripe, factor)
    third_real, third_imag = phase_table(devices, devices, devices)
    high_real, high_imag = complex_einsum(
        "pjkuq,cj->pckuq", spectrum_block[:2], spectrum_block[2:], third_real, third_imag
    )
    turn_real, turn_imag = phase_table(devices, stripe, G)
    turn_real = turn_real[None, :, None, :, None]
    turn_imag = turn_imag[None, :, None, :, None]
    high_real, high_imag = (
        high_real * turn_real - high_imag * turn_imag,
        high_real * turn_imag + high_imag * turn_real,
    )
    last_real, last_imag = phase_table(stripe, stripe, stripe)
    image_scale = 1.0 / (SUB * math.sqrt(slot_count * devices))
    image = jnp.einsum("pckuq,wu->pkqwc", high_real, last_real, precision=EXACT) - jnp.einsum(
        "pckuq,wu->pkqwc", high_imag, last_imag, precision=EXACT
    )
    return image.reshape(2, 128 // devices * factor, G) * image_scale


def solution(mesh):
    in_specs = (
        P(("row", "col"), None, None, None),
        P(("row", "col"), None),
        P(("row", "col"), None),
        P(("row", "col")),
        P(("row", "col")),
        P(("row", "col")),
        P(),
        P(),
    )
    out_specs = P(None, ("row", "col"), None)
    return jax.shard_map(local, mesh=mesh, in_specs=in_specs, out_specs=out_specs, check_vma=False)
```

profile of v0, /device:TPU:1, one launch (start us, length us, event | category | flops | bytes accessed | tf_op | source)
XLA Modules:
  0.0 768.7 jit_solution(6160132217477299611)
XLA Ops:
  7.7 11.5 %all-to-all-start = ((f32[128,2,5]{2,1,0:T(2,128)}), f32[128,2,5]{2,1,0:T(2,128)S(1)}, u32[]{:S(2)}, u32[]{:S(2)}) async-start(f32[128,2,5]{2,1,0:T(2,128)} %bitcast.14), calls=%async_computation | async-start | bytes 262144 | tf_op jit(solution)/shard_map/all_to_all | solution.py:125
  23.3 15.7 %scatter_fusion.1 = f32[256,2,2,1024]{3,2,1,0:T(2,128)} fusion(f32[256,2,2,1024]{3,2,1,0:T(2,128)} %broadcast_in_dim.18, s32[128]{0:T(128)S(1)} %fusion.135, f32[128,2,2,1024]{3,2,1,0:T(2,128)S(1)} %copy-done.8), kind=kCustom, calls=%fused_computation.3 | custom fusion | bytes 6291968 | tf_op jit(solution)/shard_map/scatter | solution.py:121
  39.0 10.7 %all-to-all-start.1 = ((f32[256,2,2,1024]{3,2,1,0:T(2,128)}), f32[256,2,2,1024]{3,2,1,0:T(2,128)}, u32[]{:S(2)}, u32[]{:S(2)}) async-start(f32[256,2,2,1024]{3,2,1,0:T(2,128)} %scatter_fusion.1), calls=%async_computation.1 | async-start | bytes 8388608 | tf_op jit(solution)/shard_map/all_to_all | solution.py:124
  50.2 15.2 %gather_fusion = bf16[256,2,2,1024]{3,2,1,0:T(2,128)(2,1)S(1)} fusion(bf16[512,2,2,2,1024]{4,3,2,1,0:T(2,128)(2,1)} %param.16, s32[256]{0:T(256)S(1)} %get-tuple-element.19), kind=kCustom, calls=%fused_computation | custom fusion | bytes 4196352 | tf_op jit(solution)/shard_map/gather | solution.py:46
  69.8 15.7 %gather_fusion.1 = bf16[256,2,2,1024]{3,2,1,0:T(2,128)(2,1)S(1)} fusion(bf16[512,2,2,2,1024]{4,3,2,1,0:T(2,128)(2,1)} %param.16, s32[256]{0:T(256)S(1)} %get-tuple-element.18), kind=kCustom, calls=%fused_computation.1 | custom fusion | bytes 4196352 | tf_op jit(solution)/shard_map/gather | solution.py:47
  90.3 12.0 %all-to-all-done.1 = f32[256,2,2,1024]{3,2,1,0:T(2,128)} async-done(((f32[256,2,2,1024]{3,2,1,0:T(2,128)}), f32[256,2,2,1024]{3,2,1,0:T(2,128)}, u32[]{:S(2)}, u32[]{:S(2)}) %all-to-all-start.1) | async-done | bytes 4194336 | tf_op jit(solution)/shard_map/all_to_all | solution.py:124
  119.7 25.0 %fusion.20 = f32[512,1024]{1,0:T(8,128)S(1)} fusion(s32[1024]{0:T(1024)S(1)} %get-tuple-element.32, s32[1024]{0:T(1024)S(1)} %get-tuple-element.33, f32[512,1024]{1,0:T(8,128)} %sub.82, f32[512]{0:T(512)S(1)} %mul.539), kind=kOutput, calls=%fused_computation.42 | convolution fusion | flops 6460801024 | bytes 4204544 | tf_op jit(solution)/shard_map/dot_general | solution.py:63
  144.7 25.1 %fusion.19 = f32[512,1024]{1,0:T(8,128)} fusion(s32[1024]{0:T(1024)S(1)} %get-tuple-element.32, s32[1024]{0:T(1024)S(1)} %get-tuple-element.33, f32[512,1024]{1,0:T(8,128)S(1)} %copy-done.9, f32[512]{0:T(512)S(1)} %mul.539), kind=kOutput, calls=%fused_computation.41 | convolution fusion | flops 6460801024 | bytes 4204544 | tf_op jit(solution)/shard_map/dot_general | solution.py:66
  169.8 25.5 %fusion.41 = f32[512,1024]{1,0:T(8,128)} fusion(f32[512,1024]{1,0:T(8,128)S(1)} %fusion.20, s32[1024]{0:T(1024)S(1)} %get-tuple-element.32, s32[1024]{0:T(1024)S(1)} %get-tuple-element.33, f32[512,1024]{1,0:T(8,128)S(1)} %copy-done.9, f32[512]{0:T(512)S(1)} %mul.539), kind=kOutput, calls=%fused_computation.59 | convolution fusion | flops 6461325312 | bytes 6301696 | tf_op jit(solution)/shard_map/dot_general | solution.py:63
  197.8 27.6 %fusion.44 = f32[512,1024]{1,0:T(8,128)} fusion(f32[512,1024]{1,0:T(8,128)} %fusion.19, s32[1024]{0:T(1024)S(1)} %get-tuple-element.32, s32[1024]{0:T(1024)S(1)} %get-tuple-element.33, f32[512,1024]{1,0:T(8,128)} %sub.82, f32[512]{0:T(512)S(1)} %mul.539), kind=kOutput, calls=%fused_computation.60 | convolution fusion | flops 6461325312 | bytes 6301696 | tf_op jit(solution)/shard_map/dot_general | solution.py:66
  234.7 7.5 broadcast_in_dim.16
  242.2 42.7 %scatter_fusion.2 = f32[513,2,2,1024]{3,2,1,0:T(2,128)} fusion(f32[513,2,2,1024]{3,2,1,0:T(2,128)} %broadcast_in_dim.16, s32[256]{0:T(256)S(1)} %get-tuple-element.20, f32[256,2,2,1024]{3,2,1,0:T(2,128)} %pad_maximum_fusion.1), kind=kCustom, calls=%fused_computation.4 | custom fusion | flops 1048576 | bytes 12583936 | tf_op jit(solution)/shard_map/scatter-add | solution.py:139
  284.9 7.3 slice.121
  292.2 23.3 %reshape.299 = f32[16,32,2,2,32,32]{5,4,3,2,1,0:T(8,128)} reshape(f32[512,2,2,1024]{3,2,1,0:T(2,128)} %slice.121) | data formatting | bytes 16777216 | tf_op jit(solution)/shard_map/reshape | solution.py:141
  315.5 37.2 %copy.65 = f32[16,32,2,2,32,32]{5,1,4,0,3,2:T(8,128)} copy(f32[16,32,2,2,32,32]{5,4,3,2,1,0:T(8,128)} %reshape.299) | data formatting | bytes 16777216 | tf_op jit(solution)/shard_map/reshape | solution.py:141
  352.7 26.1 %reshape.300 = f32[4,512,1024]{2,1,0:T(8,128)} reshape(f32[2,2,16,32,32,32]{5,4,3,2,1,0:T(8,128)} %bitcast.162) | data formatting | bytes 16777216 | tf_op jit(solution)/shard_map/reshape | solution.py:143
  378.8 12.0 %copy.45 = f32[4,512,1024]{2,0,1:T(4,128)} copy(f32[4,512,1024]{2,1,0:T(8,128)} %reshape.300) | data formatting | bytes 16777216 | tf_op jit(solution)/shard_map/reshape | solution.py:143
  390.8 7.0 all-to-all-start.2
  397.9 93.7 %all-to-all-done.2 = f32[4,512,1024]{2,0,1:T(4,128)} async-done(((f32[4,512,1024]{2,0,1:T(4,128)}), f32[4,512,1024]{2,0,1:T(4,128)}, u32[]{:S(2)}, u32[]{:S(2)}) %all-to-all-start.2) | async-done | bytes 8388640 | tf_op jit(solution)/shard_map/all_to_all | solution.py:146
  491.6 8.2 %copy.46 = f32[4,512,1024]{2,1,0:T(8,128)S(1)} copy(f32[4,512,1024]{2,0,1:T(4,128)} %all-to-all-done.2) | data formatting | bytes 16777216 | tf_op jit(solution)/shard_map/all_to_all | solution.py:146
  512.7 8.1 %fusion.88 = f32[64,2,64,128]{3,0,2,1:T(8,128)} fusion(f32[2,64,64,128]{3,2,1,0:T(8,128)} %slice.101), kind=kOutput, calls=%fused_computation.121 | convolution fusion | flops 805363712 | bytes 8388608 | tf_op jit(solution)/shard_map/prba,kb->prka/dot_general | solution.py:36
  535.8 7.4 convolution_subtract_fusion
  566.6 10.3 %copy.49 = f32[4,128,4096]{2,0,1:T(4,128)} copy(f32[4,128,4096]{1,2,0:T(8,128)} %bitcast.172) | data formatting | bytes 16777216 | tf_op jit(solution)/shard_map/reshape | solution.py:162
  582.7 102.6 %all-to-all-done.3 = f32[4,128,4096]{2,0,1:T(4,128)} async-done(((f32[4,128,4096]{2,0,1:T(4,128)}), f32[4,128,4096]{2,0,1:T(4,128)}, u32[]{:S(2)}, u32[]{:S(2)}) %all-to-all-start.3) | async-done | bytes 8388640 | tf_op jit(solution)/shard_map/all_to_all | solution.py:163
  685.3 11.9 %fusion.212 = (f32[2,128,4096]{2,0,1:T(2,128)}, f32[2,128,4096]{2,0,1:T(2,128)}) fusion(f32[4,128,4096]{2,0,1:T(4,128)} %all-to-all-done.3), kind=kLoop, calls=%fused_computation.264 | loop fusion | bytes 16777216 | tf_op jit(solution)/shard_map/slice | solution.py:167
  697.2 7.3 copy.50
  704.4 7.3 fusion.97
  717.1 7.3 copy.51
  724.4 7.3 fusion.103
  737.2 10.6 %fusion.4 = (f32[2,128,64,64]{1,3,2,0:T(8,128)}, f32[2,128,64,64]{1,3,2,0:T(8,128)}) fusion(f32[128,64]{0,1:T(8,128)S(1)} %get-tuple-element.36, f32[128,64]{0,1:T(8,128)S(1)} %get-tuple-element.37, f32[128,2,64,64]{0,3,2,1:T(8,128)} %bitcast.168, f32[128,2,64,64]{0,3,2,1:T(8,128)} %bitcast.170, f32[128,2,64,64]{0,3,2,1:T(8,128)S(1)} %bitcast.167, ...), kind=kLoop, calls=%fused_computation.17 | loop fusion | flops 8388608 | bytes 25231360 | tf_op jit(solution)/shard_map/reshape.45
  747.9 8.6 %fusion.15 = f32[64,2,128,64]{2,0,3,1:T(8,128)S(1)} fusion(f32[2,128,64,64]{1,3,2,0:T(8,128)} %get-tuple-element.25), kind=kOutput, calls=%fused_computation.30 | convolution fusion | flops 805363712 | bytes 8388608 | tf_op jit(solution)/shard_map/pckuq,wu->pkqwc/dot_general | solution.py:178
  756.5 7.1 multiply_bitcast_fusion
  (68 shorter events, 122.1 us)
Async XLA Ops:
  0.0 23.3 %copy-start.8 = (f32[128,2,2,1024]{3,2,1,0:T(2,128)S(1)}, f32[128,2,2,1024]{3,2,1,0:T(2,128)}, u32[]{:S(2)}) copy-start(f32[128,2,2,1024]{3,2,1,0:T(2,128)} %param.10) | copy-start | bytes 6291460
  7.7 31.3 %all-to-all-start = ((f32[128,2,5]{2,1,0:T(2,128)}), f32[128,2,5]{2,1,0:T(2,128)S(1)}, u32[]{:S(2)}, u32[]{:S(2)}) async-start(f32[128,2,5]{2,1,0:T(2,128)} %bitcast.14), calls=%async_computation | async-start | bytes 262144 | tf_op jit(solution)/shard_map/all_to_all | solution.py:125
  39.0 63.3 %all-to-all-start.1 = ((f32[256,2,2,1024]{3,2,1,0:T(2,128)}), f32[256,2,2,1024]{3,2,1,0:T(2,128)}, u32[]{:S(2)}, u32[]{:S(2)}) async-start(f32[256,2,2,1024]{3,2,1,0:T(2,128)} %scatter_fusion.1), calls=%async_computation.1 | async-start | bytes 8388608 | tf_op jit(solution)/shard_map/all_to_all | solution.py:124
  85.5 4.4 copy-start.10
  119.7 25.1 %copy-start.9 = (f32[512,1024]{1,0:T(8,128)S(1)}, f32[512,1024]{1,0:T(8,128)}, u32[]{:S(2)}) copy-start(f32[512,1024]{1,0:T(8,128)} %add.259) | copy-start | bytes 6291460
  390.8 100.8 %all-to-all-start.2 = ((f32[4,512,1024]{2,0,1:T(4,128)}), f32[4,512,1024]{2,0,1:T(4,128)}, u32[]{:S(2)}, u32[]{:S(2)}) async-start(f32[4,512,1024]{2,0,1:T(4,128)} %copy.45), calls=%async_computation.2 | async-start | bytes 16777216 | tf_op jit(solution)/shard_map/all_to_all | solution.py:146
  512.7 8.2 %copy-start.3 = (f32[2,64,64,128]{3,2,1,0:T(8,128)S(1)}, f32[2,64,64,128]{3,2,1,0:T(8,128)}, u32[]{:S(2)}) copy-start(f32[2,64,64,128]{3,2,1,0:T(8,128)} %slice.101) | copy-start | bytes 12582916
  520.9 5.5 copy-start.7
  535.8 7.5 copy-start.2
  535.8 7.5 copy-start.5
  577.0 108.3 %all-to-all-start.3 = ((f32[4,128,4096]{2,0,1:T(4,128)}), f32[4,128,4096]{2,0,1:T(4,128)}, u32[]{:S(2)}, u32[]{:S(2)}) async-start(f32[4,128,4096]{2,0,1:T(4,128)} %copy.49), calls=%async_computation.3 | async-start | bytes 16777216 | tf_op jit(solution)/shard_map/all_to_all | solution.py:163
  704.4 7.3 copy-start
  724.4 7.3 copy-start.1
  731.7 5.6 copy-start.4
  747.9 8.6 %copy-start.6 = (f32[2,128,64,64]{1,3,2,0:T(8,128)S(1)}, f32[2,128,64,64]{1,3,2,0:T(8,128)}, u32[]{:S(2)}) copy-start(f32[2,128,64,64]{1,3,2,0:T(8,128)} %get-tuple-element.24) | copy-start | bytes 12582916
where the time goes:
time: 777 us; the launch traced here: 769 us
  local copies, waits for them, and re-layouts  252 us (32%)
  waiting for transfers between devices  208 us (27%)
  matrix products  184 us (24%)
  other arithmetic  87.6 us (11%)
  starting transfers between devices  34.7 us (4%)
    all_to_all x1, waiting for transfers between devices, local(): lax.all_to_all(spectrum, ('row', 'col'), split_axis=1, concat_axis=1, til...  103 us
    all_to_all x1, waiting for transfers between devices, local(): lax.all_to_all(uv_grid, 'col', split_axis=1, concat_axis=2, tiled=True)  93.7 us
    reshape x2, local copies, waits for them, and re-layouts, local(): summed.reshape(tile_rows, tile_cols, 2, 2, SUB, SUB)  60.5 us
    scatter-add x1, other arithmetic, local(): jax.ops.segment_sum(spectra, tile_index, num_segments=tiles_dev + 1)  42.7 us
    reshape x2, local copies, waits for them, and re-layouts, local(): uv_grid = summed.reshape(tile_rows, tile_cols, 2, 2, SUB, SUB).transpose(...  38.1 us
    dot_general x1, matrix products, correct_subgrids(): jnp.dot(flat_real, dft_imag, precision=EXACT)  27.6 us
    unnamed x4, matrix products  25.5 us
    dot_general x1, matrix products, correct_subgrids(): jnp.dot(flat_imag, dft_imag, precision=EXACT)  25.5 us
  transfers between devices with their start and end apart: 4, of which 3 were waited for; matrix products, arithmetic and copies ran while one was open for 8% of the time, Pallas kernels for 0%

commit v1 on v0

v1 whole, which is shorter than its diff:
```python
import functools
import math

import jax
import jax.numpy as jnp
import ml_dtypes
import numpy as np
from jax import lax
from jax.experimental import pallas as pl
from jax.experimental.pallas import tpu as pltpu
from jax.sharding import PartitionSpec as P

BF = jnp.bfloat16
F32 = jnp.float32
I32 = jnp.int32

PAIR_J = (0, 8, 4, 12, 1, 9, 17, 25, 2, 10, 18, 26, 3, 11, 19, 27)
STEP_A = (0, 4, 1, 1, 2, 2, 3, 3)
STEP_B = (0, 4, 7, 7, 6, 6, 5, 5)
MSG = 72
VMEM = 56 * 1024 * 1024


def partner(j):
    return 16 if j == 0 else 32 - j


def unit(turns):
    return np.exp(-2j * np.pi * turns)


def split_np(x):
    hi = np.asarray(x, np.float32).astype(ml_dtypes.bfloat16)
    lo = (np.asarray(x, np.float64) - hi.astype(np.float64)).astype(ml_dtypes.bfloat16)
    return hi, lo


def split(x):
    hi = x.astype(BF)
    return hi, (x - hi.astype(F32)).astype(BF)


def dot(a, b):
    return lax.dot_general(a, b, (((1,), (0,)), ((), ())), preferred_element_type=F32)


def dot_nt(a, b):
    return lax.dot_general(a, b, (((1,), (1,)), ((), ())), preferred_element_type=F32)


@functools.lru_cache(None)
def tables():
    xi = np.arange(4)[:, None, None]
    y = np.arange(32)[None, :, None]
    v = np.arange(32)[None, None, :]
    b = np.zeros((8, 2, 2, 4, 32, 2, 2, 2, 32))
    for step in range(8):
        for pair in range(2):
            j = PAIR_J[2 * step + pair]
            for half, jj in enumerate((j, partner(j))):
                w = unit((xi * jj + y * v) % 32 / 32) / 32
                b[step, half, 0, :, :, pair, half, 0] = w.real
                b[step, half, 0, :, :, pair, half, 1] = w.imag
                b[step, half, 1, :, :, pair, half, 0] = -w.imag
                b[step, half, 1, :, :, pair, half, 1] = w.real
    b = b.reshape(8, 2, 256, 256)
    i = np.arange(256)
    w = unit(i[:, None] * i[None, :] % 256 / 256)
    wc = np.stack([w.real.reshape(4, 64, 256), w.imag.reshape(4, 64, 256)], 1).reshape(512, 256)
    tw = unit(i[:, None] * (np.arange(128) % 32)[None, :] / 8192)
    d = unit(np.arange(32)[:, None] * np.arange(32)[None, :] % 32 / 32)
    coef = np.stack([np.stack([d, 1j * d]), np.stack([1j * d, -d])])
    f = np.zeros((2, 3, 2, 2, 32, 2, 2, 2, 32))

    def put(kind, which, half, pm, conj):
        for pq in range(2):
            for reim in range(2):
                c = coef[pq, reim]
                f[kind, which, pm, 0, :, pq, half, reim, :] = c.real
                f[kind, which, pm, 1, :, pq, half, reim, :] = -c.imag if conj else c.imag

    put(0, 0, 0, 0, False)
    put(0, 0, 1, 1, True)
    put(0, 1, 1, 0, True)
    put(0, 1, 0, 1, False)
    put(1, 0, 0, 0, False)
    put(1, 0, 1, 1, False)
    put(1, 1, 1, 1, True)
    put(1, 2, 0, 0, True)
    f = f.reshape(2, 3, 128, 256)
    fh, fl = split_np(f)
    f = np.concatenate([fh, fl], axis=2)
    k = np.arange(256)
    q, rp, t, pm = k // 64, k // 32 % 2, k // 2 % 16, k % 2
    r = 16 * (2 * q + rp) + t
    rr = np.where(pm == 0, r, 255 - r)
    l0 = np.arange(256)
    w = unit(rr[:, None] * l0[None, :] % 256 / 256) / 4096
    wr = np.concatenate([w.real, w.imag], axis=1)
    w0 = np.where((pm == 0)[:, None], unit(r[:, None] * l0[None, :] % 256 / 256), 0) / 4096
    w16 = np.where((pm == 1)[:, None], unit((32 * r[:, None] + 16) * l0[None, :] % 8192 / 8192), 0) / 4096
    ws = np.stack([np.concatenate([w0.real, w16.real], 1), np.concatenate([-w0.imag, -w16.imag], 1)])
    kx = np.arange(32)
    qx, row = kx // 8, kx % 8
    rx = 16 * (15 - (2 * qx + row))
    wx = np.where((row < 2)[:, None], unit(-(rx[:, None] * l0[None, :] % 256) / 256), 0) / 4096
    zero = np.zeros_like(wx.real)
    wx = np.stack([np.concatenate([wx.real, zero], 1), np.concatenate([-wx.imag, zero], 1)])
    tj = unit(np.array(PAIR_J)[:, None] * l0[None, :] / 8192)
    tj = np.stack([tj.real, tj.imag], 1).astype(np.float32)
    return dict(
        b=split_np(b), wc=split_np(wc), tw=(tw.real.astype(np.float32), tw.imag.astype(np.float32)),
        f=f, wr=split_np(wr), ws=split_np(ws), wx=split_np(wx), tj=tj,
    )


def slot_kernel(pk, vc, table, target, count):
    def clear(i, _):
        count[i] = 0
        table[2 * i] = -1
        table[2 * i + 1] = -1
        return 0

    lax.fori_loop(0, 128, clear, 0)

    def place(s, _):
        row = pk[s]
        col = pk[128 + s]
        block_row = row // 16
        low = block_row < 8
        near = jnp.where(low, block_row, 15 - block_row)
        place_row = near // 2 * 4 + near % 2 + jnp.where(low, 0, 2)
        block = place_row * 8 + col // 32
        rank = count[block]
        valid = s < vc[0]
        slot = block * 2 + jnp.minimum(rank, 1)
        target[s] = jnp.where(valid, slot, -1)

        @pl.when(valid)
        def _():
            count[block] = rank + 1
            table[slot] = row % 16 * 32 + col % 32

        return 0

    lax.fori_loop(0, 128, place, 0)


def slots(packed, count):
    smem = pl.BlockSpec(memory_space=pltpu.SMEM)
    return pl.pallas_call(
        slot_kernel,
        out_shape=(jax.ShapeDtypeStruct((256,), I32), jax.ShapeDtypeStruct((128,), I32)),
        in_specs=[smem, smem],
        out_specs=(smem, smem),
        scratch_shapes=[pltpu.SMEM((128,), I32)],
        name="slots",
    )(packed, count)


def dft8(re, im):
    h = math.sqrt(0.5)

    def four(a, b):
        s0r, s0i = a[0] + a[2], b[0] + b[2]
        s1r, s1i = a[0] - a[2], b[0] - b[2]
        s2r, s2i = a[1] + a[3], b[1] + b[3]
        s3r, s3i = a[1] - a[3], b[1] - b[3]
        return (
            [s0r + s2r, s1r + s3i, s0r - s2r, s1r - s3i],
            [s0i + s2i, s1i - s3r, s0i - s2i, s1i + s3r],
        )

    er, ei = four(re[0::2], im[0::2])
    orr, oi = four(re[1::2], im[1::2])
    tr = [orr[0], (orr[1] + oi[1]) * h, oi[2], (oi[3] - orr[3]) * h]
    ti = [oi[0], (oi[1] - orr[1]) * h, -orr[2], -(oi[3] + orr[3]) * h]
    return (
        [er[k] + tr[k] for k in range(4)] + [er[k] - tr[k] for k in range(4)],
        [ei[k] + ti[k] for k in range(4)] + [ei[k] - ti[k] for k in range(4)],
    )


def source_kernel(
    pk, vc, cw, ja, jb, tgt, px, beams, bh, bl, out, got, corr, lhi, llo, perm, sems
):
    step = pl.program_id(0)

    @pl.when(step == 0)
    def _():
        for group in range(8):
            def fetch(i, _, group=group):
                s = group * 16 + i
                for e in range(2):
                    pltpu.make_async_copy(
                        beams.at[pk[256 + 128 * e + s]], got.at[s, e], sems.at[group]
                    ).start()
                return 0

            lax.fori_loop(0, 16, fetch, 0)
        slot = lax.broadcasted_iota(I32, (256, 128), 0)
        hit = jnp.where(slot == tgt[...], 1.0, 0.0).astype(BF)
        perm[:, :128] = hit
        perm[:, 128:] = hit
        for group in range(8):
            part = got.at[pl.ds(group * 16, 16)]
            pltpu.make_async_copy(part, part, sems.at[group]).wait()

            def correct(i, _, group=group):
                s = group * 16 + i
                weight = jnp.where(s < vc[0], cw[pk[512 + s]], 0.0)
                ar, ai = got[s, 0, 0].astype(F32), got[s, 0, 1].astype(F32)
                br, bi = got[s, 1, 0].astype(F32), got[s, 1, 1].astype(F32)
                gr = (ar * br + ai * bi) * weight
                gi = (ai * br - ar * bi) * weight
                pr, pi = px[s, 0], px[s, 1]
                at = pl.multiple_of(s * 32, 32)
                corr[pl.ds(at, 16), :] = pr * gr - pi * gi
                corr[pl.ds(at + 16, 16), :] = pr * gi + pi * gr
                return 0

            lax.fori_loop(0, 16, correct, 0, unroll=2)

            for f in range(2):
                base = group * 16 * 32 + f
                re = [corr[pl.ds(base + 2 * p, 16, stride=32), :] for p in range(8)]
                im = [corr[pl.ds(base + 16 + 2 * p, 16, stride=32), :] for p in range(8)]
                re, im = dft8(re, im)
                rows = slice(f * 128 + group * 16, f * 128 + group * 16 + 16)
                for k in range(8):
                    lhi[k, rows, :128], llo[k, rows, :128] = split(re[k])
                    lhi[k, rows, 128:], llo[k, rows, 128:] = split(im[k])

    acc = jnp.zeros((256, 256), F32)
    for half, pick in enumerate((ja, jb)):
        k = pick[step]
        acc = acc + dot(lhi[k], bh[0, half]) + dot(llo[k], bh[0, half]) + dot(lhi[k], bl[0, half])
    hi, lo = split(acc)
    for f in range(2):
        rows = slice(f * 128, f * 128 + 128)
        padded = dot(perm[...], jnp.concatenate([hi[rows], lo[rows]], axis=0))
        for pair in range(2):
            for q in range(4):
                out[(pair * 2 + f) * 4 + q] = padded[q * 64:(q + 1) * 64, pair * 128:(pair + 1) * 128]


def source(packed, count, weights, target, pixels, beams):
    t = tables()
    smem = pl.BlockSpec(memory_space=pltpu.SMEM)
    whole = pl.BlockSpec(memory_space=pltpu.VMEM)
    return pl.pallas_call(
        source_kernel,
        grid=(8,),
        out_shape=jax.ShapeDtypeStruct((128, 64, 128), F32),
        in_specs=[smem, smem, smem, smem, smem, whole, whole, pl.BlockSpec(memory_space=pl.ANY)]
        + [pl.BlockSpec((1, 2, 256, 256), lambda i: (i, 0, 0, 0))] * 2,
        out_specs=pl.BlockSpec((16, 64, 128), lambda i: (i, 0, 0)),
        scratch_shapes=[
            pltpu.VMEM((128, 2, 2, 16, 128), BF),
            pltpu.VMEM((128 * 32, 128), F32),
            pltpu.VMEM((8, 256, 256), BF),
            pltpu.VMEM((8, 256, 256), BF),
            pltpu.VMEM((256, 256), BF),
            pltpu.SemaphoreType.DMA((8,)),
        ],
        compiler_params=pltpu.CompilerParams(vmem_limit_bytes=VMEM),
        name="source",
    )(
        packed, count, weights, np.array(STEP_A, np.int32), np.array(STEP_B, np.int32), target,
        pixels, beams, t["b"][0], t["b"][1],
    )


def middle_kernel(
    dev, recv, tab, wh, wl, twr, twi, fmat, out, tabt, ghl, pqh, pql, zc
):
    kind = dev[0]
    quarter = dev[1]
    tabt[...] = tab[...].T
    for d in range(128):
        out[d * MSG + 64:d * MSG + 72, :] = jnp.zeros((8, 128), F32)
    lane = lax.broadcasted_iota(I32, (32, 128), 1)
    low = lane < 64

    def columns(pm, t):
        g = ghl[pm, pl.ds(pl.multiple_of(t * 256, 256), 256), :]
        for c in range(4):
            rows = slice(c * 128, c * 128 + 128)
            a = dot(wh[rows, :], g)
            b = dot(wl[rows, :], g[:, :128])
            u = a[:, :128] + a[:, 128:] + b
            ur, ui = u[:64], u[64:]
            m0 = slice(c * 64, c * 64 + 64)
            tr, ti = twr[m0, :], twi[m0, :]
            pqh[pm, m0, :128], pql[pm, m0, :128] = split(tr * ur - ti * ui)
            pqh[pm, m0, 128:], pql[pm, m0, 128:] = split(tr * ui + ti * ur)

    def mix(which, pm):
        both = fmat[kind, which]
        z = dot_nt(both, pqh[pm])
        return z[:128] + z[128:] + dot_nt(both[:128], pql[pm])

    def emit(z, row, pms):
        for pm in pms:
            for tile in range(2):
                lanes = slice(tile * 128, tile * 128 + 128)
                re, im = z[pm * 64:pm * 64 + 32, lanes], z[pm * 64 + 32:pm * 64 + 64, lanes]
                even = jnp.where(low, re, pltpu.roll(im, 64, 1))
                odd = jnp.where(low, pltpu.roll(re, 64, 1), im)
                out[pl.ds(2 * tile * MSG + row + pm, 32, stride=4 * MSG), :] = even
                out[pl.ds((2 * tile + 1) * MSG + row + pm, 32, stride=4 * MSG), :] = odd

    for rp in range(2):
        for pm in range(2):
            def block(c, _, pm=pm, rp=rp):
                first = (pm * 2 + rp) * 16 + 2 * c
                key = jnp.concatenate(
                    [tabt[pl.ds(quarter * 64 + first + k, 1), :] for k in range(2)], axis=1
                )
                parts = [split(recv[pl.ds(first + k, 128, stride=64), :]) for k in range(2)]
                rhs = jnp.concatenate(
                    [
                        jnp.concatenate([parts[0][0], parts[0][1]], axis=1),
                        jnp.concatenate([parts[1][0], parts[1][1]], axis=1),
                    ],
                    axis=0,
                )
                for chunk in range(4):
                    tile = lax.broadcasted_iota(I32, (128, 256), 0) + chunk * 128
                    hit = jnp.where(tile == key, 1.0, 0.0).astype(BF)
                    s = dot(hit, rhs)
                    hi, lo = split(s[:, :128] + s[:, 128:])
                    for i in range(4):
                        at = pl.multiple_of((chunk * 4 + i) * 256 + c * 32, 32)
                        ghl[pm, pl.ds(at, 32), :128] = hi[i * 32:i * 32 + 32]
                        ghl[pm, pl.ds(at, 32), 128:] = lo[i * 32:i * 32 + 32]
                return 0

            lax.fori_loop(0, 8, block, 0)
        zc[...] = jnp.zeros((128, 256), F32)

        def row(t, _, rp=rp):
            @pl.when((kind == 1) & (t > 0))
            def _():
                zc[...] = mix(2, 1)

            columns(0, t)
            columns(1, 15 - t)
            z = mix(0, 0) + mix(1, 1) + zc[...]
            emit(z, rp * 32 + 2 * t, (0, 1))
            return 0

        lax.fori_loop(0, 16, row, 0)

        @pl.when(kind == 1)
        def _(rp=rp):
            emit(mix(2, 1), 64 + rp, (0,))


def middle(dev, recv, table):
    t = tables()
    smem = pl.BlockSpec(memory_space=pltpu.SMEM)
    whole = pl.BlockSpec(memory_space=pltpu.VMEM)
    return pl.pallas_call(
        middle_kernel,
        out_shape=jax.ShapeDtypeStruct((128 * MSG, 128), F32),
        in_specs=[smem] + [whole] * 7,
        out_specs=whole,
        scratch_shapes=[
            pltpu.VMEM((256, 128), I32),
            pltpu.VMEM((2, 16 * 256, 256), BF),
            pltpu.VMEM((2, 256, 256), BF),
            pltpu.VMEM((2, 256, 256), BF),
            pltpu.VMEM((128, 256), F32),
        ],
        compiler_params=pltpu.CompilerParams(vmem_limit_bytes=VMEM),
        name="middle",
    )(dev, recv, table, t["wc"][0], t["wc"][1], t["tw"][0], t["tw"][1], t["f"])


def final_kernel(x, wh, wl, sh, sl, xh, xl, tj, out, val):
    pair = pl.program_id(1)

    def three(a, bh, bl):
        ah, al = split(a)
        return dot(ah, bh) + dot(al, bh) + dot(ah, bl)

    rows = jnp.concatenate([x[0, 0, q, :64, :] for q in range(4)], axis=0)
    a = rows.T

    @pl.when(pair > 0)
    def _():
        u = three(a, wh[...], wl[...])
        vr = u[:64, :256] - u[64:, 256:]
        vi = u[:64, 256:] + u[64:, :256]
        tr, ti = tj[0, 0:1, :], tj[0, 1:2, :]
        val[2 * pair] = vr * tr - vi * ti
        val[2 * pair + 1] = vr * ti + vi * tr

    @pl.when(pair == 0)
    def _():
        extra = jnp.concatenate([x[0, 0, q, 64:72, :] for q in range(4)], axis=0)
        extra = jnp.concatenate([extra, jnp.zeros((96, 128), F32)], axis=0).T[:, :32]
        v = three(a[:64], sh[0], sl[0]) + three(a[64:], sh[1], sl[1])
        v = v + three(extra[:64], xh[0], xl[0]) + three(extra[64:], xh[1], xl[1])
        val[0] = v[:, :256]
        val[1] = v[:, 256:]

    @pl.when(pair == 15)
    def _():
        index = {}
        for i, j in enumerate(PAIR_J):
            if i > 0:
                index[j if j < 16 else 32 - j] = (i, 1.0 if j < 16 else -1.0)

        def strip(i, _):
            at = pl.ds(pl.multiple_of(i * 8, 8), 8)
            for tile in range(2):
                lanes = slice(tile * 128, tile * 128 + 128)
                zero, mid = val[0, at, lanes], val[1, at, lanes]
                re = {j: val[2 * k, at, lanes] for j, (k, _) in index.items()}
                im = {j: val[2 * k + 1, at, lanes] for j, (k, _) in index.items()}

                def wave(fun, part, js, l1, signed):
                    total = None
                    for j in js:
                        turn = j * l1 % 32
                        c = fun(2 * math.pi * turn / 32)
                        if signed:
                            c = c * index[j][1]
                        if abs(c) < 1e-12:
                            continue
                        if abs(abs(c) - 1) < 1e-12:
                            term = part[j]
                            if total is None:
                                total = term if c > 0 else -term
                            else:
                                total = total + term if c > 0 else total - term
                        else:
                            term = part[j] * c
                            total = term if total is None else total + term
                    return total if total is not None else jnp.zeros((8, 128), F32)

                odd = range(1, 16, 2)
                ce, se = [None] * 9, [None] * 9
                for l1 in range(5):
                    sign = 1.0 if l1 % 2 == 0 else -1.0
                    ee = wave(math.cos, re, (4, 8, 12), l1, False)
                    ee = ee + (zero + mid if sign > 0 else zero - mid)
                    eo = wave(math.cos, re, (2, 6, 10, 14), l1, False)
                    oe = wave(math.sin, im, (4, 8, 12), l1, True)
                    oo = wave(math.sin, im, (2, 6, 10, 14), l1, True)
                    ce[l1], ce[8 - l1] = ee + eo, ee - eo
                    se[l1], se[8 - l1] = oe + oo, oo - oe
                for l1 in range(9):
                    co = wave(math.cos, re, odd, l1, False)
                    so = wave(math.sin, im, odd, l1, True)
                    p, m = ce[l1] + co, ce[l1] - co
                    s, d = se[l1] + so, se[l1] - so

                    def put(l, value):
                        out[0, at, l * 256 + tile * 128:l * 256 + tile * 128 + 128] = value

                    put(l1, p + s)
                    put(16 + l1, m + d)
                    if l1 > 0:
                        put(32 - l1, p - s)
                        if l1 < 8:
                            put(16 - l1, m - d)
            return 0

        lax.fori_loop(0, 8, strip, 0)


def final(recv):
    t = tables()
    whole = pl.BlockSpec(memory_space=pltpu.VMEM)
    return pl.pallas_call(
        final_kernel,
        grid=(2, 16),
        out_shape=jax.ShapeDtypeStruct((2, 64, 8192), F32),
        in_specs=[pl.BlockSpec((1, 1, 4, MSG, 128), lambda f, j: (j, f, 0, 0, 0))]
        + [whole] * 6
        + [pl.BlockSpec((1, 2, 256), lambda f, j: (j, 0, 0))],
        out_specs=pl.BlockSpec((1, 64, 8192), lambda f, j: (f, 0, 0)),
        scratch_shapes=[pltpu.VMEM((32, 64, 256), F32)],
        compiler_params=pltpu.CompilerParams(vmem_limit_bytes=VMEM),
        name="final",
    )(recv, *t["wr"], *t["ws"], *t["wx"], t["tj"])


def pixel_view(pixels):
    x = pixels.reshape(128, 2, 2, 8, 128).transpose(0, 1, 3, 2, 4)
    return x.reshape(128, 2, 16, 128)


def beam_view(aterms):
    x = aterms.reshape(512, 2, 2, 2, 8, 128).transpose(0, 1, 2, 4, 3, 5)
    return x.reshape(1024, 2, 16, 128)


def pack(tile_offsets, station_pairs, time_blocks, channel_blocks):
    return jnp.concatenate(
        [
            tile_offsets[:, 0], tile_offsets[:, 1],
            station_pairs[:, 0] * 2 + time_blocks, station_pairs[:, 1] * 2 + time_blocks,
            channel_blocks,
        ]
    )


def local(
    subgrid_pixels, tile_offsets, station_pairs, time_blocks, channel_blocks, valid_counts,
    aterms, channel_weights,
):
    axes = ("row", "col")
    me = lax.axis_index(axes)
    packed = pack(tile_offsets, station_pairs, time_blocks, channel_blocks)
    table, target = slots(packed, valid_counts)
    everyone = lax.all_gather(table, axes, axis=0, tiled=False)
    send = source(
        packed, valid_counts, channel_weights, target.reshape(1, 128),
        pixel_view(subgrid_pixels), beam_view(aterms),
    )
    recv = lax.all_to_all(send, axes, split_axis=0, concat_axis=0, tiled=True)
    dev = jnp.stack([(me < 8).astype(I32), me % 4]).astype(I32)
    half = middle(dev, recv.reshape(128 * 64, 128), everyone)
    half = lax.all_to_all(
        half.reshape(128, MSG, 128), axes, split_axis=0, concat_axis=0, tiled=True
    )
    return final(half.reshape(16, 2, 4, MSG, 128))


def solution(mesh):
    in_specs = (
        P(("row", "col"), None, None, None),
        P(("row", "col"), None),
        P(("row", "col"), None),
        P(("row", "col")),
        P(("row", "col")),
        P(("row", "col")),
        P(),
        P(),
    )
    out_specs = P(None, ("row", "col"), None)
    return jax.shard_map(local, mesh=mesh, in_specs=in_specs, out_specs=out_specs, check_vma=False)
```

time: 777 us -> 256 us (0.33)
  local copies, waits for them, and re-layouts: 252 us -> 3.29 us
  waiting for transfers between devices: 208 us -> 0.01 us
  matrix products: 184 us -> 0 us
  blocking collectives: 0 us -> 140 us
  Pallas kernels: 0 us -> 96.6 us
  other arithmetic: 87.6 us -> 2.03 us
  starting transfers between devices: 34.7 us -> 12 us
    all_to_all x4 -> x1, waiting for transfers between devices: 208 us -> 0.01 us  [local(): recv = lax.all_to_all(send, axes, split_axis=0, concat_axis=0, tiled=True)]
    dot_general x14 -> x0, matrix products: 159 us -> none  [the longest x1 27.6 us: correct_subgrids(): jnp.dot(flat_real, dft_imag, precision=EXACT)]
    reshape x5 -> x0, local copies, waits for them, and re-layouts: 109 us -> none  [the longest x2 60.5 us: local(): summed.reshape(tile_rows, tile_cols, 2, 2, SUB, SUB)]
    pallas_call x0 -> x4, Pallas kernels: none -> 96.6 us  [the longest x1 51 us: middle(): pl.pallas_call(middle_kernel, out_shape=jax.ShapeDtypeStruct((128 * MSG,...]
    all_gather x0 -> x1, blocking collectives: none -> 77.1 us  [local(): everyone = lax.all_gather(table, axes, axis=0, tiled=False)]
    all_to_all x0 -> x1, blocking collectives: none -> 63.4 us  [local(): lax.all_to_all(half.reshape(128, MSG, 128), axes, split_axis=0, concat_ax...]
    slice x9 -> x0, local copies, waits for them, and re-layouts: 56.1 us -> none  [the longest x2 19.2 us: local(): spectrum_block[2:]]
    scatter-add x1 -> x0, other arithmetic: 42.7 us -> none  [local(): jax.ops.segment_sum(spectra, tile_index, num_segments=tiles_dev + 1)]
  transfers between devices with their start and end apart: 4 -> 1, of which waited for: 3 -> 0; matrix products, arithmetic and copies ran while one was open for 8% -> 1% of each run, Pallas kernels for 0% -> 0%
where the time goes in v1:
time: 256 us; the launch traced here: 255 us
  blocking collectives  140 us (55%)
  Pallas kernels  96.6 us (38%)
  starting transfers between devices  12 us (5%)
  local copies, waits for them, and re-layouts  3.29 us (1%)
    all_gather x1, blocking collectives, local(): everyone = lax.all_gather(table, axes, axis=0, tiled=False)  77.1 us
    all_to_all x1, blocking collectives, local(): lax.all_to_all(half.reshape(128, MSG, 128), axes, split_axis=0, concat_ax...  63.4 us
    pallas_call x1, Pallas kernels, middle(): pl.pallas_call(middle_kernel, out_shape=jax.ShapeDtypeStruct((128 * MSG,...  51 us
    pallas_call x1, Pallas kernels, final(): pl.pallas_call(final_kernel, grid=(2, 16), out_shape=jax.ShapeDtypeStruct...  26.4 us
    pallas_call x1, Pallas kernels, source(): pl.pallas_call(source_kernel, grid=(8,), out_shape=jax.ShapeDtypeStruct((...  13.5 us
    all_to_all x1, starting transfers between devices, local(): recv = lax.all_to_all(send, axes, split_axis=0, concat_axis=0, tiled=True)  12 us
    pallas_call x1, Pallas kernels, slots(): pl.pallas_call(slot_kernel, out_shape=(jax.ShapeDtypeStruct((256,), I32),...  5.84 us
  transfers between devices with their start and end apart: 1, of which 0 were waited for; matrix products, arithmetic and copies ran while one was open for 1% of the time, Pallas kernels for 0%

profile of v1, /device:TPU:1, one launch (start us, length us, event | category | flops | bytes accessed | tf_op | source)
XLA Modules:
  0.0 255.1 jit_solution(911437523315618507)
XLA Ops:
  0.7 0.7 constant_dynamic-update-slice_fusion.4
  1.3 0.7 constant_dynamic-update-slice_fusion.3
  2.0 0.7 constant_dynamic-update-slice_fusion.2
  2.7 0.7 constant_dynamic-update-slice_fusion.1
  3.4 0.7 constant_dynamic-update-slice_fusion.pk
  4.1 0.0 copy-start
  4.1 0.6 copy-done
  4.7 5.8 %slots.1 = (s32[256]{0:T(256)}, s32[128]{0:T(128)}) custom-call(s32[640]{0:T(1024)} %copy-done, s32[1]{0:T(128)S(6)} %copy.37.vc), custom_call_target="tpu_custom_call" | custom-call | tf_op jit(solution)/shard_map/slots/pallas_call | solution.py:151
  10.5 13.5 %source.1 = f32[128,64,128]{2,1,0:T(8,128)} custom-call(s32[640]{0:T(1024)} %copy-done, s32[1]{0:T(128)S(6)} %copy.37.vc, f32[8]{0:T(128)} %cw.1, s32[8]{0:T(128)} %constant.58.clone.ja, s32[8]{0:T(128)} %constant.59.clone.jb, s32[1,128]{1,0:T(1,128)} %bitcast.38, f32[128,2,16,128]{3,2,1,0:T(8,128)} %bitcast.35, bf16[1024,2,16,128]{3,2,1,0:T(8,128)(2,1)} %bitcast.34, ...), custom_call_target="tpu_custom_call" | custom-call | tf_op jit(solution)/shard_map/source/pallas_call | solution.py:251
  24.0 0.0 copy-start.1
  24.0 12.0 %all-to-all-start = ((f32[128,64,128]{2,1,0:T(8,128)}), f32[128,64,128]{2,1,0:T(8,128)}, u32[]{:S(2)}, u32[]{:S(2)}) async-start(f32[128,64,128]{2,1,0:T(8,128)} %source.1), calls=%async_computation | async-start | bytes 8388608 | tf_op jit(solution)/shard_map/all_to_all | solution.py:525
  36.0 0.0 copy-done.1
  36.0 77.1 %all-gather.1 = s32[128,1,256]{2,1,0:T(1,128)S(1)} all-gather(s32[1,1,256]{2,1,0:T(1,128)S(1)} %bitcast.37), channel_id=2, replica_groups=mesh['row'=16,'col'=8] {'row','col'}, dimensions={0}, use_global_device_ids=true | all-gather | bytes 132096 | tf_op jit(solution)/shard_map/all_gather | solution.py:520
  113.1 0.7 copy.31
  113.8 0.6 pad_add_fusion.dev
  114.4 0.0 all-to-all-done
  114.4 51.0 %middle.1 = f32[9216,128]{1,0:T(8,128)} custom-call(s32[2]{0:T(128)} %pad_add_fusion.dev, f32[8192,128]{1,0:T(8,128)} %bitcast.13.recv, s32[128,256]{1,0:T(8,128)} %bitcast.36, bf16[512,256]{1,0:T(8,128)(2,1)} %constant.62.clone.wh, bf16[512,256]{1,0:T(8,128)(2,1)} %constant.63.clone.wl, f32[256,128]{1,0:T(8,128)} %constant.64.clone.twr, ...), custom_call_target="tpu_custom_call" | custom-call | tf_op jit(solution)/shard_map/middle/pallas_call | solution.py:364
  165.4 63.4 %all_to_all.10 = f32[128,72,128]{2,1,0:T(8,128)} all-to-all(f32[128,72,128]{2,1,0:T(8,128)} %bitcast.32), channel_id=1, replica_groups=mesh['row'=16,'col'=8] {'row','col'}, dimensions={0} | all-to-all | bytes 9437184 | tf_op jit(solution)/shard_map/all_to_all | solution.py:528
  228.7 26.4 %final.1 = f32[2,64,8192]{2,1,0:T(8,128)} custom-call(f32[16,2,4,72,128]{4,3,2,1,0:T(8,128)} %bitcast.33, bf16[256,512]{1,0:T(8,128)(2,1)} %constant.67.clone.wh, bf16[256,512]{1,0:T(8,128)(2,1)} %constant.68.clone.wl, bf16[2,256,512]{2,1,0:T(8,128)(2,1)} %constant.69.clone.sh, bf16[2,256,512]{2,1,0:T(8,128)(2,1)} %constant.70.clone.sl, ...), custom_call_target="tpu_custom_call" | custom-call | tf_op jit(solution)/shard_map/final/pallas_call | solution.py:478
  (1 shorter events, 0.0 us)
Async XLA Ops:
  4.1 0.6 copy-start
  24.0 12.0 %copy-start.1 = (s32[256]{0:T(256)S(1)}, s32[256]{0:T(256)}, u32[]{:S(2)}) copy-start(s32[256]{0:T(256)} %get-tuple-element.8) | copy-start | bytes 3076
  24.0 90.4 %all-to-all-start = ((f32[128,64,128]{2,1,0:T(8,128)}), f32[128,64,128]{2,1,0:T(8,128)}, u32[]{:S(2)}, u32[]{:S(2)}) async-start(f32[128,64,128]{2,1,0:T(8,128)} %source.1), calls=%async_computation | async-start | bytes 8388608 | tf_op jit(solution)/shard_map/all_to_all | solution.py:525

commit v2 on v1

--- a/solution.py
+++ b/solution.py
@@ -17,7 +17,6 @@
 PAIR_J = (0, 8, 4, 12, 1, 9, 17, 25, 2, 10, 18, 26, 3, 11, 19, 27)
 STEP_A = (0, 4, 1, 1, 2, 2, 3, 3)
 STEP_B = (0, 4, 7, 7, 6, 6, 5, 5)
-MSG = 72
 VMEM = 56 * 1024 * 1024
 
 
@@ -117,8 +116,8 @@
 def slot_kernel(pk, vc, table, target, count):
     def clear(i, _):
         count[i] = 0
-        table[2 * i] = -1
-        table[2 * i + 1] = -1
+        for k in range(4):
+            table[4 * i + k] = -1
         return 0
 
     lax.fori_loop(0, 128, clear, 0)
@@ -129,7 +128,7 @@
         block_row = row // 16
         low = block_row < 8
         near = jnp.where(low, block_row, 15 - block_row)
-        place_row = near // 2 * 4 + near % 2 + jnp.where(low, 0, 2)
+        place_row = near // 2 * 4 + near % 2 * 2 + jnp.where(low, 0, 1)
         block = place_row * 8 + col // 32
         rank = count[block]
         valid = s < vc[0]
@@ -139,7 +138,7 @@
         @pl.when(valid)
         def _():
             count[block] = rank + 1
-            table[slot] = row % 16 * 32 + col % 32
+            table[slot // 64 * 128 + slot % 64] = row % 16 * 32 + col % 32
 
         return 0
 
@@ -150,7 +149,7 @@
     smem = pl.BlockSpec(memory_space=pltpu.SMEM)
     return pl.pallas_call(
         slot_kernel,
-        out_shape=(jax.ShapeDtypeStruct((256,), I32), jax.ShapeDtypeStruct((128,), I32)),
+        out_shape=(jax.ShapeDtypeStruct((512,), I32), jax.ShapeDtypeStruct((128,), I32)),
         in_specs=[smem, smem],
         out_specs=(smem, smem),
         scratch_shapes=[pltpu.SMEM((128,), I32)],
@@ -271,14 +270,61 @@
     )
 
 
-def middle_kernel(
-    dev, recv, tab, wh, wl, twr, twi, fmat, out, tabt, ghl, pqh, pql, zc
+def spread(i):
+    o = lax.rem(i * 37, 128)
+    row, col = lax.axis_index("row"), lax.axis_index("col")
+    x = lax.rem(lax.div(row, 4) + lax.div(o, 32), 4)
+    y = lax.rem(lax.rem(row, 4) + lax.rem(lax.div(o, 8), 4), 4)
+    z = lax.rem(lax.div(col, 2) + lax.rem(lax.div(o, 2), 4), 4)
+    c = lax.rem(col + o, 2)
+    return x * 4 + y, z * 2 + c
+
+
+def exchange_kernel(
+    send, tabs, wh, wl, twr, twi, fmat, out, outx,
+    recv, tabr, tabt, ghl, pqh, pql, zc, stage, extra, ssem, rsem, lsem
 ):
-    kind = dev[0]
-    quarter = dev[1]
-    tabt[...] = tab[...].T
-    for d in range(128):
-        out[d * MSG + 64:d * MSG + 72, :] = jnp.zeros((8, 128), F32)
+    me = lax.axis_index("row") * 8 + lax.axis_index("col")
+    first = me < 8
+    kind = jnp.where(first, 1, 0)
+    barrier = pltpu.get_barrier_semaphore()
+
+    def each(fun):
+        def step(i, _):
+            row, col = spread(i)
+            fun(row * 8 + col, (row, col))
+            return 0
+
+        lax.fori_loop(1, 128, step, 0)
+
+    def push(src, dst, k, dev):
+        pltpu.make_async_remote_copy(
+            src_ref=src, dst_ref=dst, send_sem=ssem.at[k], recv_sem=rsem.at[k],
+            device_id=dev, device_id_type=pl.DeviceIdType.MESH,
+        ).start()
+
+    def wait(part, sem):
+        pltpu.make_async_copy(part, part, sem).wait()
+
+    def keep(src, dst):
+        copy = pltpu.make_async_copy(src, dst, lsem)
+        copy.start()
+        copy.wait()
+
+    each(lambda d, dev: pl.semaphore_signal(
+        barrier, inc=1, device_id=dev, device_id_type=pl.DeviceIdType.MESH))
+    pl.semaphore_wait(barrier, 127)
+    each(lambda d, dev: push(tabs.at[lax.rem(d, 4)], tabr.at[me], 0, dev))
+    for rp in range(2):
+        rows = pl.ds(rp * 32, 32)
+        each(lambda d, dev: push(send.at[d, rows], recv.at[me, rows], 1 + rp, dev))
+    keep(tabs.at[lax.rem(me, 4)], tabr.at[me])
+    keep(send.at[me], recv.at[me])
+    flat = recv.reshape(128 * 64, 128)
+
+    extra[...] = jnp.zeros((1024, 128), F32)
+    wait(tabr.at[pl.ds(0, 127)], rsem.at[0])
+    tabt[...] = tabr[...].reshape(128, 128).T
     lane = lax.broadcasted_iota(I32, (32, 128), 1)
     low = lane < 64
 
@@ -300,92 +346,126 @@
         z = dot_nt(both, pqh[pm])
         return z[:128] + z[128:] + dot_nt(both[:128], pql[pm])
 
-    def emit(z, row, pms):
+    def emit(dst, size, z, row, pms):
         for pm in pms:
             for tile in range(2):
                 lanes = slice(tile * 128, tile * 128 + 128)
                 re, im = z[pm * 64:pm * 64 + 32, lanes], z[pm * 64 + 32:pm * 64 + 64, lanes]
                 even = jnp.where(low, re, pltpu.roll(im, 64, 1))
                 odd = jnp.where(low, pltpu.roll(re, 64, 1), im)
-                out[pl.ds(2 * tile * MSG + row + pm, 32, stride=4 * MSG), :] = even
-                out[pl.ds((2 * tile + 1) * MSG + row + pm, 32, stride=4 * MSG), :] = odd
-
-    for rp in range(2):
+                dst[pl.ds(2 * tile * size + row + pm, 32, stride=4 * size), :] = even
+                dst[pl.ds((2 * tile + 1) * size + row + pm, 32, stride=4 * size), :] = odd
+
+    def phase(rp, _):
+        rows = pl.ds(pl.multiple_of(rp * 32, 32), 32)
+        wait(recv.at[pl.ds(0, 127), rows], rsem.at[1 + rp])
         for pm in range(2):
-            def block(c, _, pm=pm, rp=rp):
-                first = (pm * 2 + rp) * 16 + 2 * c
-                key = jnp.concatenate(
-                    [tabt[pl.ds(quarter * 64 + first + k, 1), :] for k in range(2)], axis=1
-                )
-                parts = [split(recv[pl.ds(first + k, 128, stride=64), :]) for k in range(2)]
-                rhs = jnp.concatenate(
-                    [
-                        jnp.concatenate([parts[0][0], parts[0][1]], axis=1),
-                        jnp.concatenate([parts[1][0], parts[1][1]], axis=1),
-                    ],
-                    axis=0,
-                )
+            def block(c, _, pm=pm):
+                at = rp * 32 + pm * 16 + 2 * c
+                key = jnp.concatenate([tabt[pl.ds(at + k, 1), :] for k in range(2)], axis=1)
+                parts = [split(flat[pl.ds(at + k, 128, stride=64), :]) for k in range(2)]
+                rhs = jnp.concatenate([jnp.concatenate(p, axis=1) for p in parts], axis=0)
                 for chunk in range(4):
                     tile = lax.broadcasted_iota(I32, (128, 256), 0) + chunk * 128
                     hit = jnp.where(tile == key, 1.0, 0.0).astype(BF)
                     s = dot(hit, rhs)
                     hi, lo = split(s[:, :128] + s[:, 128:])
                     for i in range(4):
-                        at = pl.multiple_of((chunk * 4 + i) * 256 + c * 32, 32)
-                        ghl[pm, pl.ds(at, 32), :128] = hi[i * 32:i * 32 + 32]
-                        ghl[pm, pl.ds(at, 32), 128:] = lo[i * 32:i * 32 + 32]
+                        to = pl.multiple_of((chunk * 4 + i) * 256 + c * 32, 32)
+                        ghl[pm, pl.ds(to, 32), :128] = hi[i * 32:i * 32 + 32]
+                        ghl[pm, pl.ds(to, 32), 128:] = lo[i * 32:i * 32 + 32]
                 return 0
 
             lax.fori_loop(0, 8, block, 0)
         zc[...] = jnp.zeros((128, 256), F32)
 
-        def row(t, _, rp=rp):
-            @pl.when((kind == 1) & (t > 0))
+        def row(t, _):
+            @pl.when(first & (t > 0))
             def _():
                 zc[...] = mix(2, 1)
 
             columns(0, t)
             columns(1, 15 - t)
-            z = mix(0, 0) + mix(1, 1) + zc[...]
-            emit(z, rp * 32 + 2 * t, (0, 1))
+            emit(stage, 64, mix(0, 0) + mix(1, 1) + zc[...], rp * 32 + 2 * t, (0, 1))
             return 0
 
         lax.fori_loop(0, 16, row, 0)
 
-        @pl.when(kind == 1)
-        def _(rp=rp):
-            emit(mix(2, 1), 64 + rp, (0,))
-
-
-def middle(dev, recv, table):
+        @pl.when(first)
+        def _():
+            emit(extra, 8, mix(2, 1), rp, (0,))
+
+        def piece(d):
+            return stage.at[pl.ds(pl.multiple_of(d * 64 + rp * 32, 32), 32), :]
+
+        each(lambda d, dev: push(piece(d), out.at[me, rows], 3 + rp, dev))
+        keep(piece(me), out.at[me, rows])
+        return 0
+
+    lax.fori_loop(0, 2, phase, 0)
+
+    def piece(d):
+        return extra.at[pl.ds(pl.multiple_of(d * 8, 8), 8), :]
+
+    @pl.when(first)
+    def _():
+        each(lambda d, dev: push(piece(d), outx.at[me], 5, dev))
+        keep(piece(me), outx.at[me])
+        wait(outx.at[pl.ds(0, 7)], rsem.at[5])
+        wait(extra.at[pl.ds(0, 127 * 8), :], ssem.at[5])
+
+    @pl.when(me >= 8)
+    def _():
+        wait(outx, rsem.at[5])
+
+    wait(tabr.at[pl.ds(0, 127)], ssem.at[0])
+    for rp in range(2):
+        part = recv.at[pl.ds(0, 127), pl.ds(rp * 32, 32)]
+        wait(part, ssem.at[1 + rp])
+        wait(part, ssem.at[3 + rp])
+        wait(out.at[pl.ds(0, 127), pl.ds(rp * 32, 32)], rsem.at[3 + rp])
+
+
+def exchange(send, tabs):
     t = tables()
-    smem = pl.BlockSpec(memory_space=pltpu.SMEM)
     whole = pl.BlockSpec(memory_space=pltpu.VMEM)
+    away = pl.BlockSpec(memory_space=pl.ANY)
     return pl.pallas_call(
-        middle_kernel,
-        out_shape=jax.ShapeDtypeStruct((128 * MSG, 128), F32),
-        in_specs=[smem] + [whole] * 7,
-        out_specs=whole,
+        exchange_kernel,
+        out_shape=(
+            jax.ShapeDtypeStruct((128, 64, 128), F32), jax.ShapeDtypeStruct((8, 8, 128), F32)
+        ),
+        in_specs=[away, whole] + [whole] * 5,
+        out_specs=(away, away),
         scratch_shapes=[
-            pltpu.VMEM((256, 128), I32),
+            pltpu.VMEM((128, 64, 128), F32),
+            pltpu.VMEM((128, 1, 128), I32),
+            pltpu.VMEM((128, 128), I32),
             pltpu.VMEM((2, 16 * 256, 256), BF),
             pltpu.VMEM((2, 256, 256), BF),
             pltpu.VMEM((2, 256, 256), BF),
             pltpu.VMEM((128, 256), F32),
+            pltpu.VMEM((128 * 64, 128), F32),
+            pltpu.VMEM((128 * 8, 128), F32),
+            pltpu.SemaphoreType.DMA((6,)),
+            pltpu.SemaphoreType.DMA((6,)),
+            pltpu.SemaphoreType.DMA,
         ],
-        compiler_params=pltpu.CompilerParams(vmem_limit_bytes=VMEM),
-        name="middle",
-    )(dev, recv, table, t["wc"][0], t["wc"][1], t["tw"][0], t["tw"][1], t["f"])
-
-
-def final_kernel(x, wh, wl, sh, sl, xh, xl, tj, out, val):
+        compiler_params=pltpu.CompilerParams(
+            vmem_limit_bytes=VMEM, collective_id=0, has_side_effects=True
+        ),
+        name="exchange",
+    )(send, tabs, t["wc"][0], t["wc"][1], t["tw"][0], t["tw"][1], t["f"])
+
+
+def final_kernel(x, ex, wh, wl, sh, sl, xh, xl, tj, out, val):
     pair = pl.program_id(1)
 
     def three(a, bh, bl):
         ah, al = split(a)
         return dot(ah, bh) + dot(al, bh) + dot(ah, bl)
 
-    rows = jnp.concatenate([x[0, 0, q, :64, :] for q in range(4)], axis=0)
+    rows = jnp.concatenate([x[0, 0, q] for q in range(4)], axis=0)
     a = rows.T
 
     @pl.when(pair > 0)
@@ -399,7 +479,7 @@
 
     @pl.when(pair == 0)
     def _():
-        extra = jnp.concatenate([x[0, 0, q, 64:72, :] for q in range(4)], axis=0)
+        extra = jnp.concatenate([ex[0, q] for q in range(4)], axis=0)
         extra = jnp.concatenate([extra, jnp.zeros((96, 128), F32)], axis=0).T[:, :32]
         v = three(a[:64], sh[0], sl[0]) + three(a[64:], sh[1], sl[1])
         v = v + three(extra[:64], xh[0], xl[0]) + three(extra[64:], xh[1], xl[1])
@@ -472,21 +552,24 @@
         lax.fori_loop(0, 8, strip, 0)
 
 
-def final(recv):
+def final(recv, extra):
     t = tables()
     whole = pl.BlockSpec(memory_space=pltpu.VMEM)
     return pl.pallas_call(
         final_kernel,
         grid=(2, 16),
         out_shape=jax.ShapeDtypeStruct((2, 64, 8192), F32),
-        in_specs=[pl.BlockSpec((1, 1, 4, MSG, 128), lambda f, j: (j, f, 0, 0, 0))]
+        in_specs=[
+            pl.BlockSpec((1, 1, 4, 64, 128), lambda f, j: (j, f, 0, 0, 0)),
+            pl.BlockSpec((1, 4, 8, 128), lambda f, j: (f, 0, 0, 0)),
+        ]
         + [whole] * 6
         + [pl.BlockSpec((1, 2, 256), lambda f, j: (j, 0, 0))],
         out_specs=pl.BlockSpec((1, 64, 8192), lambda f, j: (f, 0, 0)),
         scratch_shapes=[pltpu.VMEM((32, 64, 256), F32)],
         compiler_params=pltpu.CompilerParams(vmem_limit_bytes=VMEM),
         name="final",
-    )(recv, *t["wr"], *t["ws"], *t["wx"], t["tj"])
+    )(recv, extra, *t["wr"], *t["ws"], *t["wx"], t["tj"])
 
 
 def pixel_view(pixels):
@@ -513,22 +596,14 @@
     subgrid_pixels, tile_offsets, station_pairs, time_blocks, channel_blocks, valid_counts,
     aterms, channel_weights,
 ):
-    axes = ("row", "col")
-    me = lax.axis_index(axes)
     packed = pack(tile_offsets, station_pairs, time_blocks, channel_blocks)
     table, target = slots(packed, valid_counts)
-    everyone = lax.all_gather(table, axes, axis=0, tiled=False)
     send = source(
         packed, valid_counts, channel_weights, target.reshape(1, 128),
         pixel_view(subgrid_pixels), beam_view(aterms),
     )
-    recv = lax.all_to_all(send, axes, split_axis=0, concat_axis=0, tiled=True)
-    dev = jnp.stack([(me < 8).astype(I32), me % 4]).astype(I32)
-    half = middle(dev, recv.reshape(128 * 64, 128), everyone)
-    half = lax.all_to_all(
-        half.reshape(128, MSG, 128), axes, split_axis=0, concat_axis=0, tiled=True
-    )
-    return final(half.reshape(16, 2, 4, MSG, 128))
+    half, extra = exchange(send, table.reshape(4, 1, 128))
+    return final(half.reshape(16, 2, 4, 64, 128), extra.reshape(2, 4, 8, 128))
 
 
 def solution(mesh):

time: 256 us -> 179 us (0.70)
  the two profiles are of different devices: /device:TPU:1 before, /device:TPU:2 now
where the time goes in v2:
time: 179 us; the launch traced here: 178 us
  Pallas kernels  174 us (97%)
  local copies, waits for them, and re-layouts  2.62 us (1%)
    pallas_call x1, Pallas kernels, exchange(): pl.pallas_call(exchange_kernel, out_shape=(jax.ShapeDtypeStruct((128, 64,...  127 us
    pallas_call x1, Pallas kernels, final(): pl.pallas_call(final_kernel, grid=(2, 16), out_shape=jax.ShapeDtypeStruct...  26.5 us
    pallas_call x1, Pallas kernels, source(): pl.pallas_call(source_kernel, grid=(8,), out_shape=jax.ShapeDtypeStruct((...  13.5 us
    pallas_call x1, Pallas kernels, slots(): pl.pallas_call(slot_kernel, out_shape=(jax.ShapeDtypeStruct((512,), I32),...  7.01 us

profile of v2, /device:TPU:2, one launch (start us, length us, event | category | flops | bytes accessed | tf_op | source)
XLA Modules:
  0.0 178.5 jit_solution(12010330156987181025)
XLA Ops:
  0.7 0.7 constant_dynamic-update-slice_fusion.4
  1.3 0.7 constant_dynamic-update-slice_fusion.3
  2.0 0.7 constant_dynamic-update-slice_fusion.2
  2.7 0.7 constant_dynamic-update-slice_fusion.1
  3.4 0.7 constant_dynamic-update-slice_fusion.pk
  4.1 0.0 copy-start
  4.1 0.6 copy-done
  4.7 7.0 %slots.1 = (s32[512]{0:T(512)}, s32[128]{0:T(128)}) custom-call(s32[640]{0:T(1024)} %copy-done, s32[1]{0:T(128)S(6)} %copy.32.vc), custom_call_target="tpu_custom_call" | custom-call | tf_op jit(solution)/shard_map/slots/pallas_call | solution.py:150
  11.7 13.5 %source.1.send = f32[128,64,128]{2,1,0:T(8,128)} custom-call(s32[640]{0:T(1024)} %copy-done, s32[1]{0:T(128)S(6)} %copy.32.vc, f32[8]{0:T(128)} %cw.1, s32[8]{0:T(128)} %constant.34.clone.ja, s32[8]{0:T(128)} %constant.35.clone.jb, s32[1,128]{1,0:T(1,128)} %bitcast.31, f32[128,2,16,128]{3,2,1,0:T(8,128)} %bitcast.28, bf16[1024,2,16,128]{3,2,1,0:T(8,128)(2,1)} %bitcast.26, ...), custom_call_target="tpu_custom_call" | custom-call | tf_op jit(solution)/shard_map/source/pallas_call | solution.py:250
  25.2 126.8 %exchange.1 = (f32[128,64,128]{2,1,0:T(8,128)}, f32[8,8,128]{2,1,0:T(8,128)}) custom-call(f32[128,64,128]{2,1,0:T(8,128)} %source.1.send, s32[4,1,128]{2,1,0:T(1,128)} %bitcast.30, bf16[512,256]{1,0:T(8,128)(2,1)} %constant.38.clone.wh, bf16[512,256]{1,0:T(8,128)(2,1)} %constant.39.clone.wl, f32[256,128]{1,0:T(8,128)} %constant.40.clone.twr, ...), custom_call_target="tpu_custom_call" | custom-call | tf_op jit(solution)/shard_map/exchange/pallas_call | solution.py:433
  152.0 26.5 %final.1 = f32[2,64,8192]{2,1,0:T(8,128)} custom-call(f32[16,2,4,64,128]{4,3,2,1,0:T(8,128)} %bitcast.27, f32[2,4,8,128]{3,2,1,0:T(8,128)} %bitcast.29, bf16[256,512]{1,0:T(8,128)(2,1)} %constant.43.clone.wh, bf16[256,512]{1,0:T(8,128)(2,1)} %constant.44.clone.wl, bf16[2,256,512]{2,1,0:T(8,128)(2,1)} %constant.45.clone.sh, ...), custom_call_target="tpu_custom_call" | custom-call | tf_op jit(solution)/shard_map/final/pallas_call | solution.py:558
  (1 shorter events, 0.0 us)
Async XLA Ops:
  4.1 0.6 copy-start

commit v3 on v2

--- a/solution.py
+++ b/solution.py
@@ -113,48 +113,31 @@
     )
 
 
-def slot_kernel(pk, vc, table, target, count):
+def place(tiles, vc, table, count, perm):
     def clear(i, _):
         count[i] = 0
         for k in range(4):
             table[4 * i + k] = -1
         return 0
 
-    lax.fori_loop(0, 128, clear, 0)
-
-    def place(s, _):
-        row = pk[s]
-        col = pk[128 + s]
-        block_row = row // 16
+    lax.fori_loop(0, 128, clear, 0, unroll=8)
+    perm[...] = jnp.zeros((256, 128), F32)
+    lane = lax.broadcasted_iota(I32, (1, 128), 1)
+
+    def one(s, _):
+        row, col = tiles[0, s], tiles[1, s]
+        block_row = row >> 4
         low = block_row < 8
         near = jnp.where(low, block_row, 15 - block_row)
-        place_row = near // 2 * 4 + near % 2 * 2 + jnp.where(low, 0, 1)
-        block = place_row * 8 + col // 32
+        block = ((near << 1) + jnp.where(low, 0, 1)) * 8 + (col >> 5)
         rank = count[block]
-        valid = s < vc[0]
         slot = block * 2 + jnp.minimum(rank, 1)
-        target[s] = jnp.where(valid, slot, -1)
-
-        @pl.when(valid)
-        def _():
-            count[block] = rank + 1
-            table[slot // 64 * 128 + slot % 64] = row % 16 * 32 + col % 32
-
+        count[block] = rank + 1
+        table[((slot >> 6) << 7) + (slot & 63)] = ((row & 15) << 5) + (col & 31)
+        perm[pl.ds(slot, 1), :] = jnp.where(lane == s, 1.0, 0.0)
         return 0
 
-    lax.fori_loop(0, 128, place, 0)
-
-
-def slots(packed, count):
-    smem = pl.BlockSpec(memory_space=pltpu.SMEM)
-    return pl.pallas_call(
-        slot_kernel,
-        out_shape=(jax.ShapeDtypeStruct((512,), I32), jax.ShapeDtypeStruct((128,), I32)),
-        in_specs=[smem, smem],
-        out_specs=(smem, smem),
-        scratch_shapes=[pltpu.SMEM((128,), I32)],
-        name="slots",
-    )(packed, count)
+    lax.fori_loop(0, vc[0], one, 0)
 
 
 def dft8(re, im):
@@ -181,7 +164,8 @@
 
 
 def source_kernel(
-    pk, vc, cw, ja, jb, tgt, px, beams, bh, bl, out, got, corr, lhi, llo, perm, sems
+    tiles, pair, time, chan, vc, cw, ja, jb, px, beams, bh, bl, out, table,
+    got, corr, lhi, llo, perm, count, sems
 ):
     step = pl.program_id(0)
 
@@ -192,22 +176,19 @@
                 s = group * 16 + i
                 for e in range(2):
                     pltpu.make_async_copy(
-                        beams.at[pk[256 + 128 * e + s]], got.at[s, e], sems.at[group]
+                        beams.at[pair[e, s] * 2 + time[s]], got.at[s, e], sems.at[group]
                     ).start()
                 return 0
 
-            lax.fori_loop(0, 16, fetch, 0)
-        slot = lax.broadcasted_iota(I32, (256, 128), 0)
-        hit = jnp.where(slot == tgt[...], 1.0, 0.0).astype(BF)
-        perm[:, :128] = hit
-        perm[:, 128:] = hit
+            lax.fori_loop(0, 16, fetch, 0, unroll=4)
+        place(tiles, vc, table, count, perm)
         for group in range(8):
             part = got.at[pl.ds(group * 16, 16)]
             pltpu.make_async_copy(part, part, sems.at[group]).wait()
 
             def correct(i, _, group=group):
                 s = group * 16 + i
-                weight = jnp.where(s < vc[0], cw[pk[512 + s]], 0.0)
+                weight = jnp.where(s < vc[0], cw[chan[s]], 0.0)
                 ar, ai = got[s, 0, 0].astype(F32), got[s, 0, 1].astype(F32)
                 br, bi = got[s, 1, 0].astype(F32), got[s, 1, 1].astype(F32)
                 gr = (ar * br + ai * bi) * weight
@@ -235,37 +216,41 @@
         k = pick[step]
         acc = acc + dot(lhi[k], bh[0, half]) + dot(llo[k], bh[0, half]) + dot(lhi[k], bl[0, half])
     hi, lo = split(acc)
+    both = perm[...].astype(BF)
+    both = jnp.concatenate([both, both], axis=1)
     for f in range(2):
         rows = slice(f * 128, f * 128 + 128)
-        padded = dot(perm[...], jnp.concatenate([hi[rows], lo[rows]], axis=0))
+        padded = dot(both, jnp.concatenate([hi[rows], lo[rows]], axis=0))
         for pair in range(2):
             for q in range(4):
                 out[(pair * 2 + f) * 4 + q] = padded[q * 64:(q + 1) * 64, pair * 128:(pair + 1) * 128]
 
 
-def source(packed, count, weights, target, pixels, beams):
+def source(tiles, pair, time, chan, count, weights, pixels, beams):
     t = tables()
     smem = pl.BlockSpec(memory_space=pltpu.SMEM)
     whole = pl.BlockSpec(memory_space=pltpu.VMEM)
     return pl.pallas_call(
         source_kernel,
         grid=(8,),
-        out_shape=jax.ShapeDtypeStruct((128, 64, 128), F32),
-        in_specs=[smem, smem, smem, smem, smem, whole, whole, pl.BlockSpec(memory_space=pl.ANY)]
+        out_shape=(jax.ShapeDtypeStruct((128, 64, 128), F32), jax.ShapeDtypeStruct((512,), I32)),
+        in_specs=[smem] * 8 + [whole, pl.BlockSpec(memory_space=pl.ANY)]
         + [pl.BlockSpec((1, 2, 256, 256), lambda i: (i, 0, 0, 0))] * 2,
-        out_specs=pl.BlockSpec((16, 64, 128), lambda i: (i, 0, 0)),
+        out_specs=(pl.BlockSpec((16, 64, 128), lambda i: (i, 0, 0)), smem),
         scratch_shapes=[
             pltpu.VMEM((128, 2, 2, 16, 128), BF),
             pltpu.VMEM((128 * 32, 128), F32),
             pltpu.VMEM((8, 256, 256), BF),
             pltpu.VMEM((8, 256, 256), BF),
-            pltpu.VMEM((256, 256), BF),
+            pltpu.VMEM((256, 128), F32),
+            pltpu.SMEM((128,), I32),
             pltpu.SemaphoreType.DMA((8,)),
         ],
         compiler_params=pltpu.CompilerParams(vmem_limit_bytes=VMEM),
         name="source",
     )(
-        packed, count, weights, np.array(STEP_A, np.int32), np.array(STEP_B, np.int32), target,
+        tiles, pair, time, chan, count, weights,
+        np.array(STEP_A, np.int32), np.array(STEP_B, np.int32),
         pixels, beams, t["b"][0], t["b"][1],
     )
 
@@ -459,34 +444,35 @@
 
 
 def final_kernel(x, ex, wh, wl, sh, sl, xh, xl, tj, out, val):
-    pair = pl.program_id(1)
+    group = pl.program_id(1)
 
     def three(a, bh, bl):
         ah, al = split(a)
         return dot(ah, bh) + dot(al, bh) + dot(ah, bl)
 
-    rows = jnp.concatenate([x[0, 0, q] for q in range(4)], axis=0)
-    a = rows.T
-
-    @pl.when(pair > 0)
-    def _():
-        u = three(a, wh[...], wl[...])
-        vr = u[:64, :256] - u[64:, 256:]
-        vi = u[:64, 256:] + u[64:, :256]
-        tr, ti = tj[0, 0:1, :], tj[0, 1:2, :]
-        val[2 * pair] = vr * tr - vi * ti
-        val[2 * pair + 1] = vr * ti + vi * tr
-
-    @pl.when(pair == 0)
+    a = jnp.concatenate(
+        [jnp.concatenate([x[k, 0, q] for q in range(4)], axis=0).T for k in range(4)], axis=0
+    )
+    u = three(a, wh[...], wl[...])
+    for k in range(4):
+        v = u[k * 128:k * 128 + 128]
+        vr = v[:64, :256] - v[64:, 256:]
+        vi = v[:64, 256:] + v[64:, :256]
+        tr, ti = tj[k, 0:1, :], tj[k, 1:2, :]
+        at = 8 * group + 2 * k
+        val[at] = vr * tr - vi * ti
+        val[at + 1] = vr * ti + vi * tr
+
+    @pl.when(group == 0)
     def _():
         extra = jnp.concatenate([ex[0, q] for q in range(4)], axis=0)
         extra = jnp.concatenate([extra, jnp.zeros((96, 128), F32)], axis=0).T[:, :32]
-        v = three(a[:64], sh[0], sl[0]) + three(a[64:], sh[1], sl[1])
+        v = three(a[:64], sh[0], sl[0]) + three(a[64:128], sh[1], sl[1])
         v = v + three(extra[:64], xh[0], xl[0]) + three(extra[64:], xh[1], xl[1])
         val[0] = v[:, :256]
         val[1] = v[:, 256:]
 
-    @pl.when(pair == 15)
+    @pl.when(group == 3)
     def _():
         index = {}
         for i, j in enumerate(PAIR_J):
@@ -557,14 +543,14 @@
     whole = pl.BlockSpec(memory_space=pltpu.VMEM)
     return pl.pallas_call(
         final_kernel,
-        grid=(2, 16),
+        grid=(2, 4),
         out_shape=jax.ShapeDtypeStruct((2, 64, 8192), F32),
         in_specs=[
-            pl.BlockSpec((1, 1, 4, 64, 128), lambda f, j: (j, f, 0, 0, 0)),
+            pl.BlockSpec((4, 1, 4, 64, 128), lambda f, j: (j, f, 0, 0, 0)),
             pl.BlockSpec((1, 4, 8, 128), lambda f, j: (f, 0, 0, 0)),
         ]
         + [whole] * 6
-        + [pl.BlockSpec((1, 2, 256), lambda f, j: (j, 0, 0))],
+        + [pl.BlockSpec((4, 2, 256), lambda f, j: (j, 0, 0))],
         out_specs=pl.BlockSpec((1, 64, 8192), lambda f, j: (f, 0, 0)),
         scratch_shapes=[pltpu.VMEM((32, 64, 256), F32)],
         compiler_params=pltpu.CompilerParams(vmem_limit_bytes=VMEM),
@@ -582,24 +568,12 @@
     return x.reshape(1024, 2, 16, 128)
 
 
-def pack(tile_offsets, station_pairs, time_blocks, channel_blocks):
-    return jnp.concatenate(
-        [
-            tile_offsets[:, 0], tile_offsets[:, 1],
-            station_pairs[:, 0] * 2 + time_blocks, station_pairs[:, 1] * 2 + time_blocks,
-            channel_blocks,
-        ]
-    )
-
-
 def local(
     subgrid_pixels, tile_offsets, station_pairs, time_blocks, channel_blocks, valid_counts,
     aterms, channel_weights,
 ):
-    packed = pack(tile_offsets, station_pairs, time_blocks, channel_blocks)
-    table, target = slots(packed, valid_counts)
-    send = source(
-        packed, valid_counts, channel_weights, target.reshape(1, 128),
+    send, table = source(
+        tile_offsets.T, station_pairs.T, time_blocks, channel_blocks, valid_counts, channel_weights,
         pixel_view(subgrid_pixels), beam_view(aterms),
     )
     half, extra = exchange(send, table.reshape(4, 1, 128))

time: 179 us -> 156 us (0.87)
  the two profiles are of different devices: /device:TPU:2 before, /device:TPU:3 now
where the time goes in v3:
time: 156 us; the launch traced here: 155 us
  Pallas kernels  155 us (99%)
    pallas_call x1, Pallas kernels, exchange(): pl.pallas_call(exchange_kernel, out_shape=(jax.ShapeDtypeStruct((128, 64,...  127 us
    pallas_call x1, Pallas kernels, source(): pl.pallas_call(source_kernel, grid=(8,), out_shape=(jax.ShapeDtypeStruct(...  15.7 us
    pallas_call x1, Pallas kernels, final(): pl.pallas_call(final_kernel, grid=(2, 4), out_shape=jax.ShapeDtypeStruct(...  12.2 us

profile of v3, /device:TPU:3, one launch (start us, length us, event | category | flops | bytes accessed | tf_op | source)
XLA Modules:
  0.0 155.5 jit_solution(14332734368739897667)
XLA Ops:
  0.7 15.7 %source.1 = (f32[128,64,128]{2,1,0:T(8,128)}, s32[512]{0:T(512)}) custom-call(s32[2,128]{1,0:T(2,128)} %bitcast.20, s32[2,128]{1,0:T(2,128)} %bitcast.21, s32[128]{0:T(128)} %time.1, s32[128]{0:T(128)} %chan.1, s32[1]{0:T(128)S(6)} %copy.27.vc, f32[8]{0:T(128)} %cw.1, s32[8]{0:T(128)} %constant.32.clone.ja, s32[8]{0:T(128)} %constant.33.clone.jb, ...), custom_call_target="tpu_custom_call" | custom-call | tf_op jit(solution)/shard_map/source/pallas_call | solution.py:233
  16.4 126.9 %exchange.1 = (f32[128,64,128]{2,1,0:T(8,128)}, f32[8,8,128]{2,1,0:T(8,128)}) custom-call(f32[128,64,128]{2,1,0:T(8,128)} %get-tuple-element.9.send, s32[4,1,128]{2,1,0:T(1,128)} %bitcast.19, bf16[512,256]{1,0:T(8,128)(2,1)} %constant.36.clone.wh, bf16[512,256]{1,0:T(8,128)(2,1)} %constant.37.clone.wl, f32[256,128]{1,0:T(8,128)} %constant.38.clone.twr, ...), custom_call_target="tpu_custom_call" | custom-call | tf_op jit(solution)/shard_map/exchange/pallas_call | solution.py:418
  143.3 12.2 %final.1 = f32[2,64,8192]{2,1,0:T(8,128)} custom-call(f32[16,2,4,64,128]{4,3,2,1,0:T(8,128)} %bitcast.16, f32[2,4,8,128]{3,2,1,0:T(8,128)} %bitcast.18, bf16[256,512]{1,0:T(8,128)(2,1)} %constant.41.clone.wh, bf16[256,512]{1,0:T(8,128)(2,1)} %constant.42.clone.wl, bf16[2,256,512]{2,1,0:T(8,128)(2,1)} %constant.43.clone.sh, ...), custom_call_target="tpu_custom_call" | custom-call | tf_op jit(solution)/shard_map/final/pallas_call | solution.py:544

commit v4 on v3

--- a/solution.py
+++ b/solution.py
@@ -15,8 +15,6 @@
 I32 = jnp.int32
 
 PAIR_J = (0, 8, 4, 12, 1, 9, 17, 25, 2, 10, 18, 26, 3, 11, 19, 27)
-STEP_A = (0, 4, 1, 1, 2, 2, 3, 3)
-STEP_B = (0, 4, 7, 7, 6, 6, 5, 5)
 VMEM = 56 * 1024 * 1024
 
 
@@ -113,33 +111,6 @@
     )
 
 
-def place(tiles, vc, table, count, perm):
-    def clear(i, _):
-        count[i] = 0
-        for k in range(4):
-            table[4 * i + k] = -1
-        return 0
-
-    lax.fori_loop(0, 128, clear, 0, unroll=8)
-    perm[...] = jnp.zeros((256, 128), F32)
-    lane = lax.broadcasted_iota(I32, (1, 128), 1)
-
-    def one(s, _):
-        row, col = tiles[0, s], tiles[1, s]
-        block_row = row >> 4
-        low = block_row < 8
-        near = jnp.where(low, block_row, 15 - block_row)
-        block = ((near << 1) + jnp.where(low, 0, 1)) * 8 + (col >> 5)
-        rank = count[block]
-        slot = block * 2 + jnp.minimum(rank, 1)
-        count[block] = rank + 1
-        table[((slot >> 6) << 7) + (slot & 63)] = ((row & 15) << 5) + (col & 31)
-        perm[pl.ds(slot, 1), :] = jnp.where(lane == s, 1.0, 0.0)
-        return 0
-
-    lax.fori_loop(0, vc[0], one, 0)
-
-
 def dft8(re, im):
     h = math.sqrt(0.5)
 
@@ -163,96 +134,28 @@
     )
 
 
-def source_kernel(
-    tiles, pair, time, chan, vc, cw, ja, jb, px, beams, bh, bl, out, table,
-    got, corr, lhi, llo, perm, count, sems
-):
-    step = pl.program_id(0)
-
-    @pl.when(step == 0)
-    def _():
-        for group in range(8):
-            def fetch(i, _, group=group):
-                s = group * 16 + i
-                for e in range(2):
-                    pltpu.make_async_copy(
-                        beams.at[pair[e, s] * 2 + time[s]], got.at[s, e], sems.at[group]
-                    ).start()
-                return 0
-
-            lax.fori_loop(0, 16, fetch, 0, unroll=4)
-        place(tiles, vc, table, count, perm)
-        for group in range(8):
-            part = got.at[pl.ds(group * 16, 16)]
-            pltpu.make_async_copy(part, part, sems.at[group]).wait()
-
-            def correct(i, _, group=group):
-                s = group * 16 + i
-                weight = jnp.where(s < vc[0], cw[chan[s]], 0.0)
-                ar, ai = got[s, 0, 0].astype(F32), got[s, 0, 1].astype(F32)
-                br, bi = got[s, 1, 0].astype(F32), got[s, 1, 1].astype(F32)
-                gr = (ar * br + ai * bi) * weight
-                gi = (ai * br - ar * bi) * weight
-                pr, pi = px[s, 0], px[s, 1]
-                at = pl.multiple_of(s * 32, 32)
-                corr[pl.ds(at, 16), :] = pr * gr - pi * gi
-                corr[pl.ds(at + 16, 16), :] = pr * gi + pi * gr
-                return 0
-
-            lax.fori_loop(0, 16, correct, 0, unroll=2)
-
-            for f in range(2):
-                base = group * 16 * 32 + f
-                re = [corr[pl.ds(base + 2 * p, 16, stride=32), :] for p in range(8)]
-                im = [corr[pl.ds(base + 16 + 2 * p, 16, stride=32), :] for p in range(8)]
-                re, im = dft8(re, im)
-                rows = slice(f * 128 + group * 16, f * 128 + group * 16 + 16)
-                for k in range(8):
-                    lhi[k, rows, :128], llo[k, rows, :128] = split(re[k])
-                    lhi[k, rows, 128:], llo[k, rows, 128:] = split(im[k])
-
-    acc = jnp.zeros((256, 256), F32)
-    for half, pick in enumerate((ja, jb)):
-        k = pick[step]
-        acc = acc + dot(lhi[k], bh[0, half]) + dot(llo[k], bh[0, half]) + dot(lhi[k], bl[0, half])
-    hi, lo = split(acc)
-    both = perm[...].astype(BF)
-    both = jnp.concatenate([both, both], axis=1)
-    for f in range(2):
-        rows = slice(f * 128, f * 128 + 128)
-        padded = dot(both, jnp.concatenate([hi[rows], lo[rows]], axis=0))
-        for pair in range(2):
-            for q in range(4):
-                out[(pair * 2 + f) * 4 + q] = padded[q * 64:(q + 1) * 64, pair * 128:(pair + 1) * 128]
-
-
-def source(tiles, pair, time, chan, count, weights, pixels, beams):
-    t = tables()
-    smem = pl.BlockSpec(memory_space=pltpu.SMEM)
-    whole = pl.BlockSpec(memory_space=pltpu.VMEM)
-    return pl.pallas_call(
-        source_kernel,
-        grid=(8,),
-        out_shape=(jax.ShapeDtypeStruct((128, 64, 128), F32), jax.ShapeDtypeStruct((512,), I32)),
-        in_specs=[smem] * 8 + [whole, pl.BlockSpec(memory_space=pl.ANY)]
-        + [pl.BlockSpec((1, 2, 256, 256), lambda i: (i, 0, 0, 0))] * 2,
-        out_specs=(pl.BlockSpec((16, 64, 128), lambda i: (i, 0, 0)), smem),
-        scratch_shapes=[
-            pltpu.VMEM((128, 2, 2, 16, 128), BF),
-            pltpu.VMEM((128 * 32, 128), F32),
-            pltpu.VMEM((8, 256, 256), BF),
-            pltpu.VMEM((8, 256, 256), BF),
-            pltpu.VMEM((256, 128), F32),
-            pltpu.SMEM((128,), I32),
-            pltpu.SemaphoreType.DMA((8,)),
-        ],
-        compiler_params=pltpu.CompilerParams(vmem_limit_bytes=VMEM),
-        name="source",
-    )(
-        tiles, pair, time, chan, count, weights,
-        np.array(STEP_A, np.int32), np.array(STEP_B, np.int32),
-        pixels, beams, t["b"][0], t["b"][1],
-    )
+def place(tiles, count, tabs):
+    row, col = tiles[0:1, :], tiles[1:2, :]
+    block_row = lax.shift_right_logical(row, 4)
+    low = block_row < 8
+    near = jnp.where(low, block_row, 15 - block_row)
+    block = (near * 2 + jnp.where(low, 0, 1)) * 8 + lax.shift_right_logical(col, 5)
+    tile = (row & 15) * 32 + (col & 31)
+    down = lax.broadcasted_iota(I32, (128, 128), 0)
+    along = lax.broadcasted_iota(I32, (128, 128), 1)
+
+    def column(x):
+        return jnp.broadcast_to(x, (128, 128)).T
+
+    earlier = (column(block) == block) & (down < along)
+    rank = jnp.sum(jnp.where(earlier, 1.0, 0.0), axis=0, keepdims=True)
+    slot = block * 2 + jnp.where(rank > 0.5, 1, 0)
+    slot = jnp.where(along[0:1] < count, slot, -1)
+    slots, tile = column(slot), column(tile).astype(F32)
+    for q in range(4):
+        tabs[q] = jnp.sum(jnp.where(slots == along + 64 * q, tile, 0.0), axis=0, keepdims=True).astype(I32)
+    hit = jnp.where(lax.broadcasted_iota(I32, (256, 128), 0) == slot, 1.0, 0.0).astype(BF)
+    return jnp.concatenate([hit, hit], axis=1)
 
 
 def spread(i):
@@ -266,13 +169,25 @@
 
 
 def exchange_kernel(
-    send, tabs, wh, wl, twr, twi, fmat, out, outx,
-    recv, tabr, tabt, ghl, pqh, pql, zc, stage, extra, ssem, rsem, lsem
+    tiles, pair, time, chan, vc, cw, pixels_hbm, beams_hbm, bh_hbm, bl_hbm,
+    wh_hbm, wl_hbm, twr_hbm, twi_hbm, fmat_hbm, out, outx,
+    px, beams, bh, bl, wh, wl, twr, twi, fmat,
+    corr, lhi, llo, perm, send, tabs,
+    recv, tabr, tabt, ghl, pqh, pql, zc, stage, extra, ssem, rsem, lsem, csem
 ):
     me = lax.axis_index("row") * 8 + lax.axis_index("col")
     first = me < 8
     kind = jnp.where(first, 1, 0)
     barrier = pltpu.get_barrier_semaphore()
+    loads = [
+        pltpu.make_async_copy(src, dst, csem.at[i])
+        for i, (src, dst) in enumerate((
+            (beams_hbm, beams), (pixels_hbm, px), (bh_hbm, bh), (bl_hbm, bl), (wh_hbm, wh),
+            (wl_hbm, wl), (twr_hbm, twr), (twi_hbm, twi), (fmat_hbm, fmat),
+        ))
+    ]
+    for load in loads:
+        load.start()
 
     def each(fun):
         def step(i, _):
@@ -298,6 +213,60 @@
 
     each(lambda d, dev: pl.semaphore_signal(
         barrier, inc=1, device_id=dev, device_id_type=pl.DeviceIdType.MESH))
+    perm[...] = place(tiles, vc[0], tabs)
+    loads[0].wait()
+    loads[1].wait()
+
+    def correct(s, _):
+        weight = jnp.where(s < vc[0], cw[chan[s]], 0.0)
+        one = beams[pair[0, s] * 2 + time[s]].astype(F32)
+        two = beams[pair[1, s] * 2 + time[s]].astype(F32)
+        gr = (one[0] * two[0] + one[1] * two[1]) * weight
+        gi = (one[1] * two[0] - one[0] * two[1]) * weight
+        pr, pi = px[s, 0], px[s, 1]
+        at = pl.multiple_of(s * 32, 32)
+        corr[pl.ds(at, 16), :] = pr * gr - pi * gi
+        corr[pl.ds(at + 16, 16), :] = pr * gi + pi * gr
+        return 0
+
+    lax.fori_loop(0, 128, correct, 0, unroll=4)
+
+    def coarse(group, _):
+        for f in range(2):
+            base = group * 16 * 32 + f
+            re = [corr[pl.ds(base + 2 * p, 16, stride=32), :] for p in range(8)]
+            im = [corr[pl.ds(base + 16 + 2 * p, 16, stride=32), :] for p in range(8)]
+            re, im = dft8(re, im)
+            rows = pl.ds(pl.multiple_of(f * 128 + group * 16, 16), 16)
+            for k in range(8):
+                lhi[k, rows, :128], llo[k, rows, :128] = split(re[k])
+                lhi[k, rows, 128:], llo[k, rows, 128:] = split(im[k])
+        return 0
+
+    lax.fori_loop(0, 8, coarse, 0)
+    loads[2].wait()
+    loads[3].wait()
+
+    def fine(k, _):
+        a = jnp.where(k == 0, 0, jnp.where(k == 1, 4, lax.div(k, 2)))
+        b = jnp.where(k < 2, a, 8 - a)
+        acc = None
+        for half, at in enumerate((a, b)):
+            h = bh[k, half]
+            term = dot(lhi[at], h) + dot(llo[at], h) + dot(lhi[at], bl[k, half])
+            acc = term if acc is None else acc + term
+        hi, lo = split(acc)
+        for f in range(2):
+            rows = slice(f * 128, f * 128 + 128)
+            padded = dot(perm[...], jnp.concatenate([hi[rows], lo[rows]], axis=0))
+            for p in range(2):
+                for q in range(4):
+                    send[(k * 4 + p * 2 + f) * 4 + q] = (
+                        padded[q * 64:(q + 1) * 64, p * 128:(p + 1) * 128]
+                    )
+        return 0
+
+    lax.fori_loop(0, 8, fine, 0)
     pl.semaphore_wait(barrier, 127)
     each(lambda d, dev: push(tabs.at[lax.rem(d, 4)], tabr.at[me], 0, dev))
     for rp in range(2):
@@ -308,6 +277,8 @@
     flat = recv.reshape(128 * 64, 128)
 
     extra[...] = jnp.zeros((1024, 128), F32)
+    for load in loads[4:]:
+        load.wait()
     wait(tabr.at[pl.ds(0, 127)], rsem.at[0])
     tabt[...] = tabr[...].reshape(128, 128).T
     lane = lax.broadcasted_iota(I32, (32, 128), 1)
@@ -341,7 +312,7 @@
                 dst[pl.ds(2 * tile * size + row + pm, 32, stride=4 * size), :] = even
                 dst[pl.ds((2 * tile + 1) * size + row + pm, 32, stride=4 * size), :] = odd
 
-    def phase(rp, _):
+    def gather(rp):
         rows = pl.ds(pl.multiple_of(rp * 32, 32), 32)
         wait(recv.at[pl.ds(0, 127), rows], rsem.at[1 + rp])
         for pm in range(2):
@@ -364,7 +335,16 @@
             lax.fori_loop(0, 8, block, 0)
         zc[...] = jnp.zeros((128, 256), F32)
 
-        def row(t, _):
+    def phase(p, _):
+        rp, half = lax.div(p, 2), lax.rem(p, 2)
+
+        @pl.when(half == 0)
+        def _():
+            gather(rp)
+
+        def row(i, _):
+            t = half * 8 + i
+
             @pl.when(first & (t > 0))
             def _():
                 zc[...] = mix(2, 1)
@@ -374,55 +354,73 @@
             emit(stage, 64, mix(0, 0) + mix(1, 1) + zc[...], rp * 32 + 2 * t, (0, 1))
             return 0
 
-        lax.fori_loop(0, 16, row, 0)
-
-        @pl.when(first)
+        lax.fori_loop(0, 8, row, 0)
+
+        @pl.when(first & (half == 1))
         def _():
             emit(extra, 8, mix(2, 1), rp, (0,))
 
+        rows = pl.ds(pl.multiple_of(p * 16, 16), 16)
+
         def piece(d):
-            return stage.at[pl.ds(pl.multiple_of(d * 64 + rp * 32, 32), 32), :]
-
-        each(lambda d, dev: push(piece(d), out.at[me, rows], 3 + rp, dev))
+            return stage.at[pl.ds(pl.multiple_of(d * 64 + p * 16, 16), 16), :]
+
+        each(lambda d, dev: push(piece(d), out.at[me, rows], 4 + p, dev))
         keep(piece(me), out.at[me, rows])
         return 0
 
-    lax.fori_loop(0, 2, phase, 0)
+    lax.fori_loop(0, 4, phase, 0)
 
     def piece(d):
         return extra.at[pl.ds(pl.multiple_of(d * 8, 8), 8), :]
 
     @pl.when(first)
     def _():
-        each(lambda d, dev: push(piece(d), outx.at[me], 5, dev))
+        each(lambda d, dev: push(piece(d), outx.at[me], 3, dev))
         keep(piece(me), outx.at[me])
-        wait(outx.at[pl.ds(0, 7)], rsem.at[5])
-        wait(extra.at[pl.ds(0, 127 * 8), :], ssem.at[5])
+        wait(outx.at[pl.ds(0, 7)], rsem.at[3])
+        wait(extra.at[pl.ds(0, 127 * 8), :], ssem.at[3])
 
     @pl.when(me >= 8)
     def _():
-        wait(outx, rsem.at[5])
+        wait(outx, rsem.at[3])
 
     wait(tabr.at[pl.ds(0, 127)], ssem.at[0])
     for rp in range(2):
-        part = recv.at[pl.ds(0, 127), pl.ds(rp * 32, 32)]
-        wait(part, ssem.at[1 + rp])
-        wait(part, ssem.at[3 + rp])
-        wait(out.at[pl.ds(0, 127), pl.ds(rp * 32, 32)], rsem.at[3 + rp])
-
-
-def exchange(send, tabs):
+        wait(send.at[pl.ds(0, 127), pl.ds(rp * 32, 32)], ssem.at[1 + rp])
+    for p in range(4):
+        wait(recv.at[pl.ds(0, 127), pl.ds(p * 16, 16)], ssem.at[4 + p])
+        wait(out.at[pl.ds(0, 127), pl.ds(p * 16, 16)], rsem.at[4 + p])
+
+
+def exchange(tiles, pair, time, chan, count, weights, pixels, beams):
     t = tables()
-    whole = pl.BlockSpec(memory_space=pltpu.VMEM)
+    smem = pl.BlockSpec(memory_space=pltpu.SMEM)
     away = pl.BlockSpec(memory_space=pl.ANY)
+    constants = (*t["b"], *t["wc"], *t["tw"], t["f"])
     return pl.pallas_call(
         exchange_kernel,
         out_shape=(
             jax.ShapeDtypeStruct((128, 64, 128), F32), jax.ShapeDtypeStruct((8, 8, 128), F32)
         ),
-        in_specs=[away, whole] + [whole] * 5,
+        in_specs=[pl.BlockSpec(memory_space=pltpu.VMEM)] + [smem] * 5 + [away] * 9,
         out_specs=(away, away),
         scratch_shapes=[
+            pltpu.VMEM((128, 2, 16, 128), F32),
+            pltpu.VMEM((1024, 2, 16, 128), BF),
+            pltpu.VMEM((8, 2, 256, 256), BF),
+            pltpu.VMEM((8, 2, 256, 256), BF),
+            pltpu.VMEM((512, 256), BF),
+            pltpu.VMEM((512, 256), BF),
+            pltpu.VMEM((256, 128), F32),
+            pltpu.VMEM((256, 128), F32),
+            pltpu.VMEM((2, 3, 256, 256), BF),
+            pltpu.VMEM((128 * 32, 128), F32),
+            pltpu.VMEM((8, 256, 256), BF),
+            pltpu.VMEM((8, 256, 256), BF),
+            pltpu.VMEM((256, 256), BF),
+            pltpu.VMEM((128, 64, 128), F32),
+            pltpu.VMEM((4, 1, 128), I32),
             pltpu.VMEM((128, 64, 128), F32),
             pltpu.VMEM((128, 1, 128), I32),
             pltpu.VMEM((128, 128), I32),
@@ -432,15 +430,16 @@
             pltpu.VMEM((128, 256), F32),
             pltpu.VMEM((128 * 64, 128), F32),
             pltpu.VMEM((128 * 8, 128), F32),
-            pltpu.SemaphoreType.DMA((6,)),
-            pltpu.SemaphoreType.DMA((6,)),
+            pltpu.SemaphoreType.DMA((8,)),
+            pltpu.SemaphoreType.DMA((8,)),
             pltpu.SemaphoreType.DMA,
+            pltpu.SemaphoreType.DMA((9,)),
         ],
         compiler_params=pltpu.CompilerParams(
             vmem_limit_bytes=VMEM, collective_id=0, has_side_effects=True
         ),
         name="exchange",
-    )(send, tabs, t["wc"][0], t["wc"][1], t["tw"][0], t["tw"][1], t["f"])
+    )(tiles, pair, time, chan, count, weights, pixels, beams, *constants)
 
 
 def final_kernel(x, ex, wh, wl, sh, sl, xh, xl, tj, out, val):
@@ -572,11 +571,10 @@
     subgrid_pixels, tile_offsets, station_pairs, time_blocks, channel_blocks, valid_counts,
     aterms, channel_weights,
 ):
-    send, table = source(
+    half, extra = exchange(
         tile_offsets.T, station_pairs.T, time_blocks, channel_blocks, valid_counts, channel_weights,
         pixel_view(subgrid_pixels), beam_view(aterms),
     )
-    half, extra = exchange(send, table.reshape(4, 1, 128))
     return final(half.reshape(16, 2, 4, 64, 128), extra.reshape(2, 4, 8, 128))
 
 

time: 156 us -> 141 us (0.904)
  the two profiles are of different devices: /device:TPU:3 before, /device:TPU:1 now
where the time goes in v4:
time: 141 us; the launch traced here: 140 us
  Pallas kernels  140 us (99%)
    pallas_call x1, Pallas kernels, exchange(): pl.pallas_call(exchange_kernel, out_shape=(jax.ShapeDtypeStruct((128, 64,...  128 us
    pallas_call x1, Pallas kernels, final(): pl.pallas_call(final_kernel, grid=(2, 4), out_shape=jax.ShapeDtypeStruct(...  12.2 us

profile of v4, /device:TPU:1, one launch (start us, length us, event | category | flops | bytes accessed | tf_op | source)
XLA Modules:
  0.0 140.5 jit_solution(2053213754238405893)
XLA Ops:
  0.7 127.6 %exchange.1 = (f32[128,64,128]{2,1,0:T(8,128)}, f32[8,8,128]{2,1,0:T(8,128)}) custom-call(s32[2,128]{1,0:T(2,128)} %bitcast.18, s32[2,128]{1,0:T(2,128)} %bitcast.19, s32[128]{0:T(128)} %time.1, s32[128]{0:T(128)} %chan.1, s32[1]{0:T(128)S(6)} %copy.25.vc, f32[8]{0:T(128)} %cw.1, f32[128,2,16,128]{3,2,1,0:T(8,128)} %bitcast.16, ...), custom_call_target="tpu_custom_call" | custom-call | tf_op jit(solution)/shard_map/exchange/pallas_call | solution.py:401
  128.2 12.2 %final.1 = f32[2,64,8192]{2,1,0:T(8,128)} custom-call(f32[16,2,4,64,128]{4,3,2,1,0:T(8,128)} %bitcast.15, f32[2,4,8,128]{3,2,1,0:T(8,128)} %bitcast.17, bf16[256,512]{1,0:T(8,128)(2,1)} %constant.35.clone.wh, bf16[256,512]{1,0:T(8,128)(2,1)} %constant.36.clone.wl, bf16[2,256,512]{2,1,0:T(8,128)(2,1)} %constant.37.clone.sh, ...), custom_call_target="tpu_custom_call" | custom-call | tf_op jit(solution)/shard_map/final/pallas_call | solution.py:543

commit v5 on v4

--- a/solution.py
+++ b/solution.py
@@ -105,9 +105,12 @@
     wx = np.stack([np.concatenate([wx.real, zero], 1), np.concatenate([-wx.imag, zero], 1)])
     tj = unit(np.array(PAIR_J)[:, None] * l0[None, :] / 8192)
     tj = np.stack([tj.real, tj.imag], 1).astype(np.float32)
+    wr, ws = wr.reshape(4, 2, 32, 512), ws.reshape(2, 4, 2, 32, 512)
+    wr = [split_np(wr[:, i].reshape(128, 512)) for i in range(2)]
+    ws = [split_np(ws[:, :, i].reshape(2, 128, 512)) for i in range(2)]
     return dict(
         b=split_np(b), wc=split_np(wc), tw=(tw.real.astype(np.float32), tw.imag.astype(np.float32)),
-        f=f, wr=split_np(wr), ws=split_np(ws), wx=split_np(wx), tj=tj,
+        f=f, wr=wr, ws=ws, wx=split_np(wx), tj=tj,
     )
 
 
@@ -158,22 +161,41 @@
     return jnp.concatenate([hit, hit], axis=1)
 
 
-def spread(i):
-    o = lax.rem(i * 37, 128)
-    row, col = lax.axis_index("row"), lax.axis_index("col")
-    x = lax.rem(lax.div(row, 4) + lax.div(o, 32), 4)
-    y = lax.rem(lax.rem(row, 4) + lax.rem(lax.div(o, 8), 4), 4)
-    z = lax.rem(lax.div(col, 2) + lax.rem(lax.div(o, 2), 4), 4)
-    c = lax.rem(col + o, 2)
-    return x * 4 + y, z * 2 + c
+def three(a, b):
+    ah, al = split(a)
+    return dot(ah, b[0]) + dot(al, b[0]) + dot(ah, b[1])
+
+
+def halves(re, im):
+    return [re[:, :128], re[:, 128:], im[:, :128], im[:, 128:]]
+
+
+def row_dft(blocks, w, tj, group):
+    a = jnp.concatenate([jnp.concatenate(b, axis=0).T for b in blocks], axis=0)
+    u = three(a, (w[0][...], w[1][...]))
+    outs = []
+    for k in range(4):
+        v = u[k * 128:k * 128 + 128]
+        vr = v[:64, :256] - v[64:, 256:]
+        vi = v[:64, 256:] + v[64:, :256]
+        tr, ti = tj[4 * group + k, 0:1, :], tj[4 * group + k, 1:2, :]
+        outs += halves(vr * tr - vi * ti, vr * ti + vi * tr)
+    return outs
+
+
+def row_dft_zero(block, w):
+    a = jnp.concatenate(block, axis=0).T
+    v = three(a[:64], (w[0][0], w[1][0])) + three(a[64:], (w[0][1], w[1][1]))
+    return halves(v[:, :256], v[:, 256:])
 
 
 def exchange_kernel(
     tiles, pair, time, chan, vc, cw, pixels_hbm, beams_hbm, bh_hbm, bl_hbm,
-    wh_hbm, wl_hbm, twr_hbm, twi_hbm, fmat_hbm, out, outx,
-    px, beams, bh, bl, wh, wl, twr, twi, fmat,
+    wh_hbm, wl_hbm, twr_hbm, twi_hbm, fmat_hbm,
+    wrh_hbm, wrl_hbm, wsh_hbm, wsl_hbm, tj_hbm, out, outx, part,
+    px, beams, bh, bl, wh, wl, twr, twi, fmat, wrh, wrl, wsh, wsl, tj,
     corr, lhi, llo, perm, send, tabs,
-    recv, tabr, tabt, ghl, pqh, pql, zc, stage, extra, ssem, rsem, lsem, csem
+    recv, tabr, tabt, ghl, pqh, pql, zc, stage, extra, half0, ssem, rsem, lsem, csem
 ):
     me = lax.axis_index("row") * 8 + lax.axis_index("col")
     first = me < 8
@@ -184,18 +206,34 @@
         for i, (src, dst) in enumerate((
             (beams_hbm, beams), (pixels_hbm, px), (bh_hbm, bh), (bl_hbm, bl), (wh_hbm, wh),
             (wl_hbm, wl), (twr_hbm, twr), (twi_hbm, twi), (fmat_hbm, fmat),
+            (wrh_hbm, wrh), (wrl_hbm, wrl), (wsh_hbm, wsh), (wsl_hbm, wsl), (tj_hbm, tj),
         ))
     ]
     for load in loads:
         load.start()
+    wr, ws = (wrh, wrl), (wsh, wsl)
+
+    x, y = lax.div(lax.axis_index("row"), 4), lax.rem(lax.axis_index("row"), 4)
+    z, core = lax.div(lax.axis_index("col"), 2), lax.rem(lax.axis_index("col"), 2)
+    cols = [lax.rem(z + b // 2, 4) * 2 + lax.rem(core + b, 2) for b in range(8)]
 
     def each(fun):
-        def step(i, _):
-            row, col = spread(i)
-            fun(row * 8 + col, (row, col))
+        def step(a, _):
+            def one(b):
+                o = lax.rem(a + 5 * b, 16)
+                row = lax.rem(x + lax.div(o, 4), 4) * 4 + lax.rem(y + o, 4)
+                fun(row * 8 + cols[b], (row, cols[b]))
+
+            for b in (3, 6, 1, 4, 7, 2, 5):
+                one(b)
+
+            @pl.when(a > 0)
+            def _():
+                one(0)
+
             return 0
 
-        lax.fori_loop(1, 128, step, 0)
+        lax.fori_loop(0, 16, step, 0)
 
     def push(src, dst, k, dev):
         pltpu.make_async_remote_copy(
@@ -247,7 +285,11 @@
     loads[2].wait()
     loads[3].wait()
 
-    def fine(k, _):
+    pl.semaphore_wait(barrier, 127)
+    early, late = pl.ds(0, 32), pl.ds(32, 32)
+
+    def fine(i, _):
+        k = lax.rem(i + lax.div(me, 16), 8)
         a = jnp.where(k == 0, 0, jnp.where(k == 1, 4, lax.div(k, 2)))
         b = jnp.where(k < 2, a, 8 - a)
         acc = None
@@ -264,20 +306,25 @@
                     send[(k * 4 + p * 2 + f) * 4 + q] = (
                         padded[q * 64:(q + 1) * 64, p * 128:(p + 1) * 128]
                     )
+        for n in range(16):
+            row, col = 2 * k + n % 2, n * 3 // 2 % 8
+            d = row * 8 + col
+
+            @pl.when(d != me)
+            def _(d=d, dev=(row, jnp.int32(col))):
+                push(send.at[d, early], recv.at[me, early], 1, dev)
+
         return 0
 
     lax.fori_loop(0, 8, fine, 0)
-    pl.semaphore_wait(barrier, 127)
     each(lambda d, dev: push(tabs.at[lax.rem(d, 4)], tabr.at[me], 0, dev))
-    for rp in range(2):
-        rows = pl.ds(rp * 32, 32)
-        each(lambda d, dev: push(send.at[d, rows], recv.at[me, rows], 1 + rp, dev))
+    each(lambda d, dev: push(send.at[d, late], recv.at[me, late], 2, dev))
     keep(tabs.at[lax.rem(me, 4)], tabr.at[me])
     keep(send.at[me], recv.at[me])
     flat = recv.reshape(128 * 64, 128)
 
     extra[...] = jnp.zeros((1024, 128), F32)
-    for load in loads[4:]:
+    for load in loads[4:9]:
         load.wait()
     wait(tabr.at[pl.ds(0, 127)], rsem.at[0])
     tabt[...] = tabr[...].reshape(128, 128).T
@@ -313,8 +360,6 @@
                 dst[pl.ds((2 * tile + 1) * size + row + pm, 32, stride=4 * size), :] = odd
 
     def gather(rp):
-        rows = pl.ds(pl.multiple_of(rp * 32, 32), 32)
-        wait(recv.at[pl.ds(0, 127), rows], rsem.at[1 + rp])
         for pm in range(2):
             def block(c, _, pm=pm):
                 at = rp * 32 + pm * 16 + 2 * c
@@ -360,15 +405,28 @@
         def _():
             emit(extra, 8, mix(2, 1), rp, (0,))
 
-        rows = pl.ds(pl.multiple_of(p * 16, 16), 16)
-
-        def piece(d):
-            return stage.at[pl.ds(pl.multiple_of(d * 64 + p * 16, 16), 16), :]
-
-        each(lambda d, dev: push(piece(d), out.at[me, rows], 4 + p, dev))
-        keep(piece(me), out.at[me, rows])
+        @pl.when(p == 1)
+        def _():
+            def piece(d):
+                return stage.at[pl.ds(pl.multiple_of(d * 64, 64), 32), :]
+
+            wait(recv.at[pl.ds(0, 127), late], rsem.at[2])
+            each(lambda d, dev: push(piece(d), half0.at[me], 4, dev))
+            keep(piece(me), half0.at[me])
+
+        @pl.when(p > 1)
+        def _():
+            rows = pl.ds(pl.multiple_of(half * 16, 16), 16)
+
+            def piece(d):
+                return stage.at[pl.ds(pl.multiple_of(d * 64 + p * 16, 16), 16), :]
+
+            each(lambda d, dev: push(piece(d), out.at[me, rows], 3 + p, dev))
+            keep(piece(me), out.at[me, rows])
+
         return 0
 
+    wait(recv.at[pl.ds(0, 127), early], rsem.at[1])
     lax.fori_loop(0, 4, phase, 0)
 
     def piece(d):
@@ -385,26 +443,53 @@
     def _():
         wait(outx, rsem.at[3])
 
+    wait(send.at[pl.ds(0, 127), early], ssem.at[1])
+    wait(send.at[pl.ds(0, 127), late], ssem.at[2])
+    for load in loads[9:]:
+        load.wait()
+    wait(half0.at[pl.ds(0, 127)], rsem.at[4])
+
+    def transform(n, _):
+        f, group = lax.div(n, 4), lax.rem(n, 4)
+        turned = row_dft(
+            [[half0[((4 * group + k) * 2 + f) * 4 + q] for q in range(4)] for k in range(4)],
+            wr, tj, group,
+        )
+        for k in range(16):
+            send[n * 16 + k] = turned[k]
+
+        @pl.when(group == 0)
+        def _():
+            for k, v in enumerate(row_dft_zero([half0[f * 4 + q] for q in range(4)], ws)):
+                send[n * 16 + k] = v
+
+        pltpu.make_async_copy(
+            send.at[pl.ds(n * 16, 16)], part.at[pl.ds(n * 16, 16)], lsem
+        ).start()
+        return 0
+
+    lax.fori_loop(0, 8, transform, 0)
+    wait(part, lsem)
     wait(tabr.at[pl.ds(0, 127)], ssem.at[0])
-    for rp in range(2):
-        wait(send.at[pl.ds(0, 127), pl.ds(rp * 32, 32)], ssem.at[1 + rp])
-    for p in range(4):
-        wait(recv.at[pl.ds(0, 127), pl.ds(p * 16, 16)], ssem.at[4 + p])
-        wait(out.at[pl.ds(0, 127), pl.ds(p * 16, 16)], rsem.at[4 + p])
+    wait(half0.at[pl.ds(0, 127)], ssem.at[4])
+    for p in range(2):
+        wait(out.at[pl.ds(0, 127), pl.ds(p * 16, 16)], rsem.at[5 + p])
+        wait(recv.at[pl.ds(0, 127), pl.ds(p * 16, 16)], ssem.at[5 + p])
 
 
 def exchange(tiles, pair, time, chan, count, weights, pixels, beams):
     t = tables()
     smem = pl.BlockSpec(memory_space=pltpu.SMEM)
     away = pl.BlockSpec(memory_space=pl.ANY)
-    constants = (*t["b"], *t["wc"], *t["tw"], t["f"])
+    constants = (*t["b"], *t["wc"], *t["tw"], t["f"], *t["wr"][0], *t["ws"][0], t["tj"])
     return pl.pallas_call(
         exchange_kernel,
         out_shape=(
-            jax.ShapeDtypeStruct((128, 64, 128), F32), jax.ShapeDtypeStruct((8, 8, 128), F32)
+            jax.ShapeDtypeStruct((128, 32, 128), F32), jax.ShapeDtypeStruct((8, 8, 128), F32),
+            jax.ShapeDtypeStruct((128, 64, 128), F32),
         ),
-        in_specs=[pl.BlockSpec(memory_space=pltpu.VMEM)] + [smem] * 5 + [away] * 9,
-        out_specs=(away, away),
+        in_specs=[pl.BlockSpec(memory_space=pltpu.VMEM)] + [smem] * 5 + [away] * 14,
+        out_specs=(away, away, away),
         scratch_shapes=[
             pltpu.VMEM((128, 2, 16, 128), F32),
             pltpu.VMEM((1024, 2, 16, 128), BF),
@@ -415,6 +500,11 @@
             pltpu.VMEM((256, 128), F32),
             pltpu.VMEM((256, 128), F32),
             pltpu.VMEM((2, 3, 256, 256), BF),
+            pltpu.VMEM((128, 512), BF),
+            pltpu.VMEM((128, 512), BF),
+            pltpu.VMEM((2, 128, 512), BF),
+            pltpu.VMEM((2, 128, 512), BF),
+            pltpu.VMEM((16, 2, 256), F32),
             pltpu.VMEM((128 * 32, 128), F32),
             pltpu.VMEM((8, 256, 256), BF),
             pltpu.VMEM((8, 256, 256), BF),
@@ -430,10 +520,11 @@
             pltpu.VMEM((128, 256), F32),
             pltpu.VMEM((128 * 64, 128), F32),
             pltpu.VMEM((128 * 8, 128), F32),
+            pltpu.VMEM((128, 32, 128), F32),
             pltpu.SemaphoreType.DMA((8,)),
             pltpu.SemaphoreType.DMA((8,)),
             pltpu.SemaphoreType.DMA,
-            pltpu.SemaphoreType.DMA((9,)),
+            pltpu.SemaphoreType.DMA((14,)),
         ],
         compiler_params=pltpu.CompilerParams(
             vmem_limit_bytes=VMEM, collective_id=0, has_side_effects=True
@@ -442,34 +533,20 @@
     )(tiles, pair, time, chan, count, weights, pixels, beams, *constants)
 
 
-def final_kernel(x, ex, wh, wl, sh, sl, xh, xl, tj, out, val):
+def final_kernel(x, ex, part, wh, wl, sh, sl, xh, xl, tj, out, val):
     group = pl.program_id(1)
-
-    def three(a, bh, bl):
-        ah, al = split(a)
-        return dot(ah, bh) + dot(al, bh) + dot(ah, bl)
-
-    a = jnp.concatenate(
-        [jnp.concatenate([x[k, 0, q] for q in range(4)], axis=0).T for k in range(4)], axis=0
-    )
-    u = three(a, wh[...], wl[...])
-    for k in range(4):
-        v = u[k * 128:k * 128 + 128]
-        vr = v[:64, :256] - v[64:, 256:]
-        vi = v[:64, 256:] + v[64:, :256]
-        tr, ti = tj[k, 0:1, :], tj[k, 1:2, :]
-        at = 8 * group + 2 * k
-        val[at] = vr * tr - vi * ti
-        val[at + 1] = vr * ti + vi * tr
+    turned = row_dft([[x[k, 0, q] for q in range(4)] for k in range(4)], (wh, wl), tj, group)
+    for k in range(16):
+        val[16 * group + k] = turned[k] + part[k]
 
     @pl.when(group == 0)
     def _():
         extra = jnp.concatenate([ex[0, q] for q in range(4)], axis=0)
         extra = jnp.concatenate([extra, jnp.zeros((96, 128), F32)], axis=0).T[:, :32]
-        v = three(a[:64], sh[0], sl[0]) + three(a[64:128], sh[1], sl[1])
-        v = v + three(extra[:64], xh[0], xl[0]) + three(extra[64:], xh[1], xl[1])
-        val[0] = v[:, :256]
-        val[1] = v[:, 256:]
+        v = three(extra[:64], (xh[0], xl[0])) + three(extra[64:], (xh[1], xl[1]))
+        more = halves(v[:, :256], v[:, 256:])
+        for k, v in enumerate(row_dft_zero([x[0, 0, q] for q in range(4)], (sh, sl))):
+            val[k] = v + part[k] + more[k]
 
     @pl.when(group == 3)
     def _():
@@ -481,10 +558,9 @@
         def strip(i, _):
             at = pl.ds(pl.multiple_of(i * 8, 8), 8)
             for tile in range(2):
-                lanes = slice(tile * 128, tile * 128 + 128)
-                zero, mid = val[0, at, lanes], val[1, at, lanes]
-                re = {j: val[2 * k, at, lanes] for j, (k, _) in index.items()}
-                im = {j: val[2 * k + 1, at, lanes] for j, (k, _) in index.items()}
+                zero, mid = val[tile, at, :], val[2 + tile, at, :]
+                re = {j: val[4 * k + tile, at, :] for j, (k, _) in index.items()}
+                im = {j: val[4 * k + 2 + tile, at, :] for j, (k, _) in index.items()}
 
                 def wave(fun, part, js, l1, signed):
                     total = None
@@ -537,7 +613,7 @@
         lax.fori_loop(0, 8, strip, 0)
 
 
-def final(recv, extra):
+def final(recv, extra, part):
     t = tables()
     whole = pl.BlockSpec(memory_space=pltpu.VMEM)
     return pl.pallas_call(
@@ -545,16 +621,16 @@
         grid=(2, 4),
         out_shape=jax.ShapeDtypeStruct((2, 64, 8192), F32),
         in_specs=[
-            pl.BlockSpec((4, 1, 4, 64, 128), lambda f, j: (j, f, 0, 0, 0)),
+            pl.BlockSpec((4, 1, 4, 32, 128), lambda f, j: (j, f, 0, 0, 0)),
             pl.BlockSpec((1, 4, 8, 128), lambda f, j: (f, 0, 0, 0)),
+            pl.BlockSpec((16, 64, 128), lambda f, j: (f * 4 + j, 0, 0)),
         ]
-        + [whole] * 6
-        + [pl.BlockSpec((4, 2, 256), lambda f, j: (j, 0, 0))],
+        + [whole] * 7,
         out_specs=pl.BlockSpec((1, 64, 8192), lambda f, j: (f, 0, 0)),
-        scratch_shapes=[pltpu.VMEM((32, 64, 256), F32)],
+        scratch_shapes=[pltpu.VMEM((64, 64, 128), F32)],
         compiler_params=pltpu.CompilerParams(vmem_limit_bytes=VMEM),
         name="final",
-    )(recv, extra, *t["wr"], *t["ws"], *t["wx"], t["tj"])
+    )(recv, extra, part, *t["wr"][1], *t["ws"][1], *t["wx"], t["tj"])
 
 
 def pixel_view(pixels):
@@ -571,11 +647,11 @@
     subgrid_pixels, tile_offsets, station_pairs, time_blocks, channel_blocks, valid_counts,
     aterms, channel_weights,
 ):
-    half, extra = exchange(
+    half, extra, part = exchange(
         tile_offsets.T, station_pairs.T, time_blocks, channel_blocks, valid_counts, channel_weights,
         pixel_view(subgrid_pixels), beam_view(aterms),
     )
-    return final(half.reshape(16, 2, 4, 64, 128), extra.reshape(2, 4, 8, 128))
+    return final(half.reshape(16, 2, 4, 32, 128), extra.reshape(2, 4, 8, 128), part)
 
 
 def solution(mesh):

time: 141 us -> 150 us (1.064); the launches traced: 140 us -> 148 us
  Pallas kernels: 140 us -> 147 us
    pallas_call x1, Pallas kernels: 128 us -> 135 us  [exchange(): pl.pallas_call(exchange_kernel, out_shape=(jax.ShapeDtypeStruct((128, 32,...]
where the time goes in v5:
time: 150 us; the launch traced here: 148 us
  Pallas kernels  147 us (98%)
    pallas_call x1, Pallas kernels, exchange(): pl.pallas_call(exchange_kernel, out_shape=(jax.ShapeDtypeStruct((128, 32,...  135 us
    pallas_call x1, Pallas kernels, final(): pl.pallas_call(final_kernel, grid=(2, 4), out_shape=jax.ShapeDtypeStruct(...  12.5 us

profile of v5, /device:TPU:1, one launch (start us, length us, event | category | flops | bytes accessed | tf_op | source)
XLA Modules:
  0.0 147.9 jit_solution(11858172153682213055)
XLA Ops:
  0.7 134.7 %exchange.1 = (f32[128,32,128]{2,1,0:T(8,128)}, f32[8,8,128]{2,1,0:T(8,128)}, f32[128,64,128]{2,1,0:T(8,128)}) custom-call(s32[2,128]{1,0:T(2,128)} %bitcast.18, s32[2,128]{1,0:T(2,128)} %bitcast.19, s32[128]{0:T(128)} %time.1, s32[128]{0:T(128)} %chan.1, s32[1]{0:T(128)S(6)} %copy.29.vc, f32[8]{0:T(128)} %cw.1, f32[128,2,16,128]{3,2,1,0:T(8,128)} %bitcast.15, ...), custom_call_target="tpu_custom_call" | custom-call | tf_op jit(solution)/shard_map/exchange/pallas_call | solution.py:485
  135.4 12.5 %final.1 = f32[2,64,8192]{2,1,0:T(8,128)} custom-call(f32[16,2,4,32,128]{4,3,2,1,0:T(8,128)} %bitcast.16, f32[2,4,8,128]{3,2,1,0:T(8,128)} %bitcast.17, f32[128,64,128]{2,1,0:T(8,128)} %get-tuple-element.10.part, bf16[128,512]{1,0:T(8,128)(2,1)} %constant.48.clone.wh, bf16[128,512]{1,0:T(8,128)(2,1)} %constant.49.clone.wl, ...), custom_call_target="tpu_custom_call" | custom-call | tf_op jit(solution)/shard_map/final/pallas_call | solution.py:619

commit v6 on v5

--- a/solution.py
+++ b/solution.py
@@ -106,8 +106,8 @@
     tj = unit(np.array(PAIR_J)[:, None] * l0[None, :] / 8192)
     tj = np.stack([tj.real, tj.imag], 1).astype(np.float32)
     wr, ws = wr.reshape(4, 2, 32, 512), ws.reshape(2, 4, 2, 32, 512)
-    wr = [split_np(wr[:, i].reshape(128, 512)) for i in range(2)]
-    ws = [split_np(ws[:, :, i].reshape(2, 128, 512)) for i in range(2)]
+    wr = split_np(wr.transpose(1, 0, 2, 3).reshape(2, 128, 512))
+    ws = split_np(ws.transpose(2, 0, 1, 3, 4).reshape(2, 2, 128, 512))
     return dict(
         b=split_np(b), wc=split_np(wc), tw=(tw.real.astype(np.float32), tw.imag.astype(np.float32)),
         f=f, wr=wr, ws=ws, wx=split_np(wx), tj=tj,
@@ -189,13 +189,60 @@
     return halves(v[:, :256], v[:, 256:])
 
 
+def mix_pairs(load):
+    index = {}
+    for i, j in enumerate(PAIR_J):
+        if i > 0:
+            index[j if j < 16 else 32 - j] = (i, 1.0 if j < 16 else -1.0)
+    zero, mid = load(0, 0), load(0, 1)
+    re = {j: load(k, 0) for j, (k, _) in index.items()}
+    im = {j: load(k, 1) for j, (k, _) in index.items()}
+
+    def wave(fun, part, js, l1, signed):
+        total = jnp.zeros((8, 128), F32)
+        started = False
+        for j in js:
+            c = fun(2 * math.pi * (j * l1 % 32) / 32) * (index[j][1] if signed else 1.0)
+            if abs(c) < 1e-12:
+                continue
+            term = part[j] if abs(abs(c) - 1) < 1e-12 else part[j] * abs(c)
+            if started:
+                total = total + term if c > 0 else total - term
+            else:
+                total = term if c > 0 else -term
+            started = True
+        return total
+
+    odd, even, four = range(1, 16, 2), (2, 6, 10, 14), (4, 8, 12)
+    ce, se = [None] * 9, [None] * 9
+    for l1 in range(5):
+        ee = wave(math.cos, re, four, l1, False) + (zero + mid if l1 % 2 == 0 else zero - mid)
+        eo = wave(math.cos, re, even, l1, False)
+        oe = wave(math.sin, im, four, l1, True)
+        oo = wave(math.sin, im, even, l1, True)
+        ce[l1], ce[8 - l1] = ee + eo, ee - eo
+        se[l1], se[8 - l1] = oe + oo, oo - oe
+    outs = []
+    for l1 in range(9):
+        co = wave(math.cos, re, odd, l1, False)
+        so = wave(math.sin, im, odd, l1, True)
+        p, m = ce[l1] + co, ce[l1] - co
+        s, d = se[l1] + so, se[l1] - so
+        outs += [(l1, p + s), (16 + l1, m + d)]
+        if l1 > 0:
+            outs.append((32 - l1, p - s))
+            if l1 < 8:
+                outs.append((16 - l1, m - d))
+    return outs
+
+
 def exchange_kernel(
     tiles, pair, time, chan, vc, cw, pixels_hbm, beams_hbm, bh_hbm, bl_hbm,
     wh_hbm, wl_hbm, twr_hbm, twi_hbm, fmat_hbm,
-    wrh_hbm, wrl_hbm, wsh_hbm, wsl_hbm, tj_hbm, out, outx, part,
-    px, beams, bh, bl, wh, wl, twr, twi, fmat, wrh, wrl, wsh, wsl, tj,
+    wrh_hbm, wrl_hbm, wsh_hbm, wsl_hbm, xh_hbm, xl_hbm, tj_hbm, out,
+    px, beams, bh, bl, wh, wl, twr, twi, fmat, wrh, wrl, wsh, wsl, xh, xl, tj,
     corr, lhi, llo, perm, send, tabs,
-    recv, tabr, tabt, ghl, pqh, pql, zc, stage, extra, half0, ssem, rsem, lsem, csem
+    recv, tabr, tabt, ghl, pqh, pql, zc, stage, extra, got, gotx, image, ssem, rsem, lsem, csem
 ):
     me = lax.axis_index("row") * 8 + lax.axis_index("col")
     first = me < 8
@@ -206,12 +253,12 @@
         for i, (src, dst) in enumerate((
             (beams_hbm, beams), (pixels_hbm, px), (bh_hbm, bh), (bl_hbm, bl), (wh_hbm, wh),
             (wl_hbm, wl), (twr_hbm, twr), (twi_hbm, twi), (fmat_hbm, fmat),
-            (wrh_hbm, wrh), (wrl_hbm, wrl), (wsh_hbm, wsh), (wsl_hbm, wsl), (tj_hbm, tj),
+            (wrh_hbm, wrh), (wrl_hbm, wrl), (wsh_hbm, wsh), (wsl_hbm, wsl),
+            (xh_hbm, xh), (xl_hbm, xl), (tj_hbm, tj),
         ))
     ]
     for load in loads:
         load.start()
-    wr, ws = (wrh, wrl), (wsh, wsl)
 
     x, y = lax.div(lax.axis_index("row"), 4), lax.rem(lax.axis_index("row"), 4)
     z, core = lax.div(lax.axis_index("col"), 2), lax.rem(lax.axis_index("col"), 2)
@@ -285,11 +332,9 @@
     loads[2].wait()
     loads[3].wait()
 
-    pl.semaphore_wait(barrier, 127)
     early, late = pl.ds(0, 32), pl.ds(32, 32)
 
-    def fine(i, _):
-        k = lax.rem(i + lax.div(me, 16), 8)
+    def fine(k, _):
         a = jnp.where(k == 0, 0, jnp.where(k == 1, 4, lax.div(k, 2)))
         b = jnp.where(k < 2, a, 8 - a)
         acc = None
@@ -306,17 +351,11 @@
                     send[(k * 4 + p * 2 + f) * 4 + q] = (
                         padded[q * 64:(q + 1) * 64, p * 128:(p + 1) * 128]
                     )
-        for n in range(16):
-            row, col = 2 * k + n % 2, n * 3 // 2 % 8
-            d = row * 8 + col
-
-            @pl.when(d != me)
-            def _(d=d, dev=(row, jnp.int32(col))):
-                push(send.at[d, early], recv.at[me, early], 1, dev)
-
         return 0
 
     lax.fori_loop(0, 8, fine, 0)
+    pl.semaphore_wait(barrier, 127)
+    each(lambda d, dev: push(send.at[d, early], recv.at[me, early], 1, dev))
     each(lambda d, dev: push(tabs.at[lax.rem(d, 4)], tabr.at[me], 0, dev))
     each(lambda d, dev: push(send.at[d, late], recv.at[me, late], 2, dev))
     keep(tabs.at[lax.rem(me, 4)], tabr.at[me])
@@ -411,18 +450,18 @@
                 return stage.at[pl.ds(pl.multiple_of(d * 64, 64), 32), :]
 
             wait(recv.at[pl.ds(0, 127), late], rsem.at[2])
-            each(lambda d, dev: push(piece(d), half0.at[me], 4, dev))
-            keep(piece(me), half0.at[me])
+            each(lambda d, dev: push(piece(d), got.at[me, early], 4, dev))
+            keep(piece(me), got.at[me, early])
 
         @pl.when(p > 1)
         def _():
-            rows = pl.ds(pl.multiple_of(half * 16, 16), 16)
+            rows = pl.ds(pl.multiple_of(p * 16, 16), 16)
 
             def piece(d):
                 return stage.at[pl.ds(pl.multiple_of(d * 64 + p * 16, 16), 16), :]
 
-            each(lambda d, dev: push(piece(d), out.at[me, rows], 3 + p, dev))
-            keep(piece(me), out.at[me, rows])
+            each(lambda d, dev: push(piece(d), got.at[me, rows], 3 + p, dev))
+            keep(piece(me), got.at[me, rows])
 
         return 0
 
@@ -434,62 +473,97 @@
 
     @pl.when(first)
     def _():
-        each(lambda d, dev: push(piece(d), outx.at[me], 3, dev))
-        keep(piece(me), outx.at[me])
-        wait(outx.at[pl.ds(0, 7)], rsem.at[3])
+        each(lambda d, dev: push(piece(d), gotx.at[me], 3, dev))
+        keep(piece(me), gotx.at[me])
         wait(extra.at[pl.ds(0, 127 * 8), :], ssem.at[3])
-
-    @pl.when(me >= 8)
-    def _():
-        wait(outx, rsem.at[3])
 
     wait(send.at[pl.ds(0, 127), early], ssem.at[1])
     wait(send.at[pl.ds(0, 127), late], ssem.at[2])
     for load in loads[9:]:
         load.wait()
-    wait(half0.at[pl.ds(0, 127)], rsem.at[4])
-
-    def transform(n, _):
+    wait(got.at[pl.ds(0, 127), early], rsem.at[4])
+
+    def transform(n, _, rp):
         f, group = lax.div(n, 4), lax.rem(n, 4)
+        rows = slice(rp * 32, rp * 32 + 32)
         turned = row_dft(
-            [[half0[((4 * group + k) * 2 + f) * 4 + q] for q in range(4)] for k in range(4)],
-            wr, tj, group,
+            [[got[((4 * group + k) * 2 + f) * 4 + q, rows, :] for q in range(4)] for k in range(4)],
+            (wrh.at[rp], wrl.at[rp]), tj, group,
         )
-        for k in range(16):
-            send[n * 16 + k] = turned[k]
+
+        def add(k, v):
+            at = n * 16 + k
+            send[at] = v if rp == 0 else send[at] + v
+
+        for k in range(4, 16):
+            add(k, turned[k])
+
+        @pl.when(group > 0)
+        def _():
+            for k in range(4):
+                add(k, turned[k])
 
         @pl.when(group == 0)
         def _():
-            for k, v in enumerate(row_dft_zero([half0[f * 4 + q] for q in range(4)], ws)):
-                send[n * 16 + k] = v
-
-        pltpu.make_async_copy(
-            send.at[pl.ds(n * 16, 16)], part.at[pl.ds(n * 16, 16)], lsem
-        ).start()
+            zero = row_dft_zero(
+                [got[f * 4 + q, rows, :] for q in range(4)], (wsh.at[rp], wsl.at[rp])
+            )
+            if rp == 1:
+                edge = jnp.concatenate([gotx[f * 4 + q] for q in range(4)], axis=0)
+                edge = jnp.concatenate([edge, jnp.zeros((96, 128), F32)], axis=0).T[:, :32]
+                v = three(edge[:64], (xh[0], xl[0])) + three(edge[64:], (xh[1], xl[1]))
+                zero = [a + b for a, b in zip(zero, halves(v[:, :256], v[:, 256:]))]
+            for k in range(4):
+                add(k, zero[k])
+
         return 0
 
-    lax.fori_loop(0, 8, transform, 0)
-    wait(part, lsem)
+    lax.fori_loop(0, 8, functools.partial(transform, rp=0), 0)
+
+    @pl.when(first)
+    def _():
+        wait(gotx.at[pl.ds(0, 7)], rsem.at[3])
+
+    @pl.when(me >= 8)
+    def _():
+        wait(gotx, rsem.at[3])
+
+    for p in range(2):
+        wait(got.at[pl.ds(0, 127), pl.ds(p * 16, 16)], rsem.at[5 + p])
+
+    def picture(f, _):
+        lax.fori_loop(4 * f, 4 * f + 4, functools.partial(transform, rp=1), 0)
+
+        def strip(i, _):
+            at = pl.ds(pl.multiple_of(i * 8, 8), 8)
+            for tile in range(2):
+                mixed = mix_pairs(lambda k, part: send[f * 64 + 4 * k + 2 * part + tile, at, :])
+                for l, value in mixed:
+                    image[f, at, l * 256 + tile * 128:l * 256 + tile * 128 + 128] = value
+            pltpu.make_async_copy(image.at[f, at, :], out.at[f, at, :], lsem).start()
+            return 0
+
+        lax.fori_loop(0, 8, strip, 0)
+        return 0
+
+    lax.fori_loop(0, 2, picture, 0)
+    wait(out, lsem)
     wait(tabr.at[pl.ds(0, 127)], ssem.at[0])
-    wait(half0.at[pl.ds(0, 127)], ssem.at[4])
+    wait(got.at[pl.ds(0, 127), early], ssem.at[4])
     for p in range(2):
-        wait(out.at[pl.ds(0, 127), pl.ds(p * 16, 16)], rsem.at[5 + p])
-        wait(recv.at[pl.ds(0, 127), pl.ds(p * 16, 16)], ssem.at[5 + p])
+        wait(got.at[pl.ds(0, 127), pl.ds(p * 16, 16)], ssem.at[5 + p])
 
 
 def exchange(tiles, pair, time, chan, count, weights, pixels, beams):
     t = tables()
     smem = pl.BlockSpec(memory_space=pltpu.SMEM)
     away = pl.BlockSpec(memory_space=pl.ANY)
-    constants = (*t["b"], *t["wc"], *t["tw"], t["f"], *t["wr"][0], *t["ws"][0], t["tj"])
+    constants = (*t["b"], *t["wc"], *t["tw"], t["f"], *t["wr"], *t["ws"], *t["wx"], t["tj"])
     return pl.pallas_call(
         exchange_kernel,
-        out_shape=(
-            jax.ShapeDtypeStruct((128, 32, 128), F32), jax.ShapeDtypeStruct((8, 8, 128), F32),
-            jax.ShapeDtypeStruct((128, 64, 128), F32),
-        ),
-        in_specs=[pl.BlockSpec(memory_space=pltpu.VMEM)] + [smem] * 5 + [away] * 14,
-        out_specs=(away, away, away),
+        out_shape=jax.ShapeDtypeStruct((2, 64, 8192), F32),
+        in_specs=[pl.BlockSpec(memory_space=pltpu.VMEM)] + [smem] * 5 + [away] * 16,
+        out_specs=away,
         scratch_shapes=[
             pltpu.VMEM((128, 2, 16, 128), F32),
             pltpu.VMEM((1024, 2, 16, 128), BF),
@@ -500,10 +574,12 @@
             pltpu.VMEM((256, 128), F32),
             pltpu.VMEM((256, 128), F32),
             pltpu.VMEM((2, 3, 256, 256), BF),
-            pltpu.VMEM((128, 512), BF),
-            pltpu.VMEM((128, 512), BF),
             pltpu.VMEM((2, 128, 512), BF),
             pltpu.VMEM((2, 128, 512), BF),
+            pltpu.VMEM((2, 2, 128, 512), BF),
+            pltpu.VMEM((2, 2, 128, 512), BF),
+            pltpu.VMEM((2, 32, 512), BF),
+            pltpu.VMEM((2, 32, 512), BF),
             pltpu.VMEM((16, 2, 256), F32),
             pltpu.VMEM((128 * 32, 128), F32),
             pltpu.VMEM((8, 256, 256), BF),
@@ -520,11 +596,13 @@
             pltpu.VMEM((128, 256), F32),
             pltpu.VMEM((128 * 64, 128), F32),
             pltpu.VMEM((128 * 8, 128), F32),
-            pltpu.VMEM((128, 32, 128), F32),
+            pltpu.VMEM((128, 64, 128), F32),
+            pltpu.VMEM((8, 8, 128), F32),
+            pltpu.VMEM((2, 64, 8192), F32),
             pltpu.SemaphoreType.DMA((8,)),
             pltpu.SemaphoreType.DMA((8,)),
             pltpu.SemaphoreType.DMA,
-            pltpu.SemaphoreType.DMA((14,)),
+            pltpu.SemaphoreType.DMA((16,)),
         ],
         compiler_params=pltpu.CompilerParams(
             vmem_limit_bytes=VMEM, collective_id=0, has_side_effects=True
@@ -533,106 +611,6 @@
     )(tiles, pair, time, chan, count, weights, pixels, beams, *constants)
 
 
-def final_kernel(x, ex, part, wh, wl, sh, sl, xh, xl, tj, out, val):
-    group = pl.program_id(1)
-    turned = row_dft([[x[k, 0, q] for q in range(4)] for k in range(4)], (wh, wl), tj, group)
-    for k in range(16):
-        val[16 * group + k] = turned[k] + part[k]
-
-    @pl.when(group == 0)
-    def _():
-        extra = jnp.concatenate([ex[0, q] for q in range(4)], axis=0)
-        extra = jnp.concatenate([extra, jnp.zeros((96, 128), F32)], axis=0).T[:, :32]
-        v = three(extra[:64], (xh[0], xl[0])) + three(extra[64:], (xh[1], xl[1]))
-        more = halves(v[:, :256], v[:, 256:])
-        for k, v in enumerate(row_dft_zero([x[0, 0, q] for q in range(4)], (sh, sl))):
-            val[k] = v + part[k] + more[k]
-
-    @pl.when(group == 3)
-    def _():
-        index = {}
-        for i, j in enumerate(PAIR_J):
-            if i > 0:
-                index[j if j < 16 else 32 - j] = (i, 1.0 if j < 16 else -1.0)
-
-        def strip(i, _):
-            at = pl.ds(pl.multiple_of(i * 8, 8), 8)
-            for tile in range(2):
-                zero, mid = val[tile, at, :], val[2 + tile, at, :]
-                re = {j: val[4 * k + tile, at, :] for j, (k, _) in index.items()}
-                im = {j: val[4 * k + 2 + tile, at, :] for j, (k, _) in index.items()}
-
-                def wave(fun, part, js, l1, signed):
-                    total = None
-                    for j in js:
-                        turn = j * l1 % 32
-                        c = fun(2 * math.pi * turn / 32)
-                        if signed:
-                            c = c * index[j][1]
-                        if abs(c) < 1e-12:
-                            continue
-                        if abs(abs(c) - 1) < 1e-12:
-                            term = part[j]
-                            if total is None:
-                                total = term if c > 0 else -term
-                            else:
-                                total = total + term if c > 0 else total - term
-                        else:
-                            term = part[j] * c
-                            total = term if total is None else total + term
-                    return total if total is not None else jnp.zeros((8, 128), F32)
-
-                odd = range(1, 16, 2)
-                ce, se = [None] * 9, [None] * 9
-                for l1 in range(5):
-                    sign = 1.0 if l1 % 2 == 0 else -1.0
-                    ee = wave(math.cos, re, (4, 8, 12), l1, False)
-                    ee = ee + (zero + mid if sign > 0 else zero - mid)
-                    eo = wave(math.cos, re, (2, 6, 10, 14), l1, False)
-                    oe = wave(math.sin, im, (4, 8, 12), l1, True)
-                    oo = wave(math.sin, im, (2, 6, 10, 14), l1, True)
-                    ce[l1], ce[8 - l1] = ee + eo, ee - eo
-                    se[l1], se[8 - l1] = oe + oo, oo - oe
-                for l1 in range(9):
-                    co = wave(math.cos, re, odd, l1, False)
-                    so = wave(math.sin, im, odd, l1, True)
-                    p, m = ce[l1] + co, ce[l1] - co
-                    s, d = se[l1] + so, se[l1] - so
-
-                    def put(l, value):
-                        out[0, at, l * 256 + tile * 128:l * 256 + tile * 128 + 128] = value
-
-                    put(l1, p + s)
-                    put(16 + l1, m + d)
-                    if l1 > 0:
-                        put(32 - l1, p - s)
-                        if l1 < 8:
-                            put(16 - l1, m - d)
-            return 0
-
-        lax.fori_loop(0, 8, strip, 0)
-
-
-def final(recv, extra, part):
-    t = tables()
-    whole = pl.BlockSpec(memory_space=pltpu.VMEM)
-    return pl.pallas_call(
-        final_kernel,
-        grid=(2, 4),
-        out_shape=jax.ShapeDtypeStruct((2, 64, 8192), F32),
-        in_specs=[
-            pl.BlockSpec((4, 1, 4, 32, 128), lambda f, j: (j, f, 0, 0, 0)),
-            pl.BlockSpec((1, 4, 8, 128), lambda f, j: (f, 0, 0, 0)),
-            pl.BlockSpec((16, 64, 128), lambda f, j: (f * 4 + j, 0, 0)),
-        ]
-        + [whole] * 7,
-        out_specs=pl.BlockSpec((1, 64, 8192), lambda f, j: (f, 0, 0)),
-        scratch_shapes=[pltpu.VMEM((64, 64, 128), F32)],
-        compiler_params=pltpu.CompilerParams(vmem_limit_bytes=VMEM),
-        name="final",
-    )(recv, extra, part, *t["wr"][1], *t["ws"][1], *t["wx"], t["tj"])
-
-
 def pixel_view(pixels):
     x = pixels.reshape(128, 2, 2, 8, 128).transpose(0, 1, 3, 2, 4)
     return x.reshape(128, 2, 16, 128)
@@ -647,11 +625,10 @@
     subgrid_pixels, tile_offsets, station_pairs, time_blocks, channel_blocks, valid_counts,
     aterms, channel_weights,
 ):
-    half, extra, part = exchange(
+    return exchange(
         tile_offsets.T, station_pairs.T, time_blocks, channel_blocks, valid_counts, channel_weights,
         pixel_view(subgrid_pixels), beam_view(aterms),
     )
-    return final(half.reshape(16, 2, 4, 32, 128), extra.reshape(2, 4, 8, 128), part)
 
 
 def solution(mesh):

time: 150 us -> 143 us (0.953); the launches traced: 148 us -> 143 us
  Pallas kernels: 147 us -> 137 us
  local copies, waits for them, and re-layouts: 0 us -> 4.61 us
    pallas_call x2 -> x1, Pallas kernels: 147 us -> 137 us  [exchange(): pl.pallas_call(exchange_kernel, out_shape=jax.ShapeDtypeStruct((2, 64, 81...]
    unnamed x0 -> x1, local copies, waits for them, and re-layouts: none -> 4.61 us
where the time goes in v6:
time: 143 us
  Pallas kernels  137 us (96%)
  local copies, waits for them, and re-layouts  4.61 us (3%)
    pallas_call x1, Pallas kernels, exchange(): pl.pallas_call(exchange_kernel, out_shape=jax.ShapeDtypeStruct((2, 64, 81...  137 us
    unnamed x1, local copies, waits for them, and re-layouts  4.61 us

profile of v6, /device:TPU:1, one launch (start us, length us, event | category | flops | bytes accessed | tf_op | source)
XLA Modules:
  0.0 142.6 jit_solution(1410748883978231265)
XLA Ops:
  0.7 137.3 %exchange.1 = f32[2,64,8192]{2,1,0:T(8,128)} custom-call(s32[2,128]{1,0:T(2,128)} %bitcast.14, s32[2,128]{1,0:T(2,128)} %bitcast.15, s32[128]{0:T(128)} %time.1, s32[128]{0:T(128)} %chan.1, s32[1]{0:T(128)S(6)} %copy.26.vc, f32[8]{0:T(128)} %cw.1, f32[128,2,16,128]{3,2,1,0:T(8,128)} %bitcast.13, bf16[1024,2,16,128]{3,2,1,0:T(8,128)(2,1)} %bitcast.12, ...), custom_call_target="tpu_custom_call" | custom-call | tf_op jit(solution)/shard_map/exchange/pallas_call | solution.py:562
  137.9 4.6 %copy.27 = f32[2,64,8192]{2,1,0:T(8,128)} copy(f32[2,64,8192]{2,1,0:T(8,128)} %exchange.1) | data formatting | bytes 8388608

commit v7 on v6

--- a/solution.py
+++ b/solution.py
@@ -67,7 +67,7 @@
     tw = unit(i[:, None] * (np.arange(128) % 32)[None, :] / 8192)
     d = unit(np.arange(32)[:, None] * np.arange(32)[None, :] % 32 / 32)
     coef = np.stack([np.stack([d, 1j * d]), np.stack([1j * d, -d])])
-    f = np.zeros((2, 3, 2, 2, 32, 2, 2, 2, 32))
+    f = np.zeros((2, 2, 2, 2, 32, 2, 2, 2, 32))
 
     def put(kind, which, half, pm, conj):
         for pq in range(2):
@@ -83,8 +83,8 @@
     put(1, 0, 0, 0, False)
     put(1, 0, 1, 1, False)
     put(1, 1, 1, 1, True)
-    put(1, 2, 0, 0, True)
-    f = f.reshape(2, 3, 128, 256)
+    put(1, 1, 0, 0, True)
+    f = f.reshape(2, 2, 128, 256)
     fh, fl = split_np(f)
     f = np.concatenate([fh, fl], axis=2)
     k = np.arange(256)
@@ -242,7 +242,7 @@
     wrh_hbm, wrl_hbm, wsh_hbm, wsl_hbm, xh_hbm, xl_hbm, tj_hbm, out,
     px, beams, bh, bl, wh, wl, twr, twi, fmat, wrh, wrl, wsh, wsl, xh, xl, tj,
     corr, lhi, llo, perm, send, tabs,
-    recv, tabr, tabt, ghl, pqh, pql, zc, stage, extra, got, gotx, image, ssem, rsem, lsem, csem
+    recv, tabr, tabt, ghl, pqh, pql, held, stage, extra, got, gotx, image, ssem, rsem, lsem, csem
 ):
     me = lax.axis_index("row") * 8 + lax.axis_index("col")
     first = me < 8
@@ -370,6 +370,8 @@
     lane = lax.broadcasted_iota(I32, (32, 128), 1)
     low = lane < 64
 
+    shifted = first & (lax.broadcasted_iota(I32, (64, 128), 1) < 64)
+
     def columns(pm, t):
         g = ghl[pm, pl.ds(pl.multiple_of(t * 256, 256), 256), :]
         for c in range(4):
@@ -380,8 +382,12 @@
             ur, ui = u[:64], u[64:]
             m0 = slice(c * 64, c * 64 + 64)
             tr, ti = twr[m0, :], twi[m0, :]
-            pqh[pm, m0, :128], pql[pm, m0, :128] = split(tr * ur - ti * ui)
-            pqh[pm, m0, 128:], pql[pm, m0, 128:] = split(tr * ui + ti * ur)
+            for lanes, value in (
+                (slice(0, 128), tr * ur - ti * ui), (slice(128, 256), tr * ui + ti * ur)
+            ):
+                if pm == 1:
+                    value, held[m0, lanes] = jnp.where(shifted, held[m0, lanes], value), value
+                pqh[pm, m0, lanes], pql[pm, m0, lanes] = split(value)
 
     def mix(which, pm):
         both = fmat[kind, which]
@@ -417,7 +423,7 @@
                 return 0
 
             lax.fori_loop(0, 8, block, 0)
-        zc[...] = jnp.zeros((128, 256), F32)
+        held[...] = jnp.zeros((256, 256), F32)
 
     def phase(p, _):
         rp, half = lax.div(p, 2), lax.rem(p, 2)
@@ -429,20 +435,18 @@
         def row(i, _):
             t = half * 8 + i
 
-            @pl.when(first & (t > 0))
-            def _():
-                zc[...] = mix(2, 1)
-
             columns(0, t)
             columns(1, 15 - t)
-            emit(stage, 64, mix(0, 0) + mix(1, 1) + zc[...], rp * 32 + 2 * t, (0, 1))
+            emit(stage, 64, mix(0, 0) + mix(1, 1), rp * 32 + 2 * t, (0, 1))
             return 0
 
         lax.fori_loop(0, 8, row, 0)
 
         @pl.when(first & (half == 1))
         def _():
-            emit(extra, 8, mix(2, 1), rp, (0,))
+            for lanes in (slice(0, 128), slice(128, 256)):
+                pqh[1, :, lanes], pql[1, :, lanes] = split(held[:, lanes])
+            emit(extra, 8, mix(1, 1), rp, (0,))
 
         @pl.when(p == 1)
         def _():
@@ -475,7 +479,6 @@
     def _():
         each(lambda d, dev: push(piece(d), gotx.at[me], 3, dev))
         keep(piece(me), gotx.at[me])
-        wait(extra.at[pl.ds(0, 127 * 8), :], ssem.at[3])
 
     wait(send.at[pl.ds(0, 127), early], ssem.at[1])
     wait(send.at[pl.ds(0, 127), late], ssem.at[2])
@@ -548,6 +551,10 @@
 
     lax.fori_loop(0, 2, picture, 0)
     wait(out, lsem)
+    @pl.when(first)
+    def _():
+        wait(extra.at[pl.ds(0, 127 * 8), :], ssem.at[3])
+
     wait(tabr.at[pl.ds(0, 127)], ssem.at[0])
     wait(got.at[pl.ds(0, 127), early], ssem.at[4])
     for p in range(2):
@@ -573,7 +580,7 @@
             pltpu.VMEM((512, 256), BF),
             pltpu.VMEM((256, 128), F32),
             pltpu.VMEM((256, 128), F32),
-            pltpu.VMEM((2, 3, 256, 256), BF),
+            pltpu.VMEM((2, 2, 256, 256), BF),
             pltpu.VMEM((2, 128, 512), BF),
             pltpu.VMEM((2, 128, 512), BF),
             pltpu.VMEM((2, 2, 128, 512), BF),
@@ -593,7 +600,7 @@
             pltpu.VMEM((2, 16 * 256, 256), BF),
             pltpu.VMEM((2, 256, 256), BF),
             pltpu.VMEM((2, 256, 256), BF),
-            pltpu.VMEM((128, 256), F32),
+            pltpu.VMEM((256, 256), F32),
             pltpu.VMEM((128 * 64, 128), F32),
             pltpu.VMEM((128 * 8, 128), F32),
             pltpu.VMEM((128, 64, 128), F32),

time: 143 us -> 134 us (0.937)
  the two profiles are of different devices: /device:TPU:1 before, /device:TPU:5 now
where the time goes in v7:
time: 134 us; the launch traced here: 133 us
  Pallas kernels  128 us (96%)
  local copies, waits for them, and re-layouts  4.61 us (3%)
    pallas_call x1, Pallas kernels, exchange(): pl.pallas_call(exchange_kernel, out_shape=jax.ShapeDtypeStruct((2, 64, 81...  128 us
    unnamed x1, local copies, waits for them, and re-layouts  4.61 us

profile of v7, /device:TPU:5, one launch (start us, length us, event | category | flops | bytes accessed | tf_op | source)
XLA Modules:
  0.0 133.5 jit_solution(3761714249464428805)
XLA Ops:
  0.7 128.2 %exchange.1 = f32[2,64,8192]{2,1,0:T(8,128)} custom-call(s32[2,128]{1,0:T(2,128)} %bitcast.14, s32[2,128]{1,0:T(2,128)} %bitcast.15, s32[128]{0:T(128)} %time.1, s32[128]{0:T(128)} %chan.1, s32[1]{0:T(128)S(6)} %copy.26.vc, f32[8]{0:T(128)} %cw.1, f32[128,2,16,128]{3,2,1,0:T(8,128)} %bitcast.13, bf16[1024,2,16,128]{3,2,1,0:T(8,128)(2,1)} %bitcast.12, ...), custom_call_target="tpu_custom_call" | custom-call | tf_op jit(solution)/shard_map/exchange/pallas_call | solution.py:569
  128.9 4.6 %copy.27 = f32[2,64,8192]{2,1,0:T(8,128)} copy(f32[2,64,8192]{2,1,0:T(8,128)} %exchange.1) | data formatting | bytes 8388608

commit v8 on v7

--- a/solution.py
+++ b/solution.py
@@ -98,9 +98,9 @@
     w16 = np.where((pm == 1)[:, None], unit((32 * r[:, None] + 16) * l0[None, :] % 8192 / 8192), 0) / 4096
     ws = np.stack([np.concatenate([w0.real, w16.real], 1), np.concatenate([-w0.imag, -w16.imag], 1)])
     kx = np.arange(32)
-    qx, row = kx // 8, kx % 8
+    qx, row = kx // 2 % 4, kx % 2
     rx = 16 * (15 - (2 * qx + row))
-    wx = np.where((row < 2)[:, None], unit(-(rx[:, None] * l0[None, :] % 256) / 256), 0) / 4096
+    wx = np.where((kx < 8)[:, None], unit(-(rx[:, None] * l0[None, :] % 256) / 256), 0) / 4096
     zero = np.zeros_like(wx.real)
     wx = np.stack([np.concatenate([wx.real, zero], 1), np.concatenate([-wx.imag, zero], 1)])
     tj = unit(np.array(PAIR_J)[:, None] * l0[None, :] / 8192)
@@ -242,10 +242,19 @@
     wrh_hbm, wrl_hbm, wsh_hbm, wsl_hbm, xh_hbm, xl_hbm, tj_hbm, out,
     px, beams, bh, bl, wh, wl, twr, twi, fmat, wrh, wrl, wsh, wsl, xh, xl, tj,
     corr, lhi, llo, perm, send, tabs,
-    recv, tabr, tabt, ghl, pqh, pql, held, stage, extra, got, gotx, image, ssem, rsem, lsem, csem
+    recv, tabr, tabt, ghl, pqh, pql, held, stage, extra, got, gotx, edges, image, ssem, rsem, lsem, csem
 ):
-    me = lax.axis_index("row") * 8 + lax.axis_index("col")
-    first = me < 8
+    line, column = lax.axis_index("row"), lax.axis_index("col")
+    x, y = lax.div(line, 4), lax.rem(line, 4)
+    z, core = lax.div(column, 2), lax.rem(column, 2)
+    me = line * 8 + column
+
+    def unit_of(row, col):
+        turn = lax.rem(lax.div(row, 4) + row + lax.div(col, 2), 4)
+        return (turn * 2 + lax.rem(col, 2)) * 16 + row
+
+    mine = unit_of(line, column)
+    first = mine < 8
     kind = jnp.where(first, 1, 0)
     barrier = pltpu.get_barrier_semaphore()
     loads = [
@@ -260,8 +269,6 @@
     for load in loads:
         load.start()
 
-    x, y = lax.div(lax.axis_index("row"), 4), lax.rem(lax.axis_index("row"), 4)
-    z, core = lax.div(lax.axis_index("col"), 2), lax.rem(lax.axis_index("col"), 2)
     cols = [lax.rem(z + b // 2, 4) * 2 + lax.rem(core + b, 2) for b in range(8)]
 
     def each(fun):
@@ -333,8 +340,10 @@
     loads[3].wait()
 
     early, late = pl.ds(0, 32), pl.ds(32, 32)
-
-    def fine(k, _):
+    pl.semaphore_wait(barrier, 127)
+
+    def fine(i, _):
+        k = lax.rem(i + lax.div(mine, 16), 8)
         a = jnp.where(k == 0, 0, jnp.where(k == 1, 4, lax.div(k, 2)))
         b = jnp.where(k < 2, a, 8 - a)
         acc = None
@@ -351,18 +360,27 @@
                     send[(k * 4 + p * 2 + f) * 4 + q] = (
                         padded[q * 64:(q + 1) * 64, p * 128:(p + 1) * 128]
                     )
+        for n in range(16):
+            o = n * 7 % 16
+            tx, ty = lax.rem(x + o // 4, 4), lax.rem(y + o % 4, 4)
+            tz = lax.rem(lax.div(k, 2) + 8 - tx - ty, 4)
+            dev = (tx * 4 + ty, tz * 2 + lax.rem(k, 2))
+            if o > 0:
+                push(send.at[k * 16 + dev[0], early], recv.at[me, early], 1, dev)
+            else:
+                @pl.when(i > 0)
+                def _(dev=dev):
+                    push(send.at[k * 16 + dev[0], early], recv.at[me, early], 1, dev)
+
         return 0
 
     lax.fori_loop(0, 8, fine, 0)
-    pl.semaphore_wait(barrier, 127)
-    each(lambda d, dev: push(send.at[d, early], recv.at[me, early], 1, dev))
-    each(lambda d, dev: push(tabs.at[lax.rem(d, 4)], tabr.at[me], 0, dev))
-    each(lambda d, dev: push(send.at[d, late], recv.at[me, late], 2, dev))
-    keep(tabs.at[lax.rem(me, 4)], tabr.at[me])
-    keep(send.at[me], recv.at[me])
+    each(lambda d, dev: push(tabs.at[lax.rem(dev[0], 4)], tabr.at[me], 0, dev))
+    each(lambda d, dev: push(send.at[unit_of(*dev), late], recv.at[me, late], 2, dev))
+    keep(tabs.at[y], tabr.at[me])
+    keep(send.at[mine], recv.at[me])
     flat = recv.reshape(128 * 64, 128)
 
-    extra[...] = jnp.zeros((1024, 128), F32)
     for load in loads[4:9]:
         load.wait()
     wait(tabr.at[pl.ds(0, 127)], rsem.at[0])
@@ -394,15 +412,18 @@
         z = dot_nt(both, pqh[pm])
         return z[:128] + z[128:] + dot_nt(both[:128], pql[pm])
 
-    def emit(dst, size, z, row, pms):
-        for pm in pms:
+    def turn(z, pm, tile):
+        lanes = slice(tile * 128, tile * 128 + 128)
+        re, im = z[pm * 64:pm * 64 + 32, lanes], z[pm * 64 + 32:pm * 64 + 64, lanes]
+        return (
+            jnp.where(low, re, pltpu.roll(im, 64, 1)), jnp.where(low, pltpu.roll(re, 64, 1), im)
+        )
+
+    def emit(z, row):
+        for pm in range(2):
             for tile in range(2):
-                lanes = slice(tile * 128, tile * 128 + 128)
-                re, im = z[pm * 64:pm * 64 + 32, lanes], z[pm * 64 + 32:pm * 64 + 64, lanes]
-                even = jnp.where(low, re, pltpu.roll(im, 64, 1))
-                odd = jnp.where(low, pltpu.roll(re, 64, 1), im)
-                dst[pl.ds(2 * tile * size + row + pm, 32, stride=4 * size), :] = even
-                dst[pl.ds((2 * tile + 1) * size + row + pm, 32, stride=4 * size), :] = odd
+                for q, rows in enumerate(turn(z, pm, tile)):
+                    stage[pl.ds((2 * tile + q) * 64 + row + pm, 32, stride=256), :] = rows
 
     def gather(rp):
         for pm in range(2):
@@ -437,7 +458,7 @@
 
             columns(0, t)
             columns(1, 15 - t)
-            emit(stage, 64, mix(0, 0) + mix(1, 1), rp * 32 + 2 * t, (0, 1))
+            emit(mix(0, 0) + mix(1, 1), rp * 32 + 2 * t)
             return 0
 
         lax.fori_loop(0, 8, row, 0)
@@ -446,7 +467,11 @@
         def _():
             for lanes in (slice(0, 128), slice(128, 256)):
                 pqh[1, :, lanes], pql[1, :, lanes] = split(held[:, lanes])
-            emit(extra, 8, mix(1, 1), rp, (0,))
+            edge = mix(1, 1)
+            for tile in range(2):
+                for q, rows in enumerate(turn(edge, 0, tile)):
+                    for m in range(32):
+                        extra[m * 4 + 2 * tile + q, pl.ds(rp, 1), :] = rows[m:m + 1]
 
         @pl.when(p == 1)
         def _():
@@ -454,8 +479,8 @@
                 return stage.at[pl.ds(pl.multiple_of(d * 64, 64), 32), :]
 
             wait(recv.at[pl.ds(0, 127), late], rsem.at[2])
-            each(lambda d, dev: push(piece(d), got.at[me, early], 4, dev))
-            keep(piece(me), got.at[me, early])
+            each(lambda d, dev: push(piece(d), got.at[mine, early], 4, dev))
+            keep(piece(me), got.at[mine, early])
 
         @pl.when(p > 1)
         def _():
@@ -464,21 +489,18 @@
             def piece(d):
                 return stage.at[pl.ds(pl.multiple_of(d * 64 + p * 16, 16), 16), :]
 
-            each(lambda d, dev: push(piece(d), got.at[me, rows], 3 + p, dev))
-            keep(piece(me), got.at[me, rows])
+            each(lambda d, dev: push(piece(d), got.at[mine, rows], 3 + p, dev))
+            keep(piece(me), got.at[mine, rows])
 
         return 0
 
     wait(recv.at[pl.ds(0, 127), early], rsem.at[1])
     lax.fori_loop(0, 4, phase, 0)
 
-    def piece(d):
-        return extra.at[pl.ds(pl.multiple_of(d * 8, 8), 8), :]
-
     @pl.when(first)
     def _():
-        each(lambda d, dev: push(piece(d), gotx.at[me], 3, dev))
-        keep(piece(me), gotx.at[me])
+        each(lambda d, dev: push(extra.at[d], gotx.at[mine], 3, dev))
+        keep(extra.at[me], gotx.at[mine])
 
     wait(send.at[pl.ds(0, 127), early], ssem.at[1])
     wait(send.at[pl.ds(0, 127), late], ssem.at[2])
@@ -512,8 +534,9 @@
                 [got[f * 4 + q, rows, :] for q in range(4)], (wsh.at[rp], wsl.at[rp])
             )
             if rp == 1:
-                edge = jnp.concatenate([gotx[f * 4 + q] for q in range(4)], axis=0)
-                edge = jnp.concatenate([edge, jnp.zeros((96, 128), F32)], axis=0).T[:, :32]
+                for q in range(4):
+                    edges[2 * q:2 * q + 2, :] = gotx[f * 4 + q]
+                edge = jnp.concatenate([edges[...], jnp.zeros((120, 128), F32)], axis=0).T[:, :32]
                 v = three(edge[:64], (xh[0], xl[0])) + three(edge[64:], (xh[1], xl[1]))
                 zero = [a + b for a, b in zip(zero, halves(v[:, :256], v[:, 256:]))]
             for k in range(4):
@@ -527,7 +550,7 @@
     def _():
         wait(gotx.at[pl.ds(0, 7)], rsem.at[3])
 
-    @pl.when(me >= 8)
+    @pl.when(mine >= 8)
     def _():
         wait(gotx, rsem.at[3])
 
@@ -553,7 +576,7 @@
     wait(out, lsem)
     @pl.when(first)
     def _():
-        wait(extra.at[pl.ds(0, 127 * 8), :], ssem.at[3])
+        wait(extra.at[pl.ds(0, 127)], ssem.at[3])
 
     wait(tabr.at[pl.ds(0, 127)], ssem.at[0])
     wait(got.at[pl.ds(0, 127), early], ssem.at[4])
@@ -602,9 +625,10 @@
             pltpu.VMEM((2, 256, 256), BF),
             pltpu.VMEM((256, 256), F32),
             pltpu.VMEM((128 * 64, 128), F32),
-            pltpu.VMEM((128 * 8, 128), F32),
+            pltpu.VMEM((128, 2, 128), F32),
             pltpu.VMEM((128, 64, 128), F32),
-            pltpu.VMEM((8, 8, 128), F32),
+            pltpu.VMEM((8, 2, 128), F32),
+            pltpu.VMEM((8, 128), F32),
             pltpu.VMEM((2, 64, 8192), F32),
             pltpu.SemaphoreType.DMA((8,)),
             pltpu.SemaphoreType.DMA((8,)),

time: 134 us -> 132 us (0.985)
  the two profiles are of different devices: /device:TPU:5 before, /device:TPU:1 now
where the time goes in v8:
time: 132 us
  Pallas kernels  127 us (96%)
  local copies, waits for them, and re-layouts  4.61 us (3%)
    pallas_call x1, Pallas kernels, exchange(): pl.pallas_call(exchange_kernel, out_shape=jax.ShapeDtypeStruct((2, 64, 81...  127 us
    unnamed x1, local copies, waits for them, and re-layouts  4.61 us

profile of v8, /device:TPU:1, one launch (start us, length us, event | category | flops | bytes accessed | tf_op | source)
XLA Modules:
  0.0 131.9 jit_solution(14668668830722509661)
XLA Ops:
  0.7 126.7 %exchange.1 = f32[2,64,8192]{2,1,0:T(8,128)} custom-call(s32[2,128]{1,0:T(2,128)} %bitcast.14, s32[2,128]{1,0:T(2,128)} %bitcast.15, s32[128]{0:T(128)} %time.1, s32[128]{0:T(128)} %chan.1, s32[1]{0:T(128)S(6)} %copy.26.vc, f32[8]{0:T(128)} %cw.1, f32[128,2,16,128]{3,2,1,0:T(8,128)} %bitcast.13, bf16[1024,2,16,128]{3,2,1,0:T(8,128)(2,1)} %bitcast.12, ...), custom_call_target="tpu_custom_call" | custom-call | tf_op jit(solution)/shard_map/exchange/pallas_call | solution.py:592
  127.3 4.6 %copy.27 = f32[2,64,8192]{2,1,0:T(8,128)} copy(f32[2,64,8192]{2,1,0:T(8,128)} %exchange.1) | data formatting | bytes 8388608

commit v9 on v8

--- a/solution.py
+++ b/solution.py
@@ -106,11 +106,23 @@
     tj = unit(np.array(PAIR_J)[:, None] * l0[None, :] / 8192)
     tj = np.stack([tj.real, tj.imag], 1).astype(np.float32)
     wr, ws = wr.reshape(4, 2, 32, 512), ws.reshape(2, 4, 2, 32, 512)
-    wr = split_np(wr.transpose(1, 0, 2, 3).reshape(2, 128, 512))
-    ws = split_np(ws.transpose(2, 0, 1, 3, 4).reshape(2, 2, 128, 512))
+    late = [w.reshape(*w.shape[:-2], 16, 2, 512) for w in (wr[:, 1], ws[:, :, 1])]
+    wr = split_np(wr[:, 0].reshape(128, 512))
+    ws = split_np(ws[:, :, 0].reshape(2, 128, 512))
+
+    def doubled(w):
+        h, l = split_np(w)
+        shape = (*w.shape[:-4], 256, 512)
+        return (
+            np.stack([h, h], axis=-4).reshape(shape),
+            np.stack([l, np.zeros_like(l)], axis=-4).reshape(shape),
+        )
+
+    vr = doubled(late[0].transpose(2, 0, 1, 3))
+    vs = doubled(late[1].transpose(0, 3, 1, 2, 4))
     return dict(
         b=split_np(b), wc=split_np(wc), tw=(tw.real.astype(np.float32), tw.imag.astype(np.float32)),
-        f=f, wr=wr, ws=ws, wx=split_np(wx), tj=tj,
+        f=f, wr=wr, ws=ws, vr=vr, vs=vs, wx=split_np(wx), tj=tj,
     )
 
 
@@ -239,8 +251,8 @@
 def exchange_kernel(
     tiles, pair, time, chan, vc, cw, pixels_hbm, beams_hbm, bh_hbm, bl_hbm,
     wh_hbm, wl_hbm, twr_hbm, twi_hbm, fmat_hbm,
-    wrh_hbm, wrl_hbm, wsh_hbm, wsl_hbm, xh_hbm, xl_hbm, tj_hbm, out,
-    px, beams, bh, bl, wh, wl, twr, twi, fmat, wrh, wrl, wsh, wsl, xh, xl, tj,
+    wrh_hbm, wrl_hbm, wsh_hbm, wsl_hbm, vrh_hbm, vrl_hbm, vsh_hbm, vsl_hbm, xh_hbm, xl_hbm, tj_hbm, out,
+    px, beams, bh, bl, wh, wl, twr, twi, fmat, wrh, wrl, wsh, wsl, vrh, vrl, vsh, vsl, xh, xl, tj,
     corr, lhi, llo, perm, send, tabs,
     recv, tabr, tabt, ghl, pqh, pql, held, stage, extra, got, gotx, edges, image, ssem, rsem, lsem, csem
 ):
@@ -263,6 +275,7 @@
             (beams_hbm, beams), (pixels_hbm, px), (bh_hbm, bh), (bl_hbm, bl), (wh_hbm, wh),
             (wl_hbm, wl), (twr_hbm, twr), (twi_hbm, twi), (fmat_hbm, fmat),
             (wrh_hbm, wrh), (wrl_hbm, wrl), (wsh_hbm, wsh), (wsl_hbm, wsl),
+            (vrh_hbm, vrh), (vrl_hbm, vrl), (vsh_hbm, vsh), (vsl_hbm, vsl),
             (xh_hbm, xh), (xl_hbm, xl), (tj_hbm, tj),
         ))
     ]
@@ -387,6 +400,7 @@
     tabt[...] = tabr[...].reshape(128, 128).T
     lane = lax.broadcasted_iota(I32, (32, 128), 1)
     low = lane < 64
+    even = (lane & 32) == 0
 
     shifted = first & (lax.broadcasted_iota(I32, (64, 128), 1) < 64)
 
@@ -419,11 +433,27 @@
             jnp.where(low, re, pltpu.roll(im, 64, 1)), jnp.where(low, pltpu.roll(re, 64, 1), im)
         )
 
-    def emit(z, row):
+    def emit(z, t):
         for pm in range(2):
             for tile in range(2):
                 for q, rows in enumerate(turn(z, pm, tile)):
-                    stage[pl.ds((2 * tile + q) * 64 + row + pm, 32, stride=256), :] = rows
+                    stage[pl.ds((2 * tile + q) * 64 + 2 * t + pm, 32, stride=256), :] = rows
+
+    def emit_by_m(z, t):
+        for tile in range(2):
+            a = [z[i * 32:i * 32 + 32, tile * 128:tile * 128 + 128] for i in range(4)]
+            c = [
+                jnp.where(low, a[0], pltpu.roll(a[2], 64, 1)), jnp.where(low, a[1], pltpu.roll(a[3], 64, 1)),
+                jnp.where(low, pltpu.roll(a[0], 64, 1), a[2]), jnp.where(low, pltpu.roll(a[1], 64, 1), a[3]),
+            ]
+            for q in range(2):
+                b = (
+                    jnp.where(even, c[2 * q], pltpu.roll(c[2 * q + 1], 32, 1)),
+                    jnp.where(even, pltpu.roll(c[2 * q], 96, 1), c[2 * q + 1]),
+                )
+                for h in range(2):
+                    at = (2 * tile + q) * 64 + 32 + 16 * h
+                    stage[pl.ds(at + t, 32, stride=256), :] = b[h]
 
     def gather(rp):
         for pm in range(2):
@@ -446,24 +476,22 @@
             lax.fori_loop(0, 8, block, 0)
         held[...] = jnp.zeros((256, 256), F32)
 
-    def phase(p, _):
-        rp, half = lax.div(p, 2), lax.rem(p, 2)
-
-        @pl.when(half == 0)
-        def _():
-            gather(rp)
-
-        def row(i, _):
-            t = half * 8 + i
-
+    def phase(rp):
+        gather(rp)
+
+        def row(t, _):
             columns(0, t)
             columns(1, 15 - t)
-            emit(mix(0, 0) + mix(1, 1), rp * 32 + 2 * t)
+            z = mix(0, 0) + mix(1, 1)
+            if rp == 0:
+                emit(z, t)
+            else:
+                emit_by_m(z, t)
             return 0
 
-        lax.fori_loop(0, 8, row, 0)
-
-        @pl.when(first & (half == 1))
+        lax.fori_loop(0, 16, row, 0)
+
+        @pl.when(first)
         def _():
             for lanes in (slice(0, 128), slice(128, 256)):
                 pqh[1, :, lanes], pql[1, :, lanes] = split(held[:, lanes])
@@ -471,31 +499,24 @@
             for tile in range(2):
                 for q, rows in enumerate(turn(edge, 0, tile)):
                     for m in range(32):
-                        extra[m * 4 + 2 * tile + q, pl.ds(rp, 1), :] = rows[m:m + 1]
-
-        @pl.when(p == 1)
-        def _():
-            def piece(d):
-                return stage.at[pl.ds(pl.multiple_of(d * 64, 64), 32), :]
-
-            wait(recv.at[pl.ds(0, 127), late], rsem.at[2])
-            each(lambda d, dev: push(piece(d), got.at[mine, early], 4, dev))
-            keep(piece(me), got.at[mine, early])
-
-        @pl.when(p > 1)
-        def _():
-            rows = pl.ds(pl.multiple_of(p * 16, 16), 16)
-
-            def piece(d):
-                return stage.at[pl.ds(pl.multiple_of(d * 64 + p * 16, 16), 16), :]
-
-            each(lambda d, dev: push(piece(d), got.at[mine, rows], 3 + p, dev))
-            keep(piece(me), got.at[mine, rows])
-
-        return 0
+                        extra[m * 4 + 2 * tile + q, rp:rp + 1, :] = rows[m:m + 1]
+
+    def deliver(start, size, k):
+        rows = pl.ds(start, size)
+
+        def piece(d):
+            return stage.at[pl.ds(pl.multiple_of(d * 64 + start, 16), size), :]
+
+        each(lambda d, dev: push(piece(d), got.at[mine, rows], k, dev))
+        keep(piece(me), got.at[mine, rows])
 
     wait(recv.at[pl.ds(0, 127), early], rsem.at[1])
-    lax.fori_loop(0, 4, phase, 0)
+    phase(0)
+    wait(recv.at[pl.ds(0, 127), late], rsem.at[2])
+    deliver(0, 32, 4)
+    phase(1)
+    deliver(32, 16, 5)
+    deliver(48, 16, 6)
 
     @pl.when(first)
     def _():
@@ -508,43 +529,68 @@
         load.wait()
     wait(got.at[pl.ds(0, 127), early], rsem.at[4])
 
-    def transform(n, _, rp):
+    def transform(n, _):
         f, group = lax.div(n, 4), lax.rem(n, 4)
-        rows = slice(rp * 32, rp * 32 + 32)
         turned = row_dft(
-            [[got[((4 * group + k) * 2 + f) * 4 + q, rows, :] for q in range(4)] for k in range(4)],
-            (wrh.at[rp], wrl.at[rp]), tj, group,
+            [[got[((4 * group + k) * 2 + f) * 4 + q, :32, :] for q in range(4)] for k in range(4)],
+            (wrh, wrl), tj, group,
         )
-
-        def add(k, v):
-            at = n * 16 + k
-            send[at] = v if rp == 0 else send[at] + v
-
-        for k in range(4, 16):
-            add(k, turned[k])
-
-        @pl.when(group > 0)
-        def _():
-            for k in range(4):
-                add(k, turned[k])
+        for k in range(16):
+            send[n * 16 + k] = turned[k]
 
         @pl.when(group == 0)
         def _():
-            zero = row_dft_zero(
-                [got[f * 4 + q, rows, :] for q in range(4)], (wsh.at[rp], wsl.at[rp])
+            for k, v in enumerate(row_dft_zero([got[f * 4 + q, :32, :] for q in range(4)], (wsh, wsl))):
+                send[n * 16 + k] = v
+
+        return 0
+
+    lax.fori_loop(0, 8, transform, 0)
+
+    def finish(n, _, h):
+        f, group = lax.div(n, 4), lax.rem(n, 4)
+        here = slice(h * 32, h * 32 + 32)
+        parts = []
+        for k in range(4):
+            base = ((4 * group + k) * 2 + f) * 4
+            v = jnp.concatenate(
+                [got[base + q, 32 + 16 * h:48 + 16 * h, :] for q in range(4)], axis=0
             )
-            if rp == 1:
-                for q in range(4):
-                    edges[2 * q:2 * q + 2, :] = gotx[f * 4 + q]
-                edge = jnp.concatenate([edges[...], jnp.zeros((120, 128), F32)], axis=0).T[:, :32]
-                v = three(edge[:64], (xh[0], xl[0])) + three(edge[64:], (xh[1], xl[1]))
-                zero = [a + b for a, b in zip(zero, halves(v[:, :256], v[:, 256:]))]
-            for k in range(4):
-                add(k, zero[k])
+            hi = v.astype(BF).astype(F32)
+            a = jnp.concatenate([hi, v - hi], axis=0).T.astype(BF)
+            parts.append(jnp.concatenate([a[:64], a[64:]], axis=1))
+        a = jnp.concatenate(parts, axis=0)
+        u = dot(a, vrh[...]) + dot(a, vrl[...])
+
+        def add(k, pieces):
+            for i, v in enumerate(pieces):
+                send[n * 16 + 4 * k + i, here, :] += v
+
+        for k in range(4):
+            v = u[k * 64:k * 64 + 64]
+            re, im = v[:32, :256] - v[32:, 256:], v[:32, 256:] + v[32:, :256]
+            tr, ti = tj[4 * group + k, 0:1, :], tj[4 * group + k, 1:2, :]
+            pieces = halves(re * tr - im * ti, re * ti + im * tr)
+            if k > 0:
+                add(k, pieces)
+            else:
+                @pl.when(group > 0)
+                def _(pieces=pieces):
+                    add(0, pieces)
+
+        @pl.when(group == 0)
+        def _():
+            for q in range(4):
+                edges[2 * q:2 * q + 2, :] = gotx[f * 4 + q]
+            edge = jnp.concatenate([edges[...], jnp.zeros((120, 128), F32)], axis=0).T[:, :32]
+            v = three(edge[h * 32:h * 32 + 32], (xh[0], xl[0]))
+            v = v + three(edge[64 + h * 32:96 + h * 32], (xh[1], xl[1]))
+            for i in range(2):
+                one = parts[0][i * 32:i * 32 + 32]
+                v = v + dot(one, vsh[i]) + dot(one, vsl[i])
+            add(0, halves(v[:, :256], v[:, 256:]))
 
         return 0
-
-    lax.fori_loop(0, 8, functools.partial(transform, rp=0), 0)
 
     @pl.when(first)
     def _():
@@ -554,25 +600,25 @@
     def _():
         wait(gotx, rsem.at[3])
 
-    for p in range(2):
-        wait(got.at[pl.ds(0, 127), pl.ds(p * 16, 16)], rsem.at[5 + p])
-
-    def picture(f, _):
-        lax.fori_loop(4 * f, 4 * f + 4, functools.partial(transform, rp=1), 0)
-
-        def strip(i, _):
-            at = pl.ds(pl.multiple_of(i * 8, 8), 8)
-            for tile in range(2):
-                mixed = mix_pairs(lambda k, part: send[f * 64 + 4 * k + 2 * part + tile, at, :])
-                for l, value in mixed:
-                    image[f, at, l * 256 + tile * 128:l * 256 + tile * 128 + 128] = value
-            pltpu.make_async_copy(image.at[f, at, :], out.at[f, at, :], lsem).start()
+    for h in range(2):
+        wait(got.at[pl.ds(0, 127), pl.ds(h * 16, 16)], rsem.at[5 + h])
+
+        def picture(f, _, h=h):
+            lax.fori_loop(4 * f, 4 * f + 4, functools.partial(finish, h=h), 0)
+
+            def strip(i, _):
+                at = pl.ds(pl.multiple_of(h * 32 + i * 8, 8), 8)
+                for tile in range(2):
+                    mixed = mix_pairs(lambda k, part: send[f * 64 + 4 * k + 2 * part + tile, at, :])
+                    for l, value in mixed:
+                        image[f, at, l * 256 + tile * 128:l * 256 + tile * 128 + 128] = value
+                pltpu.make_async_copy(image.at[f, at, :], out.at[f, at, :], lsem).start()
+                return 0
+
+            lax.fori_loop(0, 4, strip, 0)
             return 0
 
-        lax.fori_loop(0, 8, strip, 0)
-        return 0
-
-    lax.fori_loop(0, 2, picture, 0)
+        lax.fori_loop(0, 2, picture, 0)
     wait(out, lsem)
     @pl.when(first)
     def _():
@@ -588,11 +634,11 @@
     t = tables()
     smem = pl.BlockSpec(memory_space=pltpu.SMEM)
     away = pl.BlockSpec(memory_space=pl.ANY)
-    constants = (*t["b"], *t["wc"], *t["tw"], t["f"], *t["wr"], *t["ws"], *t["wx"], t["tj"])
+    constants = (*t["b"], *t["wc"], *t["tw"], t["f"], *t["wr"], *t["ws"], *t["vr"], *t["vs"], *t["wx"], t["tj"])
     return pl.pallas_call(
         exchange_kernel,
         out_shape=jax.ShapeDtypeStruct((2, 64, 8192), F32),
-        in_specs=[pl.BlockSpec(memory_space=pltpu.VMEM)] + [smem] * 5 + [away] * 16,
+        in_specs=[pl.BlockSpec(memory_space=pltpu.VMEM)] + [smem] * 5 + [away] * 20,
         out_specs=away,
         scratch_shapes=[
             pltpu.VMEM((128, 2, 16, 128), F32),
@@ -604,10 +650,14 @@
             pltpu.VMEM((256, 128), F32),
             pltpu.VMEM((256, 128), F32),
             pltpu.VMEM((2, 2, 256, 256), BF),
+            pltpu.VMEM((128, 512), BF),
+            pltpu.VMEM((128, 512), BF),
             pltpu.VMEM((2, 128, 512), BF),
             pltpu.VMEM((2, 128, 512), BF),
-            pltpu.VMEM((2, 2, 128, 512), BF),
-            pltpu.VMEM((2, 2, 128, 512), BF),
+            pltpu.VMEM((256, 512), BF),
+            pltpu.VMEM((256, 512), BF),
+            pltpu.VMEM((2, 256, 512), BF),
+            pltpu.VMEM((2, 256, 512), BF),
             pltpu.VMEM((2, 32, 512), BF),
             pltpu.VMEM((2, 32, 512), BF),
             pltpu.VMEM((16, 2, 256), F32),
@@ -633,7 +683,7 @@
             pltpu.SemaphoreType.DMA((8,)),
             pltpu.SemaphoreType.DMA((8,)),
             pltpu.SemaphoreType.DMA,
-            pltpu.SemaphoreType.DMA((16,)),
+            pltpu.SemaphoreType.DMA((20,)),
         ],
         compiler_params=pltpu.CompilerParams(
             vmem_limit_bytes=VMEM, collective_id=0, has_side_effects=True

time: 132 us -> 129 us (0.977)
  Pallas kernels: 127 us -> 124 us
    pallas_call x1, Pallas kernels: 127 us -> 124 us  [exchange(): pl.pallas_call(exchange_kernel, out_shape=jax.ShapeDtypeStruct((2, 64, 81...]
where the time goes in v9:
time: 129 us
  Pallas kernels  124 us (96%)
  local copies, waits for them, and re-layouts  4.61 us (4%)
    pallas_call x1, Pallas kernels, exchange(): pl.pallas_call(exchange_kernel, out_shape=jax.ShapeDtypeStruct((2, 64, 81...  124 us
    unnamed x1, local copies, waits for them, and re-layouts  4.61 us

profile of v9, /device:TPU:1, one launch (start us, length us, event | category | flops | bytes accessed | tf_op | source)
XLA Modules:
  0.0 129.0 jit_solution(5125543213481759980)
XLA Ops:
  0.7 123.8 %exchange.1 = f32[2,64,8192]{2,1,0:T(8,128)} custom-call(s32[2,128]{1,0:T(2,128)} %bitcast.14, s32[2,128]{1,0:T(2,128)} %bitcast.15, s32[128]{0:T(128)} %time.1, s32[128]{0:T(128)} %chan.1, s32[1]{0:T(128)S(6)} %copy.30.vc, f32[8]{0:T(128)} %cw.1, f32[128,2,16,128]{3,2,1,0:T(8,128)} %bitcast.13, bf16[1024,2,16,128]{3,2,1,0:T(8,128)(2,1)} %bitcast.12, ...), custom_call_target="tpu_custom_call" | custom-call | tf_op jit(solution)/shard_map/exchange/pallas_call | solution.py:638
  124.4 4.6 %copy.31 = f32[2,64,8192]{2,1,0:T(8,128)} copy(f32[2,64,8192]{2,1,0:T(8,128)} %exchange.1) | data formatting | bytes 8388608

commit v10 on v9

--- a/solution.py
+++ b/solution.py
@@ -248,13 +248,25 @@
     return outs
 
 
+def paint(load, image, out, sem):
+    def strip(i, _):
+        at = pl.ds(pl.multiple_of(i * 8, 8), 8)
+        for tile in range(2):
+            for l, value in mix_pairs(lambda k, part: load(4 * k + 2 * part + tile, at)):
+                image[at, l * 256 + tile * 128:l * 256 + tile * 128 + 128] = value
+        pltpu.make_async_copy(image.at[at, :], out.at[at, :], sem).start()
+        return 0
+
+    lax.fori_loop(0, 4, strip, 0)
+
+
 def exchange_kernel(
     tiles, pair, time, chan, vc, cw, pixels_hbm, beams_hbm, bh_hbm, bl_hbm,
     wh_hbm, wl_hbm, twr_hbm, twi_hbm, fmat_hbm,
-    wrh_hbm, wrl_hbm, wsh_hbm, wsl_hbm, vrh_hbm, vrl_hbm, vsh_hbm, vsl_hbm, xh_hbm, xl_hbm, tj_hbm, out,
+    wrh_hbm, wrl_hbm, wsh_hbm, wsl_hbm, vrh_hbm, vrl_hbm, vsh_hbm, vsl_hbm, xh_hbm, xl_hbm, tj_hbm, out, rest,
     px, beams, bh, bl, wh, wl, twr, twi, fmat, wrh, wrl, wsh, wsl, vrh, vrl, vsh, vsl, xh, xl, tj,
     corr, lhi, llo, perm, send, tabs,
-    recv, tabr, tabt, ghl, pqh, pql, held, stage, extra, got, gotx, edges, image, ssem, rsem, lsem, csem
+    recv, tabr, tabt, ghl, pqh, pql, held, stage, extra, got, gotx, edges, image, ssem, rsem, lsem, msem, csem
 ):
     line, column = lax.axis_index("row"), lax.axis_index("col")
     x, y = lax.div(line, 4), lax.rem(line, 4)
@@ -512,8 +524,8 @@
 
     wait(recv.at[pl.ds(0, 127), early], rsem.at[1])
     phase(0)
+    deliver(0, 32, 4)
     wait(recv.at[pl.ds(0, 127), late], rsem.at[2])
-    deliver(0, 32, 4)
     phase(1)
     deliver(32, 16, 5)
     deliver(48, 16, 6)
@@ -606,20 +618,17 @@
         def picture(f, _, h=h):
             lax.fori_loop(4 * f, 4 * f + 4, functools.partial(finish, h=h), 0)
 
-            def strip(i, _):
-                at = pl.ds(pl.multiple_of(h * 32 + i * 8, 8), 8)
-                for tile in range(2):
-                    mixed = mix_pairs(lambda k, part: send[f * 64 + 4 * k + 2 * part + tile, at, :])
-                    for l, value in mixed:
-                        image[f, at, l * 256 + tile * 128:l * 256 + tile * 128 + 128] = value
-                pltpu.make_async_copy(image.at[f, at, :], out.at[f, at, :], lsem).start()
-                return 0
-
-            lax.fori_loop(0, 4, strip, 0)
+            if h == 0:
+                paint(lambda k, at: send[f * 64 + k, at, :], image.at[f], out.at[f], lsem)
+            else:
+                mine_f = pl.ds(f * 64, 64)
+                pltpu.make_async_copy(send.at[mine_f, late], rest.at[mine_f], msem).start()
             return 0
 
         lax.fori_loop(0, 2, picture, 0)
     wait(out, lsem)
+    wait(rest, msem)
+
     @pl.when(first)
     def _():
         wait(extra.at[pl.ds(0, 127)], ssem.at[3])
@@ -637,9 +646,11 @@
     constants = (*t["b"], *t["wc"], *t["tw"], t["f"], *t["wr"], *t["ws"], *t["vr"], *t["vs"], *t["wx"], t["tj"])
     return pl.pallas_call(
         exchange_kernel,
-        out_shape=jax.ShapeDtypeStruct((2, 64, 8192), F32),
+        out_shape=(
+            jax.ShapeDtypeStruct((2, 32, 8192), F32), jax.ShapeDtypeStruct((128, 32, 128), F32)
+        ),
         in_specs=[pl.BlockSpec(memory_space=pltpu.VMEM)] + [smem] * 5 + [away] * 20,
-        out_specs=away,
+        out_specs=(away, away),
         scratch_shapes=[
             pltpu.VMEM((128, 2, 16, 128), F32),
             pltpu.VMEM((1024, 2, 16, 128), BF),
@@ -679,9 +690,10 @@
             pltpu.VMEM((128, 64, 128), F32),
             pltpu.VMEM((8, 2, 128), F32),
             pltpu.VMEM((8, 128), F32),
-            pltpu.VMEM((2, 64, 8192), F32),
+            pltpu.VMEM((2, 32, 8192), F32),
             pltpu.SemaphoreType.DMA((8,)),
             pltpu.SemaphoreType.DMA((8,)),
+            pltpu.SemaphoreType.DMA,
             pltpu.SemaphoreType.DMA,
             pltpu.SemaphoreType.DMA((20,)),
         ],
@@ -692,6 +704,39 @@
     )(tiles, pair, time, chan, count, weights, pixels, beams, *constants)
 
 
+def final_kernel(half, rest, out, val, through, image, sems):
+    parts = [(rest.at[pl.ds(f * 64, 64)], val.at[f]) for f in range(2)]
+    parts += [(half.at[f], through.at[f]) for f in range(2)]
+    loads = [pltpu.make_async_copy(src, dst, sems.at[i]) for i, (src, dst) in enumerate(parts)]
+    for load in loads:
+        load.start()
+    for f in range(2):
+        loads[f].wait()
+        paint(lambda k, at: val[f, k, at, :], image.at[f], out.at[f, pl.ds(32, 32), :], sems.at[4])
+        loads[2 + f].wait()
+        pltpu.make_async_copy(through.at[f], out.at[f, pl.ds(0, 32), :], sems.at[5]).start()
+    pltpu.make_async_copy(image, image, sems.at[4]).wait()
+    pltpu.make_async_copy(through, through, sems.at[5]).wait()
+
+
+def final(half, rest):
+    away = pl.BlockSpec(memory_space=pl.ANY)
+    return pl.pallas_call(
+        final_kernel,
+        out_shape=jax.ShapeDtypeStruct((2, 64, 8192), F32),
+        in_specs=[away, away],
+        out_specs=away,
+        scratch_shapes=[
+            pltpu.VMEM((2, 64, 32, 128), F32),
+            pltpu.VMEM((2, 32, 8192), F32),
+            pltpu.VMEM((2, 32, 8192), F32),
+            pltpu.SemaphoreType.DMA((6,)),
+        ],
+        compiler_params=pltpu.CompilerParams(vmem_limit_bytes=VMEM),
+        name="final",
+    )(half, rest)
+
+
 def pixel_view(pixels):
     x = pixels.reshape(128, 2, 2, 8, 128).transpose(0, 1, 3, 2, 4)
     return x.reshape(128, 2, 16, 128)
@@ -706,10 +751,10 @@
     subgrid_pixels, tile_offsets, station_pairs, time_blocks, channel_blocks, valid_counts,
     aterms, channel_weights,
 ):
-    return exchange(
+    return final(*exchange(
         tile_offsets.T, station_pairs.T, time_blocks, channel_blocks, valid_counts, channel_weights,
         pixel_view(subgrid_pixels), beam_view(aterms),
-    )
+    ))
 
 
 def solution(mesh):

time: 129 us -> 127 us (0.984)
  local copies, waits for them, and re-layouts: 4.61 us -> 0 us
  Pallas kernels: 124 us -> 127 us
    unnamed x1 -> x0, local copies, waits for them, and re-layouts: 4.61 us -> none
    pallas_call x1 -> x2, Pallas kernels: 124 us -> 127 us  [the longest x1 123 us: exchange(): pl.pallas_call(exchange_kernel, out_shape=(jax.ShapeDtypeStruct((2, 32, 8...]
where the time goes in v10:
time: 127 us
  Pallas kernels  127 us (100%)
    pallas_call x1, Pallas kernels, exchange(): pl.pallas_call(exchange_kernel, out_shape=(jax.ShapeDtypeStruct((2, 32, 8...  123 us
    pallas_call x1, Pallas kernels, final(): pl.pallas_call(final_kernel, out_shape=jax.ShapeDtypeStruct((2, 64, 8192)...  3.57 us

profile of v10, /device:TPU:1, one launch (start us, length us, event | category | flops | bytes accessed | tf_op | source)
XLA Modules:
  0.0 127.4 jit_solution(11639644330638561133)
XLA Ops:
  0.7 123.1 %exchange.1 = (f32[2,32,8192]{2,1,0:T(8,128)}, f32[128,32,128]{2,1,0:T(8,128)}) custom-call(s32[2,128]{1,0:T(2,128)} %bitcast.14, s32[2,128]{1,0:T(2,128)} %bitcast.15, s32[128]{0:T(128)} %time.1, s32[128]{0:T(128)} %chan.1, s32[1]{0:T(128)S(6)} %copy.29.vc, f32[8]{0:T(128)} %cw.1, f32[128,2,16,128]{3,2,1,0:T(8,128)} %bitcast.13, ...), custom_call_target="tpu_custom_call" | custom-call | tf_op jit(solution)/shard_map/exchange/pallas_call | solution.py:647
  123.8 3.6 %final.1 = f32[2,64,8192]{2,1,0:T(8,128)} custom-call(f32[2,32,8192]{2,1,0:T(8,128)} %get-tuple-element.7.half, f32[128,32,128]{2,1,0:T(8,128)} %get-tuple-element.8.rest), custom_call_target="tpu_custom_call" | custom-call | tf_op jit(solution)/shard_map/final/pallas_call | solution.py:724

commit v11 on v10

--- a/solution.py
+++ b/solution.py
@@ -272,6 +272,8 @@
     x, y = lax.div(line, 4), lax.rem(line, 4)
     z, core = lax.div(column, 2), lax.rem(column, 2)
     me = line * 8 + column
+    group = (x * 4 + z) * 2 + core
+    order = group * 4 + y
 
     def unit_of(row, col):
         turn = lax.rem(lax.div(row, 4) + row + lax.div(col, 2), 4)
@@ -366,6 +368,10 @@
 
     early, late = pl.ds(0, 32), pl.ds(32, 32)
     pl.semaphore_wait(barrier, 127)
+    for i in range(1, 4):
+        to = lax.rem(y + i, 4)
+        push(tabs.at[to], tabr.at[order], 0, (x * 4 + to, column))
+    keep(tabs.at[y], tabr.at[order])
 
     def fine(i, _):
         k = lax.rem(i + lax.div(mine, 16), 8)
@@ -391,24 +397,32 @@
             tz = lax.rem(lax.div(k, 2) + 8 - tx - ty, 4)
             dev = (tx * 4 + ty, tz * 2 + lax.rem(k, 2))
             if o > 0:
-                push(send.at[k * 16 + dev[0], early], recv.at[me, early], 1, dev)
+                push(send.at[k * 16 + dev[0], early], recv.at[order, early], 1, dev)
             else:
                 @pl.when(i > 0)
                 def _(dev=dev):
-                    push(send.at[k * 16 + dev[0], early], recv.at[me, early], 1, dev)
+                    push(send.at[k * 16 + dev[0], early], recv.at[order, early], 1, dev)
 
         return 0
 
     lax.fori_loop(0, 8, fine, 0)
-    each(lambda d, dev: push(tabs.at[lax.rem(dev[0], 4)], tabr.at[me], 0, dev))
-    each(lambda d, dev: push(send.at[unit_of(*dev), late], recv.at[me, late], 2, dev))
-    keep(tabs.at[y], tabr.at[me])
-    keep(send.at[mine], recv.at[me])
+    wait(tabr.at[pl.ds(0, 3)], rsem.at[0])
+    block = tabr.at[pl.ds(group * 4, 4)]
+
+    def share(i, _):
+        row = lax.rem(x + lax.div(i, 8), 4) * 4 + y
+        col = lax.rem(z + lax.div(i, 2), 4) * 2 + lax.rem(core + i, 2)
+        push(block, block, 7, (row, col))
+        return 0
+
+    lax.fori_loop(1, 32, share, 0)
+    each(lambda d, dev: push(send.at[unit_of(*dev), late], recv.at[order, late], 2, dev))
+    keep(send.at[mine], recv.at[order])
     flat = recv.reshape(128 * 64, 128)
 
     for load in loads[4:9]:
         load.wait()
-    wait(tabr.at[pl.ds(0, 127)], rsem.at[0])
+    wait(tabr.at[pl.ds(0, 124)], rsem.at[7])
     tabt[...] = tabr[...].reshape(128, 128).T
     lane = lax.broadcasted_iota(I32, (32, 128), 1)
     low = lane < 64
@@ -633,7 +647,8 @@
     def _():
         wait(extra.at[pl.ds(0, 127)], ssem.at[3])
 
-    wait(tabr.at[pl.ds(0, 127)], ssem.at[0])
+    wait(tabr.at[pl.ds(0, 3)], ssem.at[0])
+    wait(tabr.at[pl.ds(0, 124)], ssem.at[7])
     wait(got.at[pl.ds(0, 127), early], ssem.at[4])
     for p in range(2):
         wait(got.at[pl.ds(0, 127), pl.ds(p * 16, 16)], ssem.at[5 + p])

time: 127 us -> 135 us (1.063)
  Pallas kernels: 127 us -> 134 us
    pallas_call x1, Pallas kernels: 123 us -> 131 us  [exchange(): pl.pallas_call(exchange_kernel, out_shape=(jax.ShapeDtypeStruct((2, 32, 8...]
where the time goes in v11:
time: 135 us
  Pallas kernels  134 us (99%)
    pallas_call x1, Pallas kernels, exchange(): pl.pallas_call(exchange_kernel, out_shape=(jax.ShapeDtypeStruct((2, 32, 8...  131 us
    pallas_call x1, Pallas kernels, final(): pl.pallas_call(final_kernel, out_shape=jax.ShapeDtypeStruct((2, 64, 8192)...  3.57 us

profile of v11, /device:TPU:1, one launch (start us, length us, event | category | flops | bytes accessed | tf_op | source)
XLA Modules:
  0.0 134.7 jit_solution(15463637614955015252)
XLA Ops:
  0.7 130.5 %exchange.1 = (f32[2,32,8192]{2,1,0:T(8,128)}, f32[128,32,128]{2,1,0:T(8,128)}) custom-call(s32[2,128]{1,0:T(2,128)} %bitcast.14, s32[2,128]{1,0:T(2,128)} %bitcast.15, s32[128]{0:T(128)} %time.1, s32[128]{0:T(128)} %chan.1, s32[1]{0:T(128)S(6)} %copy.29.vc, f32[8]{0:T(128)} %cw.1, f32[128,2,16,128]{3,2,1,0:T(8,128)} %bitcast.13, ...), custom_call_target="tpu_custom_call" | custom-call | tf_op jit(solution)/shard_map/exchange/pallas_call | solution.py:662
  131.2 3.6 %final.1 = f32[2,64,8192]{2,1,0:T(8,128)} custom-call(f32[2,32,8192]{2,1,0:T(8,128)} %get-tuple-element.7.half, f32[128,32,128]{2,1,0:T(8,128)} %get-tuple-element.8.rest), custom_call_target="tpu_custom_call" | custom-call | tf_op jit(solution)/shard_map/final/pallas_call | solution.py:739

commit v12 on v11

--- a/solution.py
+++ b/solution.py
@@ -371,9 +371,22 @@
     for i in range(1, 4):
         to = lax.rem(y + i, 4)
         push(tabs.at[to], tabr.at[order], 0, (x * 4 + to, column))
-    keep(tabs.at[y], tabr.at[order])
+    tabr[order] = tabs[y]
 
     def fine(i, _):
+        @pl.when(i == 2)
+        def _():
+            wait(tabr.at[pl.ds(0, 3)], rsem.at[0])
+            block = tabr.at[pl.ds(group * 4, 4)]
+
+            def share(i, _):
+                row = lax.rem(x + lax.div(i, 8), 4) * 4 + y
+                col = lax.rem(z + lax.div(i, 2), 4) * 2 + lax.rem(core + i, 2)
+                push(block, block, 7, (row, col))
+                return 0
+
+            lax.fori_loop(1, 32, share, 0)
+
         k = lax.rem(i + lax.div(mine, 16), 8)
         a = jnp.where(k == 0, 0, jnp.where(k == 1, 4, lax.div(k, 2)))
         b = jnp.where(k < 2, a, 8 - a)
@@ -406,16 +419,6 @@
         return 0
 
     lax.fori_loop(0, 8, fine, 0)
-    wait(tabr.at[pl.ds(0, 3)], rsem.at[0])
-    block = tabr.at[pl.ds(group * 4, 4)]
-
-    def share(i, _):
-        row = lax.rem(x + lax.div(i, 8), 4) * 4 + y
-        col = lax.rem(z + lax.div(i, 2), 4) * 2 + lax.rem(core + i, 2)
-        push(block, block, 7, (row, col))
-        return 0
-
-    lax.fori_loop(1, 32, share, 0)
     each(lambda d, dev: push(send.at[unit_of(*dev), late], recv.at[order, late], 2, dev))
     keep(send.at[mine], recv.at[order])
     flat = recv.reshape(128 * 64, 128)

time: 135 us -> 136 us (level)
  no operation moved by 1% of the time
where the time goes in v12:
time: 136 us
  Pallas kernels  135 us (99%)
    pallas_call x1, Pallas kernels, exchange(): pl.pallas_call(exchange_kernel, out_shape=(jax.ShapeDtypeStruct((2, 32, 8...  131 us
    pallas_call x1, Pallas kernels, final(): pl.pallas_call(final_kernel, out_shape=jax.ShapeDtypeStruct((2, 64, 8192)...  3.57 us

profile of v12, /device:TPU:1, one launch (start us, length us, event | category | flops | bytes accessed | tf_op | source)
XLA Modules:
  0.0 135.5 jit_solution(6787920496020325290)
XLA Ops:
  0.7 131.3 %exchange.1 = (f32[2,32,8192]{2,1,0:T(8,128)}, f32[128,32,128]{2,1,0:T(8,128)}) custom-call(s32[2,128]{1,0:T(2,128)} %bitcast.14, s32[2,128]{1,0:T(2,128)} %bitcast.15, s32[128]{0:T(128)} %time.1, s32[128]{0:T(128)} %chan.1, s32[1]{0:T(128)S(6)} %copy.29.vc, f32[8]{0:T(128)} %cw.1, f32[128,2,16,128]{3,2,1,0:T(8,128)} %bitcast.13, ...), custom_call_target="tpu_custom_call" | custom-call | tf_op jit(solution)/shard_map/exchange/pallas_call | solution.py:665
  132.0 3.6 %final.1 = f32[2,64,8192]{2,1,0:T(8,128)} custom-call(f32[2,32,8192]{2,1,0:T(8,128)} %get-tuple-element.7.half, f32[128,32,128]{2,1,0:T(8,128)} %get-tuple-element.8.rest), custom_call_target="tpu_custom_call" | custom-call | tf_op jit(solution)/shard_map/final/pallas_call | solution.py:742
